TPU v7x, 32 devices: a whole 2x2x4 slice. The times are simulated.
32 devices in a mesh: blk: 16 (over z, y, core), rep: 2 (over x).
Axes of the slice: x: 2, y: 2, z: 4, core: 2. Of those that a mesh axis runs over, the one named last changes fastest.
Arguments:
- features: float32 [16384, 128], P('blk'), may hold values from -6 to 6
- factors: float32 [16384, 128], P('blk'), may hold values from -2.4 to 2.4
Outputs:
- grads: float32 [16384, 128], P(('blk', 'rep'))
All inputs are finite; a program needn't handle non-finite values.
Results may differ from a plain program's by a relative error of at most 0.00018.
Values sent between devices are 32-bit elements; how exact they have to be, the bound alone decides.
No kernel may reach another device: no remote copies, remote signals or barrier semaphores. Data moves between devices by JAX's collectives and lax.ppermute only.
A program may use at most 128 MiB of HBM per device.

v0:
```python
import jax
import jax.numpy as jnp
from jax import lax
from jax.sharding import PartitionSpec as P


def shifted(x, axis, by):
    peers = lax.axis_size(axis)
    return lax.ppermute(x, axis, [(i, (i + by) % peers) for i in range(peers)])


def pair_terms(own_feat, own_fac, part_feat, part_fac):
    hi = lax.Precision.HIGHEST
    width = own_feat.shape[1]
    rank = own_fac.shape[1] // 2
    cross = jnp.dot(own_feat, part_feat.T, precision=hi)
    own_sq = jnp.sum(own_feat * own_feat, axis=1)
    part_sq = jnp.sum(part_feat * part_feat, axis=1)
    kernel = jnp.exp(-(own_sq[:, None] + part_sq[None, :] - 2.0 * cross) / (2.0 * width))
    coupling = jnp.dot(own_fac[:, :rank], part_fac[:, rank:].T, precision=hi)
    coupling = coupling + jnp.dot(own_fac[:, rank:], part_fac[:, :rank].T, precision=hi)
    weight = coupling * kernel
    own_term = jnp.sum(weight, axis=1)[:, None] * own_feat - jnp.dot(
        weight, part_feat, precision=hi
    )
    return (weight, -own_term / width)


def partner_term(weight, own_feat, part_feat):
    width = own_feat.shape[1]
    back = lax.dot_general(
        weight, own_feat, (((0,), (0,)), ((), ())), precision=lax.Precision.HIGHEST
    )
    total = jnp.sum(weight, axis=0)[:, None] * part_feat - back
    return -total / width


def body(features, factors):
    count = features.shape[0]
    replicas = lax.axis_size("rep")
    share = count // replicas
    first = lax.axis_index("rep") * share
    slice_feat = lax.dynamic_slice_in_dim(features, first, share, 0)
    slice_fac = lax.dynamic_slice_in_dim(factors, first, share, 0)
    blocks = lax.axis_size("blk")
    half = blocks // 2
    weight, start_acc = pair_terms(features, factors, slice_feat, slice_fac)
    carried = jnp.zeros(slice_feat.shape, jnp.float32)

    def advance(offset, state):
        trav_feat, trav_fac, trav_grad, own_sum = state
        trav_feat, trav_fac, trav_grad = shifted((trav_feat, trav_fac, trav_grad), "blk", 1)
        weight, own_term = pair_terms(features, factors, trav_feat, trav_fac)
        keep = jnp.where(2 * offset == blocks, 0.0, 1.0).astype(jnp.float32)
        trav_grad = trav_grad + keep * partner_term(weight, features, trav_feat)
        return (trav_feat, trav_fac, trav_grad, own_sum + own_term)

    state = lax.fori_loop(1, half + 1, advance, (slice_feat, slice_fac, carried, start_acc))
    returned = shifted(state[2], "blk", -half)
    own_acc = state[3]
    summed = lax.psum_scatter(own_acc, "rep", scatter_dimension=0, tiled=True)
    return summed + returned


def solution(mesh):
    placed = (P("blk", None), P("blk", None))
    return jax.shard_map(
        body, mesh=mesh, in_specs=placed, out_specs=P(("blk", "rep"), None), check_vma=False
    )
```

profile of v0, /device:TPU:0, one launch (start us, length us, event | category | flops | bytes accessed | tf_op | source)
XLA Modules:
  0.0 214.0 jit_solution(13495826556612312867)
XLA Ops:
  6.5 3.1 %fusion.12 = f32[512,1024]{1,0:T(8,128)S(1)} fusion(f32[1024,128]{1,0:T(8,128)} %param.5, s32[]{:T(128)S(6)} %select_n.14), kind=kOutput, calls=%fused_computation.20 | convolution fusion | flops 402653184 | bytes 2883588 | tf_op jit(solution)/shard_map/dot_general | solution.py:21
  12.5 3.4 %fusion.20 = (f32[1024]{0:T(1024)S(1)}, f32[1024,512]{0,1:T(8,128)S(1)}) fusion(f32[512,128]{1,0:T(8,128)} %get-tuple-element.290, f32[1024,128]{1,0:T(8,128)S(1)} %copy-done, f32[512]{0:T(512)S(1)} %get-tuple-element.228, f32[1024]{0:T(1024)S(1)} %multiply_reduce_fusion.1, f32[512,1024]{1,0:T(8,128)S(1)} %fusion.14, f32[512,1024]{1,0:T(8,128)S(1)} %fusion.12), kind=kOutput, calls=%fused_computation.31 | convolution fusion | flops 809499648 | bytes 7088128 | tf_op jit(solution)/shard_map/dot_general | solution.py:16
  15.9 4.5 %fusion.11 = f32[1024,128]{1,0:T(8,128)S(1)} fusion(f32[1024,512]{0,1:T(8,128)S(1)} %get-tuple-element.232, f32[512,128]{1,0:T(8,128)} %get-tuple-element.290, f32[1024,128]{1,0:T(8,128)S(1)} %copy-done, f32[1024]{0:T(1024)S(1)} %get-tuple-element.231), kind=kOutput, calls=%fused_computation.18 | convolution fusion | flops 805830656 | bytes 3411968 | tf_op jit(solution)/shard_map/dot_general | solution.py:23
  20.5 171.8 %while.22 = (s32[]{:T(128)}, f32[512,128]{1,0:T(8,128)}, f32[512,128]{1,0:T(8,128)S(1)}, f32[512,128]{1,0:T(8,128)S(1)}, f32[1024,128]{1,0:T(8,128)S(1)}, /*inde...) while((s32[]{:T(128)}, f32[512,128]{1,0:T(8,128)}, ...), condition=%wide.region_7.0_spmd.clone, body=%wide.region_3.7_spmd.clone.sunk | while | flops 3227121664 | bytes 25186624 | solution.py:58
  21.2 2.6 %collective-permute-start = (f32[512,128]{1,0:T(8,128)}, f32[512,128]{1,0:T(8,128)S(1)}, u32[]{:S(2)}, u32[]{:S(2)}) collective-permute-start(f32[512,128]{1,0:T(8,128)} %get-tuple-element.305), channel_id=1, source_target_pairs={{0,2},{2,4},{4,6},{6,8},{8,10},{10,12},{12,14},{14,16},{16,18},{18... | collective-permute-start | bytes 786440 | tf_op jit(solution)/shard_map/while/body/eval_jaxpr/ppermute | solution.py:9
  24.0 6.3 %collective-permute-done.1 = f32[512,128]{1,0:T(8,128)S(1)} collective-permute-done((f32[512,128]{1,0:T(8,128)S(1)}, f32[512,128]{1,0:T(8,128)S(1)}, u32[]{:S(2)}, u32[]{:S(2)}) %collective-permute-start.1) | collective-permute-done | bytes 262176 | tf_op jit(solution)/shard_map/while/body/eval_jaxpr/ppermute | solution.py:9
  30.2 1.9 fusion.54
  34.9 2.6 %fusion.56 = (f32[1024]{0:T(1024)S(1)}, f32[512]{0:T(512)S(1)}, f32[1024,512]{1,0:T(8,128)S(1)}) fusion(f32[1024,128]{1,0:T(8,128)S(1)} %get-tuple-element.326, f32[512,128]{1,0:T(8,128)S(1)} %collective-permute-done, f32[512]{0:T(512)S(1)} %multiply_reduce_fusion.4, f32[1024]{0:T(1024)S(1)} %get-tuple-element.325, f32[1024,512]{1,0:T(8,128)S(1)} %fusion.54, ...), kind=kOutput, calls=%fused_computation.30.clone.1 | convolution fusion | flops 810023424 | bytes 7090176 | tf_op jit(solution)/shard_map/while/body/eval_jaxpr/dot_general | solution.py:16
  37.5 2.0 multiply_add_fusion.5
  39.5 3.5 %multiply_add_fusion.4 = f32[512,128]{1,0:T(8,128)S(1)} fusion(f32[512,128]{1,0:T(8,128)S(1)} %collective-permute-done.2, f32[512,128]{1,0:T(8,128)S(1)} %collective-permute-done, f32[]{:T(128)S(6)} %mul.184, f32[512]{0:T(512)S(1)} %get-tuple-element.286, f32[1024,512]{1,0:T(8,128)S(1)} %get-tuple-element.287, f32[1024,128]{1,0:T(8,128)S(1)} %get-tuple-element.326), kind=kOutput, calls=%fused_computation.8.clone.1 | convolution fusion | flops 805634048 | bytes 3409924 | tf_op jit(solution)/shard_map/while/body/eval_jaxpr/dot_general | solution.py:31
  43.3 8.3 %collective-permute-done.1 = f32[512,128]{1,0:T(8,128)S(1)} collective-permute-done((f32[512,128]{1,0:T(8,128)S(1)}, f32[512,128]{1,0:T(8,128)S(1)}, u32[]{:S(2)}, u32[]{:S(2)}) %collective-permute-start.1) | collective-permute-done | bytes 262176 | tf_op jit(solution)/shard_map/while/body/eval_jaxpr/ppermute | solution.py:9
  51.6 1.9 fusion.54
  56.2 2.6 %fusion.56 = (f32[1024]{0:T(1024)S(1)}, f32[512]{0:T(512)S(1)}, f32[1024,512]{1,0:T(8,128)S(1)}) fusion(f32[1024,128]{1,0:T(8,128)S(1)} %get-tuple-element.326, f32[512,128]{1,0:T(8,128)S(1)} %collective-permute-done, f32[512]{0:T(512)S(1)} %multiply_reduce_fusion.4, f32[1024]{0:T(1024)S(1)} %get-tuple-element.325, f32[1024,512]{1,0:T(8,128)S(1)} %fusion.54, ...), kind=kOutput, calls=%fused_computation.30.clone.1 | convolution fusion | flops 810023424 | bytes 7090176 | tf_op jit(solution)/shard_map/while/body/eval_jaxpr/dot_general | solution.py:16
  58.8 2.0 multiply_add_fusion.5
  60.8 3.5 %multiply_add_fusion.4 = f32[512,128]{1,0:T(8,128)S(1)} fusion(f32[512,128]{1,0:T(8,128)S(1)} %collective-permute-done.2, f32[512,128]{1,0:T(8,128)S(1)} %collective-permute-done, f32[]{:T(128)S(6)} %mul.184, f32[512]{0:T(512)S(1)} %get-tuple-element.286, f32[1024,512]{1,0:T(8,128)S(1)} %get-tuple-element.287, f32[1024,128]{1,0:T(8,128)S(1)} %get-tuple-element.326), kind=kOutput, calls=%fused_computation.8.clone.1 | convolution fusion | flops 805634048 | bytes 3409924 | tf_op jit(solution)/shard_map/while/body/eval_jaxpr/dot_general | solution.py:31
  64.6 8.3 %collective-permute-done.1 = f32[512,128]{1,0:T(8,128)S(1)} collective-permute-done((f32[512,128]{1,0:T(8,128)S(1)}, f32[512,128]{1,0:T(8,128)S(1)}, u32[]{:S(2)}, u32[]{:S(2)}) %collective-permute-start.1) | collective-permute-done | bytes 262176 | tf_op jit(solution)/shard_map/while/body/eval_jaxpr/ppermute | solution.py:9
  72.9 1.9 fusion.54
  77.6 2.6 %fusion.56 = (f32[1024]{0:T(1024)S(1)}, f32[512]{0:T(512)S(1)}, f32[1024,512]{1,0:T(8,128)S(1)}) fusion(f32[1024,128]{1,0:T(8,128)S(1)} %get-tuple-element.326, f32[512,128]{1,0:T(8,128)S(1)} %collective-permute-done, f32[512]{0:T(512)S(1)} %multiply_reduce_fusion.4, f32[1024]{0:T(1024)S(1)} %get-tuple-element.325, f32[1024,512]{1,0:T(8,128)S(1)} %fusion.54, ...), kind=kOutput, calls=%fused_computation.30.clone.1 | convolution fusion | flops 810023424 | bytes 7090176 | tf_op jit(solution)/shard_map/while/body/eval_jaxpr/dot_general | solution.py:16
  80.1 2.0 multiply_add_fusion.5
  82.2 3.5 %multiply_add_fusion.4 = f32[512,128]{1,0:T(8,128)S(1)} fusion(f32[512,128]{1,0:T(8,128)S(1)} %collective-permute-done.2, f32[512,128]{1,0:T(8,128)S(1)} %collective-permute-done, f32[]{:T(128)S(6)} %mul.184, f32[512]{0:T(512)S(1)} %get-tuple-element.286, f32[1024,512]{1,0:T(8,128)S(1)} %get-tuple-element.287, f32[1024,128]{1,0:T(8,128)S(1)} %get-tuple-element.326), kind=kOutput, calls=%fused_computation.8.clone.1 | convolution fusion | flops 805634048 | bytes 3409924 | tf_op jit(solution)/shard_map/while/body/eval_jaxpr/dot_general | solution.py:31
  85.9 8.3 %collective-permute-done.1 = f32[512,128]{1,0:T(8,128)S(1)} collective-permute-done((f32[512,128]{1,0:T(8,128)S(1)}, f32[512,128]{1,0:T(8,128)S(1)}, u32[]{:S(2)}, u32[]{:S(2)}) %collective-permute-start.1) | collective-permute-done | bytes 262176 | tf_op jit(solution)/shard_map/while/body/eval_jaxpr/ppermute | solution.py:9
  94.2 1.9 fusion.54
  98.9 2.6 %fusion.56 = (f32[1024]{0:T(1024)S(1)}, f32[512]{0:T(512)S(1)}, f32[1024,512]{1,0:T(8,128)S(1)}) fusion(f32[1024,128]{1,0:T(8,128)S(1)} %get-tuple-element.326, f32[512,128]{1,0:T(8,128)S(1)} %collective-permute-done, f32[512]{0:T(512)S(1)} %multiply_reduce_fusion.4, f32[1024]{0:T(1024)S(1)} %get-tuple-element.325, f32[1024,512]{1,0:T(8,128)S(1)} %fusion.54, ...), kind=kOutput, calls=%fused_computation.30.clone.1 | convolution fusion | flops 810023424 | bytes 7090176 | tf_op jit(solution)/shard_map/while/body/eval_jaxpr/dot_general | solution.py:16
  101.4 2.0 multiply_add_fusion.5
  103.5 3.5 %multiply_add_fusion.4 = f32[512,128]{1,0:T(8,128)S(1)} fusion(f32[512,128]{1,0:T(8,128)S(1)} %collective-permute-done.2, f32[512,128]{1,0:T(8,128)S(1)} %collective-permute-done, f32[]{:T(128)S(6)} %mul.184, f32[512]{0:T(512)S(1)} %get-tuple-element.286, f32[1024,512]{1,0:T(8,128)S(1)} %get-tuple-element.287, f32[1024,128]{1,0:T(8,128)S(1)} %get-tuple-element.326), kind=kOutput, calls=%fused_computation.8.clone.1 | convolution fusion | flops 805634048 | bytes 3409924 | tf_op jit(solution)/shard_map/while/body/eval_jaxpr/dot_general | solution.py:31
  107.2 8.3 %collective-permute-done.1 = f32[512,128]{1,0:T(8,128)S(1)} collective-permute-done((f32[512,128]{1,0:T(8,128)S(1)}, f32[512,128]{1,0:T(8,128)S(1)}, u32[]{:S(2)}, u32[]{:S(2)}) %collective-permute-start.1) | collective-permute-done | bytes 262176 | tf_op jit(solution)/shard_map/while/body/eval_jaxpr/ppermute | solution.py:9
  115.5 1.9 fusion.54
  120.2 2.6 %fusion.56 = (f32[1024]{0:T(1024)S(1)}, f32[512]{0:T(512)S(1)}, f32[1024,512]{1,0:T(8,128)S(1)}) fusion(f32[1024,128]{1,0:T(8,128)S(1)} %get-tuple-element.326, f32[512,128]{1,0:T(8,128)S(1)} %collective-permute-done, f32[512]{0:T(512)S(1)} %multiply_reduce_fusion.4, f32[1024]{0:T(1024)S(1)} %get-tuple-element.325, f32[1024,512]{1,0:T(8,128)S(1)} %fusion.54, ...), kind=kOutput, calls=%fused_computation.30.clone.1 | convolution fusion | flops 810023424 | bytes 7090176 | tf_op jit(solution)/shard_map/while/body/eval_jaxpr/dot_general | solution.py:16
  122.8 2.0 multiply_add_fusion.5
  124.8 3.5 %multiply_add_fusion.4 = f32[512,128]{1,0:T(8,128)S(1)} fusion(f32[512,128]{1,0:T(8,128)S(1)} %collective-permute-done.2, f32[512,128]{1,0:T(8,128)S(1)} %collective-permute-done, f32[]{:T(128)S(6)} %mul.184, f32[512]{0:T(512)S(1)} %get-tuple-element.286, f32[1024,512]{1,0:T(8,128)S(1)} %get-tuple-element.287, f32[1024,128]{1,0:T(8,128)S(1)} %get-tuple-element.326), kind=kOutput, calls=%fused_computation.8.clone.1 | convolution fusion | flops 805634048 | bytes 3409924 | tf_op jit(solution)/shard_map/while/body/eval_jaxpr/dot_general | solution.py:31
  128.5 8.3 %collective-permute-done.1 = f32[512,128]{1,0:T(8,128)S(1)} collective-permute-done((f32[512,128]{1,0:T(8,128)S(1)}, f32[512,128]{1,0:T(8,128)S(1)}, u32[]{:S(2)}, u32[]{:S(2)}) %collective-permute-start.1) | collective-permute-done | bytes 262176 | tf_op jit(solution)/shard_map/while/body/eval_jaxpr/ppermute | solution.py:9
  136.9 1.9 fusion.54
  141.5 2.6 %fusion.56 = (f32[1024]{0:T(1024)S(1)}, f32[512]{0:T(512)S(1)}, f32[1024,512]{1,0:T(8,128)S(1)}) fusion(f32[1024,128]{1,0:T(8,128)S(1)} %get-tuple-element.326, f32[512,128]{1,0:T(8,128)S(1)} %collective-permute-done, f32[512]{0:T(512)S(1)} %multiply_reduce_fusion.4, f32[1024]{0:T(1024)S(1)} %get-tuple-element.325, f32[1024,512]{1,0:T(8,128)S(1)} %fusion.54, ...), kind=kOutput, calls=%fused_computation.30.clone.1 | convolution fusion | flops 810023424 | bytes 7090176 | tf_op jit(solution)/shard_map/while/body/eval_jaxpr/dot_general | solution.py:16
  144.1 2.0 multiply_add_fusion.5
  146.1 3.5 %multiply_add_fusion.4 = f32[512,128]{1,0:T(8,128)S(1)} fusion(f32[512,128]{1,0:T(8,128)S(1)} %collective-permute-done.2, f32[512,128]{1,0:T(8,128)S(1)} %collective-permute-done, f32[]{:T(128)S(6)} %mul.184, f32[512]{0:T(512)S(1)} %get-tuple-element.286, f32[1024,512]{1,0:T(8,128)S(1)} %get-tuple-element.287, f32[1024,128]{1,0:T(8,128)S(1)} %get-tuple-element.326), kind=kOutput, calls=%fused_computation.8.clone.1 | convolution fusion | flops 805634048 | bytes 3409924 | tf_op jit(solution)/shard_map/while/body/eval_jaxpr/dot_general | solution.py:31
  149.9 8.3 %collective-permute-done.1 = f32[512,128]{1,0:T(8,128)S(1)} collective-permute-done((f32[512,128]{1,0:T(8,128)S(1)}, f32[512,128]{1,0:T(8,128)S(1)}, u32[]{:S(2)}, u32[]{:S(2)}) %collective-permute-start.1) | collective-permute-done | bytes 262176 | tf_op jit(solution)/shard_map/while/body/eval_jaxpr/ppermute | solution.py:9
  158.2 1.9 fusion.54
  162.9 2.6 %fusion.56 = (f32[1024]{0:T(1024)S(1)}, f32[512]{0:T(512)S(1)}, f32[1024,512]{1,0:T(8,128)S(1)}) fusion(f32[1024,128]{1,0:T(8,128)S(1)} %get-tuple-element.326, f32[512,128]{1,0:T(8,128)S(1)} %collective-permute-done, f32[512]{0:T(512)S(1)} %multiply_reduce_fusion.4, f32[1024]{0:T(1024)S(1)} %get-tuple-element.325, f32[1024,512]{1,0:T(8,128)S(1)} %fusion.54, ...), kind=kOutput, calls=%fused_computation.30.clone.1 | convolution fusion | flops 810023424 | bytes 7090176 | tf_op jit(solution)/shard_map/while/body/eval_jaxpr/dot_general | solution.py:16
  165.4 2.0 multiply_add_fusion.5
  167.4 3.5 %multiply_add_fusion.4 = f32[512,128]{1,0:T(8,128)S(1)} fusion(f32[512,128]{1,0:T(8,128)S(1)} %collective-permute-done.2, f32[512,128]{1,0:T(8,128)S(1)} %collective-permute-done, f32[]{:T(128)S(6)} %mul.184, f32[512]{0:T(512)S(1)} %get-tuple-element.286, f32[1024,512]{1,0:T(8,128)S(1)} %get-tuple-element.287, f32[1024,128]{1,0:T(8,128)S(1)} %get-tuple-element.326), kind=kOutput, calls=%fused_computation.8.clone.1 | convolution fusion | flops 805634048 | bytes 3409924 | tf_op jit(solution)/shard_map/while/body/eval_jaxpr/dot_general | solution.py:31
  171.2 8.3 %collective-permute-done.1 = f32[512,128]{1,0:T(8,128)S(1)} collective-permute-done((f32[512,128]{1,0:T(8,128)S(1)}, f32[512,128]{1,0:T(8,128)S(1)}, u32[]{:S(2)}, u32[]{:S(2)}) %collective-permute-start.1) | collective-permute-done | bytes 262176 | tf_op jit(solution)/shard_map/while/body/eval_jaxpr/ppermute | solution.py:9
  179.5 1.9 fusion.54
  181.4 1.9 fusion.55
  184.2 2.6 %fusion.56 = (f32[1024]{0:T(1024)S(1)}, f32[512]{0:T(512)S(1)}, f32[1024,512]{1,0:T(8,128)S(1)}) fusion(f32[1024,128]{1,0:T(8,128)S(1)} %get-tuple-element.326, f32[512,128]{1,0:T(8,128)S(1)} %collective-permute-done, f32[512]{0:T(512)S(1)} %multiply_reduce_fusion.4, f32[1024]{0:T(1024)S(1)} %get-tuple-element.325, f32[1024,512]{1,0:T(8,128)S(1)} %fusion.54, ...), kind=kOutput, calls=%fused_computation.30.clone.1 | convolution fusion | flops 810023424 | bytes 7090176 | tf_op jit(solution)/shard_map/while/body/eval_jaxpr/dot_general | solution.py:16
  186.7 2.0 multiply_add_fusion.5
  188.8 3.5 %multiply_add_fusion.4 = f32[512,128]{1,0:T(8,128)S(1)} fusion(f32[512,128]{1,0:T(8,128)S(1)} %collective-permute-done.2, f32[512,128]{1,0:T(8,128)S(1)} %collective-permute-done, f32[]{:T(128)S(6)} %mul.184, f32[512]{0:T(512)S(1)} %get-tuple-element.286, f32[1024,512]{1,0:T(8,128)S(1)} %get-tuple-element.287, f32[1024,128]{1,0:T(8,128)S(1)} %get-tuple-element.326), kind=kOutput, calls=%fused_computation.8.clone.1 | convolution fusion | flops 805634048 | bytes 3409924 | tf_op jit(solution)/shard_map/while/body/eval_jaxpr/dot_general | solution.py:31
  193.2 7.3 %collective-permute-done.3 = f32[512,128]{1,0:T(8,128)S(1)} collective-permute-done((f32[512,128]{1,0:T(8,128)S(1)}, f32[512,128]{1,0:T(8,128)S(1)}, u32[]{:S(2)}, u32[]{:S(2)}) %collective-permute-start.3) | collective-permute-done | bytes 262176 | tf_op jit(solution)/shard_map/ppermute | solution.py:9
  200.4 5.1 %reduce-scatter.2.cloned.1.call-done = f32[512,128]{1,0:T(8,128)} async-done(((f32[1024,128]{1,0:T(8,128)}), f32[512,128]{1,0:T(8,128)}) %reduce-scatter.2.cloned.1.call-update) | async-done | bytes 262160 | tf_op jit(solution)/shard_map/reduce_scatter | solution.py:61
  (94 shorter events, 27.4 us)
Async XLA Ops:
  6.5 3.1 %copy-start.1 = (f32[1024,128]{1,0:T(8,128)S(1)}, f32[1024,128]{1,0:T(8,128)}, u32[]{:S(2)}) copy-start(f32[1024,128]{1,0:T(8,128)} %param.5) | copy-start | bytes 1572868
  6.5 3.1 %copy-start = (f32[1024,128]{1,0:T(8,128)S(1)}, f32[1024,128]{1,0:T(8,128)}, u32[]{:S(2)}) copy-start(f32[1024,128]{1,0:T(8,128)} %param.4) | copy-start | bytes 1572868
  6.5 199.0 %reduce-scatter.2.cloned.1.call-start = ((), (), s32[]{:S(2)}) async-start(), calls=%async_computation.1 | async-start | bytes 786432 | tf_op jit(solution)/shard_map/reduce_scatter | solution.py:61
  15.9 4.6 %copy-start.3 = (f32[512,128]{1,0:T(8,128)S(1)}, f32[512,128]{1,0:T(8,128)}, u32[]{:S(2)}) copy-start(f32[512,128]{1,0:T(8,128)} %custom-call) | copy-start | bytes 786436
  20.7 9.6 %collective-permute-start.1 = (f32[512,128]{1,0:T(8,128)S(1)}, f32[512,128]{1,0:T(8,128)S(1)}, u32[]{:S(2)}, u32[]{:S(2)}) collective-permute-start(f32[512,128]{1,0:T(8,128)S(1)} %get-tuple-element.306), channel_id=1, source_target_pairs={{0,2},{2,4},{4,6},{6,8},{8,10},{10,12},{12,14},{14,16},{16,18},{18... | collective-permute-start | bytes 786440 | tf_op jit(solution)/shard_map/while/body/eval_jaxpr/ppermute | solution.py:9
  21.2 12.8 %collective-permute-start = (f32[512,128]{1,0:T(8,128)}, f32[512,128]{1,0:T(8,128)S(1)}, u32[]{:S(2)}, u32[]{:S(2)}) collective-permute-start(f32[512,128]{1,0:T(8,128)} %get-tuple-element.305), channel_id=1, source_target_pairs={{0,2},{2,4},{4,6},{6,8},{8,10},{10,12},{12,14},{14,16},{16,18},{18... | collective-permute-start | bytes 786440 | tf_op jit(solution)/shard_map/while/body/eval_jaxpr/ppermute | solution.py:9
  23.9 15.7 %collective-permute-start.2 = (f32[512,128]{1,0:T(8,128)S(1)}, f32[512,128]{1,0:T(8,128)S(1)}, u32[]{:S(2)}, u32[]{:S(2)}) collective-permute-start(f32[512,128]{1,0:T(8,128)S(1)} %broadcast_select_fusion.2), channel_id=1, source_target_pairs={{0,2},{2,4},{4,6},{6,8},{8,10},{10,12},{12,14},{14,16},{16,18},{18... | collective-permute-start | bytes 786440 | tf_op jit(solution)/shard_map/while/body/eval_jaxpr/ppermute | solution.py:9
  43.0 8.5 %collective-permute-start.1 = (f32[512,128]{1,0:T(8,128)S(1)}, f32[512,128]{1,0:T(8,128)S(1)}, u32[]{:S(2)}, u32[]{:S(2)}) collective-permute-start(f32[512,128]{1,0:T(8,128)S(1)} %get-tuple-element.306), channel_id=1, source_target_pairs={{0,2},{2,4},{4,6},{6,8},{8,10},{10,12},{12,14},{14,16},{16,18},{18... | collective-permute-start | bytes 786440 | tf_op jit(solution)/shard_map/while/body/eval_jaxpr/ppermute | solution.py:9
  43.1 12.3 %collective-permute-start = (f32[512,128]{1,0:T(8,128)}, f32[512,128]{1,0:T(8,128)S(1)}, u32[]{:S(2)}, u32[]{:S(2)}) collective-permute-start(f32[512,128]{1,0:T(8,128)} %get-tuple-element.305), channel_id=1, source_target_pairs={{0,2},{2,4},{4,6},{6,8},{8,10},{10,12},{12,14},{14,16},{16,18},{18... | collective-permute-start | bytes 786440 | tf_op jit(solution)/shard_map/while/body/eval_jaxpr/ppermute | solution.py:9
  43.2 17.7 %collective-permute-start.2 = (f32[512,128]{1,0:T(8,128)S(1)}, f32[512,128]{1,0:T(8,128)S(1)}, u32[]{:S(2)}, u32[]{:S(2)}) collective-permute-start(f32[512,128]{1,0:T(8,128)S(1)} %broadcast_select_fusion.2), channel_id=1, source_target_pairs={{0,2},{2,4},{4,6},{6,8},{8,10},{10,12},{12,14},{14,16},{16,18},{18... | collective-permute-start | bytes 786440 | tf_op jit(solution)/shard_map/while/body/eval_jaxpr/ppermute | solution.py:9
  64.3 8.5 %collective-permute-start.1 = (f32[512,128]{1,0:T(8,128)S(1)}, f32[512,128]{1,0:T(8,128)S(1)}, u32[]{:S(2)}, u32[]{:S(2)}) collective-permute-start(f32[512,128]{1,0:T(8,128)S(1)} %get-tuple-element.306), channel_id=1, source_target_pairs={{0,2},{2,4},{4,6},{6,8},{8,10},{10,12},{12,14},{14,16},{16,18},{18... | collective-permute-start | bytes 786440 | tf_op jit(solution)/shard_map/while/body/eval_jaxpr/ppermute | solution.py:9
  64.4 12.3 %collective-permute-start = (f32[512,128]{1,0:T(8,128)}, f32[512,128]{1,0:T(8,128)S(1)}, u32[]{:S(2)}, u32[]{:S(2)}) collective-permute-start(f32[512,128]{1,0:T(8,128)} %get-tuple-element.305), channel_id=1, source_target_pairs={{0,2},{2,4},{4,6},{6,8},{8,10},{10,12},{12,14},{14,16},{16,18},{18... | collective-permute-start | bytes 786440 | tf_op jit(solution)/shard_map/while/body/eval_jaxpr/ppermute | solution.py:9
  64.5 17.6 %collective-permute-start.2 = (f32[512,128]{1,0:T(8,128)S(1)}, f32[512,128]{1,0:T(8,128)S(1)}, u32[]{:S(2)}, u32[]{:S(2)}) collective-permute-start(f32[512,128]{1,0:T(8,128)S(1)} %broadcast_select_fusion.2), channel_id=1, source_target_pairs={{0,2},{2,4},{4,6},{6,8},{8,10},{10,12},{12,14},{14,16},{16,18},{18... | collective-permute-start | bytes 786440 | tf_op jit(solution)/shard_map/while/body/eval_jaxpr/ppermute | solution.py:9
  85.7 8.5 %collective-permute-start.1 = (f32[512,128]{1,0:T(8,128)S(1)}, f32[512,128]{1,0:T(8,128)S(1)}, u32[]{:S(2)}, u32[]{:S(2)}) collective-permute-start(f32[512,128]{1,0:T(8,128)S(1)} %get-tuple-element.306), channel_id=1, source_target_pairs={{0,2},{2,4},{4,6},{6,8},{8,10},{10,12},{12,14},{14,16},{16,18},{18... | collective-permute-start | bytes 786440 | tf_op jit(solution)/shard_map/while/body/eval_jaxpr/ppermute | solution.py:9
  85.7 12.3 %collective-permute-start = (f32[512,128]{1,0:T(8,128)}, f32[512,128]{1,0:T(8,128)S(1)}, u32[]{:S(2)}, u32[]{:S(2)}) collective-permute-start(f32[512,128]{1,0:T(8,128)} %get-tuple-element.305), channel_id=1, source_target_pairs={{0,2},{2,4},{4,6},{6,8},{8,10},{10,12},{12,14},{14,16},{16,18},{18... | collective-permute-start | bytes 786440 | tf_op jit(solution)/shard_map/while/body/eval_jaxpr/ppermute | solution.py:9
  85.8 17.6 %collective-permute-start.2 = (f32[512,128]{1,0:T(8,128)S(1)}, f32[512,128]{1,0:T(8,128)S(1)}, u32[]{:S(2)}, u32[]{:S(2)}) collective-permute-start(f32[512,128]{1,0:T(8,128)S(1)} %broadcast_select_fusion.2), channel_id=1, source_target_pairs={{0,2},{2,4},{4,6},{6,8},{8,10},{10,12},{12,14},{14,16},{16,18},{18... | collective-permute-start | bytes 786440 | tf_op jit(solution)/shard_map/while/body/eval_jaxpr/ppermute | solution.py:9
  107.0 8.5 %collective-permute-start.1 = (f32[512,128]{1,0:T(8,128)S(1)}, f32[512,128]{1,0:T(8,128)S(1)}, u32[]{:S(2)}, u32[]{:S(2)}) collective-permute-start(f32[512,128]{1,0:T(8,128)S(1)} %get-tuple-element.306), channel_id=1, source_target_pairs={{0,2},{2,4},{4,6},{6,8},{8,10},{10,12},{12,14},{14,16},{16,18},{18... | collective-permute-start | bytes 786440 | tf_op jit(solution)/shard_map/while/body/eval_jaxpr/ppermute | solution.py:9
  107.0 12.3 %collective-permute-start = (f32[512,128]{1,0:T(8,128)}, f32[512,128]{1,0:T(8,128)S(1)}, u32[]{:S(2)}, u32[]{:S(2)}) collective-permute-start(f32[512,128]{1,0:T(8,128)} %get-tuple-element.305), channel_id=1, source_target_pairs={{0,2},{2,4},{4,6},{6,8},{8,10},{10,12},{12,14},{14,16},{16,18},{18... | collective-permute-start | bytes 786440 | tf_op jit(solution)/shard_map/while/body/eval_jaxpr/ppermute | solution.py:9
  107.1 17.7 %collective-permute-start.2 = (f32[512,128]{1,0:T(8,128)S(1)}, f32[512,128]{1,0:T(8,128)S(1)}, u32[]{:S(2)}, u32[]{:S(2)}) collective-permute-start(f32[512,128]{1,0:T(8,128)S(1)} %broadcast_select_fusion.2), channel_id=1, source_target_pairs={{0,2},{2,4},{4,6},{6,8},{8,10},{10,12},{12,14},{14,16},{16,18},{18... | collective-permute-start | bytes 786440 | tf_op jit(solution)/shard_map/while/body/eval_jaxpr/ppermute | solution.py:9
  128.3 8.5 %collective-permute-start.1 = (f32[512,128]{1,0:T(8,128)S(1)}, f32[512,128]{1,0:T(8,128)S(1)}, u32[]{:S(2)}, u32[]{:S(2)}) collective-permute-start(f32[512,128]{1,0:T(8,128)S(1)} %get-tuple-element.306), channel_id=1, source_target_pairs={{0,2},{2,4},{4,6},{6,8},{8,10},{10,12},{12,14},{14,16},{16,18},{18... | collective-permute-start | bytes 786440 | tf_op jit(solution)/shard_map/while/body/eval_jaxpr/ppermute | solution.py:9
  128.4 12.3 %collective-permute-start = (f32[512,128]{1,0:T(8,128)}, f32[512,128]{1,0:T(8,128)S(1)}, u32[]{:S(2)}, u32[]{:S(2)}) collective-permute-start(f32[512,128]{1,0:T(8,128)} %get-tuple-element.305), channel_id=1, source_target_pairs={{0,2},{2,4},{4,6},{6,8},{8,10},{10,12},{12,14},{14,16},{16,18},{18... | collective-permute-start | bytes 786440 | tf_op jit(solution)/shard_map/while/body/eval_jaxpr/ppermute | solution.py:9
  128.5 17.6 %collective-permute-start.2 = (f32[512,128]{1,0:T(8,128)S(1)}, f32[512,128]{1,0:T(8,128)S(1)}, u32[]{:S(2)}, u32[]{:S(2)}) collective-permute-start(f32[512,128]{1,0:T(8,128)S(1)} %broadcast_select_fusion.2), channel_id=1, source_target_pairs={{0,2},{2,4},{4,6},{6,8},{8,10},{10,12},{12,14},{14,16},{16,18},{18... | collective-permute-start | bytes 786440 | tf_op jit(solution)/shard_map/while/body/eval_jaxpr/ppermute | solution.py:9
  149.6 8.5 %collective-permute-start.1 = (f32[512,128]{1,0:T(8,128)S(1)}, f32[512,128]{1,0:T(8,128)S(1)}, u32[]{:S(2)}, u32[]{:S(2)}) collective-permute-start(f32[512,128]{1,0:T(8,128)S(1)} %get-tuple-element.306), channel_id=1, source_target_pairs={{0,2},{2,4},{4,6},{6,8},{8,10},{10,12},{12,14},{14,16},{16,18},{18... | collective-permute-start | bytes 786440 | tf_op jit(solution)/shard_map/while/body/eval_jaxpr/ppermute | solution.py:9
  149.7 12.3 %collective-permute-start = (f32[512,128]{1,0:T(8,128)}, f32[512,128]{1,0:T(8,128)S(1)}, u32[]{:S(2)}, u32[]{:S(2)}) collective-permute-start(f32[512,128]{1,0:T(8,128)} %get-tuple-element.305), channel_id=1, source_target_pairs={{0,2},{2,4},{4,6},{6,8},{8,10},{10,12},{12,14},{14,16},{16,18},{18... | collective-permute-start | bytes 786440 | tf_op jit(solution)/shard_map/while/body/eval_jaxpr/ppermute | solution.py:9
  149.8 17.6 %collective-permute-start.2 = (f32[512,128]{1,0:T(8,128)S(1)}, f32[512,128]{1,0:T(8,128)S(1)}, u32[]{:S(2)}, u32[]{:S(2)}) collective-permute-start(f32[512,128]{1,0:T(8,128)S(1)} %broadcast_select_fusion.2), channel_id=1, source_target_pairs={{0,2},{2,4},{4,6},{6,8},{8,10},{10,12},{12,14},{14,16},{16,18},{18... | collective-permute-start | bytes 786440 | tf_op jit(solution)/shard_map/while/body/eval_jaxpr/ppermute | solution.py:9
  171.0 8.5 %collective-permute-start.1 = (f32[512,128]{1,0:T(8,128)S(1)}, f32[512,128]{1,0:T(8,128)S(1)}, u32[]{:S(2)}, u32[]{:S(2)}) collective-permute-start(f32[512,128]{1,0:T(8,128)S(1)} %get-tuple-element.306), channel_id=1, source_target_pairs={{0,2},{2,4},{4,6},{6,8},{8,10},{10,12},{12,14},{14,16},{16,18},{18... | collective-permute-start | bytes 786440 | tf_op jit(solution)/shard_map/while/body/eval_jaxpr/ppermute | solution.py:9
  171.0 12.3 %collective-permute-start = (f32[512,128]{1,0:T(8,128)}, f32[512,128]{1,0:T(8,128)S(1)}, u32[]{:S(2)}, u32[]{:S(2)}) collective-permute-start(f32[512,128]{1,0:T(8,128)} %get-tuple-element.305), channel_id=1, source_target_pairs={{0,2},{2,4},{4,6},{6,8},{8,10},{10,12},{12,14},{14,16},{16,18},{18... | collective-permute-start | bytes 786440 | tf_op jit(solution)/shard_map/while/body/eval_jaxpr/ppermute | solution.py:9
  171.1 17.7 %collective-permute-start.2 = (f32[512,128]{1,0:T(8,128)S(1)}, f32[512,128]{1,0:T(8,128)S(1)}, u32[]{:S(2)}, u32[]{:S(2)}) collective-permute-start(f32[512,128]{1,0:T(8,128)S(1)} %broadcast_select_fusion.2), channel_id=1, source_target_pairs={{0,2},{2,4},{4,6},{6,8},{8,10},{10,12},{12,14},{14,16},{16,18},{18... | collective-permute-start | bytes 786440 | tf_op jit(solution)/shard_map/while/body/eval_jaxpr/ppermute | solution.py:9
  192.3 0.8 copy-start.2
  193.1 7.3 %collective-permute-start.3 = (f32[512,128]{1,0:T(8,128)S(1)}, f32[512,128]{1,0:T(8,128)S(1)}, u32[]{:S(2)}, u32[]{:S(2)}) collective-permute-start(f32[512,128]{1,0:T(8,128)S(1)} %get-tuple-element.182), channel_id=1, source_target_pairs={{0,16},{2,18},{4,20},{6,22},{8,24},{10,26},{12,28},{14,30},{16,0},... | collective-permute-start | bytes 786440 | tf_op jit(solution)/shard_map/ppermute | solution.py:9
Sparse Core Ops, SparseCore 0:
  193.2 12.2 reduce-scatter.1
where the time goes:
time: 214 us
  matrix products  108 us (50%)
  waiting for transfers between devices  76.8 us (36%)
  between operations  13.5 us (6%)
  local copies, waits for them, and re-layouts  6.58 us (3%)
  starting transfers between devices  4.54 us (2%)
  other arithmetic  4.01 us (2%)
    ppermute x25, waiting for transfers between devices, shifted(): return lax.ppermute(x, axis, [(i, (i + by) % peers) for i in range(peers)])  71.7 us
    dot_general x8, matrix products, partner_term(): lax.dot_general(weight, own_feat, (((0,), (0,)), ((), ())), precision=lax...  27.9 us
    dot_general x9, matrix products, pair_terms(): cross = jnp.dot(own_feat, part_feat.T, precision=hi)  23.8 us
    dot_general x9, matrix products, pair_terms(): jnp.dot(weight, part_feat, precision=hi)  20.8 us
    dot_general x9, matrix products, pair_terms(): jnp.dot(own_fac[:, rank:], part_fac[:, :rank].T, precision=hi)  17.9 us
    dot_general x9, matrix products, pair_terms(): coupling = jnp.dot(own_fac[:, :rank], part_fac[:, rank:].T, precision=hi)  17.2 us
    while x16, local copies, waits for them, and re-layouts  5.79 us
    reduce_scatter x1, waiting for transfers between devices, body(): summed = lax.psum_scatter(own_acc, 'rep', scatter_dimension=0, tiled=True)  5.08 us
  transfers between devices with their start and end apart: 26, of which 10 were waited for; matrix products, arithmetic and copies ran while one was open for 35% of the time, Pallas kernels for 0%

commit v1 on v0

v1 whole, which is shorter than its diff:
```python
import functools
import math

import jax
import jax.numpy as jnp
from jax import lax
from jax.experimental import pallas as pl
from jax.experimental.pallas import tpu as pltpu
from jax.sharding import PartitionSpec as P

F32, BF16 = jnp.float32, jnp.bfloat16
NT = (((1,), (1,)), ((), ()))
VMEM_LIMIT = 56 << 20


def split(x):
    high = x.astype(BF16)
    low = (x - high.astype(F32)).astype(BF16)
    return high, low


def scaled(feat, fac):
    width = feat.shape[1]
    feat = feat * math.sqrt(math.log2(math.e) / width)
    norm = jnp.sum(feat * feat, axis=1, keepdims=True)
    return feat, fac * jnp.exp2(-0.5 * norm)


def prep_kernel(rows_ref, feat_ref, fac_ref):
    width = rows_ref.shape[1] // 2
    feat, fac = scaled(rows_ref[:, :width], rows_ref[:, width:])
    for out, x in ((feat_ref, feat), (fac_ref, fac)):
        high, low = split(x)
        out[:, :width] = high
        out[:, width:] = low


def prep(rows):
    count, width = rows.shape
    block = min(512, count)
    spec = pl.BlockSpec((block, width), lambda i: (i, 0))
    return pl.pallas_call(
        prep_kernel,
        grid=(count // block,),
        in_specs=[spec],
        out_specs=[spec, spec],
        out_shape=[jax.ShapeDtypeStruct((count, width), BF16)] * 2,
        compiler_params=pltpu.CompilerParams(vmem_limit_bytes=VMEM_LIMIT),
        name="prep_rows",
    )(rows)


def pair_kernel(n_units, has_acc, *refs):
    feat_ref, fac_ref = refs[:2]
    units = refs[2 : 2 + n_units]
    acc_ref = refs[2 + n_units] if has_acc else None
    out_ref, cross_rhs, coup_rhs, value = refs[2 + n_units + has_acc :]
    width = out_ref.shape[1]
    first = 0
    for unit in units:
        here = pl.ds(first, unit.shape[0])
        feat, fac = scaled(unit[:, :width], unit[:, width:])
        fac = jnp.concatenate([fac[:, width // 2 :], fac[:, : width // 2]], axis=1)
        high, low = split(feat)
        cross_rhs[here, :] = jnp.concatenate([high, high, low, low], axis=1)
        value[here, :] = jnp.concatenate([high, low], axis=1)
        high, low = split(fac)
        coup_rhs[here, :] = jnp.concatenate([high, high, low, low], axis=1)
        first += unit.shape[0]
    count = first
    tile = math.gcd(256, count)
    rows = math.gcd(1024, out_ref.shape[0])

    def dot_nt(a, b):
        return lax.dot_general(a, b, NT, preferred_element_type=F32)

    def chunk(i, _):
        at = pl.ds(pl.multiple_of(i * rows, rows), rows)
        feat, fac = feat_ref[at, :], fac_ref[at, :]
        total, sums_high, sums_low = None, None, None
        for j in range(0, count, tile):
            here = slice(j, j + tile)
            cross = dot_nt(feat, cross_rhs[here, : 2 * width]) + dot_nt(feat, cross_rhs[here, 2 * width :])
            coup = dot_nt(fac, coup_rhs[here, : 2 * width]) + dot_nt(fac, coup_rhs[here, 2 * width :])
            weight = jnp.exp2(cross) * coup
            high = weight.astype(BF16)
            back = high.astype(F32)
            rest = weight - back
            low = rest.astype(BF16)
            both = jnp.dot(high, value[here, :], preferred_element_type=F32)
            one = jnp.dot(low, value[here, :width], preferred_element_type=F32)
            term = both[:, :width] + both[:, width:] + one
            total = term if total is None else total + term
            for k in range(0, tile, width):
                sums_high = back[:, k : k + width] if sums_high is None else sums_high + back[:, k : k + width]
                rest32 = low.astype(F32)[:, k : k + width]
                sums_low = rest32 if sums_low is None else sums_low + rest32
        sum_high = jnp.sum(sums_high, axis=1, keepdims=True)
        sum_low = jnp.sum(sums_low, axis=1, keepdims=True)
        own_high, own_low = feat[:, :width].astype(F32), feat[:, width:].astype(F32)
        term = total - sum_high * (own_high + own_low) - sum_low * own_high
        out_ref[at, :] = term if acc_ref is None else acc_ref[at, :] + term
        return 0

    lax.fori_loop(0, out_ref.shape[0] // rows, chunk, 0)


def pairs(feat, fac, units, acc=None, start=0, rows=None):
    width = feat.shape[1] // 2
    rows = feat.shape[0] if rows is None else rows
    count = sum(u.shape[0] for u in units)
    block = start // rows
    row_spec = pl.BlockSpec((rows, 2 * width), lambda i: (block, 0))
    acc_spec = pl.BlockSpec((rows, width), lambda i: (block, 0))
    unit_specs = [pl.BlockSpec(u.shape, lambda i: (0, 0)) for u in units]
    has_acc = acc is not None
    whole = rows == feat.shape[0]
    n_pairs = rows * count
    return pl.pallas_call(
        functools.partial(pair_kernel, len(units), has_acc),
        grid=(1,),
        in_specs=[row_spec, row_spec, *unit_specs] + [acc_spec] * has_acc,
        out_specs=pl.BlockSpec((rows, width), lambda i: (0, 0)),
        out_shape=jax.ShapeDtypeStruct((rows, width), F32),
        scratch_shapes=[
            pltpu.VMEM((count, 4 * width), BF16),
            pltpu.VMEM((count, 4 * width), BF16),
            pltpu.VMEM((count, 2 * width), BF16),
        ],
        input_output_aliases={2 + len(units): 0} if has_acc and whole else {},
        compiler_params=pltpu.CompilerParams(vmem_limit_bytes=VMEM_LIMIT),
        cost_estimate=pl.CostEstimate(
            flops=2 * n_pairs * 12 * width, bytes_accessed=8 * rows * width + 8 * count * width, transcendentals=n_pairs
        ),
        name="pair_terms",
    )(feat, fac, *units, *([acc] if has_acc else []))


def ring_order(homes):
    if homes % 2:
        return list(range(homes))
    return list(range(0, homes, 2)) + list(range(homes - 1, 0, -2))


def body(features, factors):
    count, width = features.shape
    replicas = lax.axis_size("rep")
    blocks = lax.axis_size("blk")
    cores = 2 if blocks % 2 == 0 else 1
    homes = blocks // cores
    share = count // replicas
    rep = lax.axis_index("rep")
    order = ring_order(homes)

    def ring(x, by):
        moves = [
            (order[p] * cores + c, order[(p + by) % homes] * cores + c) for p in range(homes) for c in range(cores)
        ]
        return lax.ppermute(x, "blk", moves)

    def other_core(x):
        return lax.ppermute(x, "blk", [(b, b ^ 1) for b in range(blocks)])

    own = jnp.concatenate([features, factors], axis=1)
    own = lax.dynamic_slice_in_dim(jnp.concatenate([own, own]), (rep + 1) % replicas * share, count, 0)
    unit = own[count - share :]

    full = (homes - 1) // 2
    ahead, behind = [unit], [unit]
    for _ in range(full):
        ahead.append(ring(ahead[-1], 1))
        behind.append(ring(behind[-1], -1))
    last = ahead[full:] + behind[full:] if full else []
    if homes % 2 == 0 and homes > 1:
        last = [ring(ahead[full][: share // 2], 1), ring(behind[full][share // 2 :], -1)]
        steps = [[unit]] + [[ahead[s], behind[s]] for s in range(1, full + 1)]
    else:
        steps = [[unit]] + [[ahead[s], behind[s]] for s in range(1, full)]
        if not last:
            steps, last = [], [unit]

    rows = jnp.concatenate([other_core(own), own]) if cores == 2 else own
    feat, fac = prep(rows)
    acc = None
    for units in steps:
        acc = pairs(feat, fac, units, acc)
    if acc is None:
        acc = jnp.zeros((rows.shape[0], width), F32)

    at = 0
    carried = None
    if cores == 2:
        carried = other_core(pairs(feat, fac, last, acc, 0, count))
        at = count
    mine = None
    arrived = []
    for k in range(1, replicas):
        part = pairs(feat, fac, last, acc, at, share)
        if carried is not None:
            part = part + carried[(k - 1) * share : k * share]
        arrived.append(lax.ppermute(part, "rep", [(r, (r + k) % replicas) for r in range(replicas)]))
        at += share
    mine = pairs(feat, fac, last, acc, at, share)
    if carried is not None:
        mine = mine + carried[count - share :]
    for part in arrived:
        mine = mine + part
    return mine * (1.0 / (width * math.sqrt(math.log2(math.e) / width)))


def solution(mesh):
    placed = (P("blk", None), P("blk", None))
    return jax.shard_map(
        body, mesh=mesh, in_specs=placed, out_specs=P(("blk", "rep"), None), check_vma=False
    )
```

time: 214 us -> 89.3 us (0.42)
  matrix products: 108 us -> 0 us
  waiting for transfers between devices: 76.8 us -> 16.5 us
  Pallas kernels: 0 us -> 53.5 us
  between operations: 13.5 us -> 0.06 us
  starting transfers between devices: 4.54 us -> 11.2 us
  local copies, waits for them, and re-layouts: 6.58 us -> 2.15 us
    dot_general x44 -> x0, matrix products: 108 us -> none  [the longest x8 27.9 us: partner_term(): lax.dot_general(weight, own_feat, (((0,), (0,)), ((), ())), precision=lax...]
    ppermute x25 -> x11, waiting for transfers between devices: 71.7 us -> 16.5 us  [the longest x8 12.5 us: ring(): return lax.ppermute(x, 'blk', moves)]
    pallas_call x0 -> x8, Pallas kernels: none -> 53.5 us  [the longest x7 49.6 us: pairs(): pl.pallas_call(functools.partial(pair_kernel, len(units), has_acc), grid=...]
    ppermute x25 -> x11, starting transfers between devices: 4.53 us -> 11.2 us  [the longest x8 9.06 us: ring(): return lax.ppermute(x, 'blk', moves)]
    while x16 -> x0, local copies, waits for them, and re-layouts: 5.79 us -> none
    reduce_scatter x1 -> x0, waiting for transfers between devices: 5.08 us -> none  [body(): summed = lax.psum_scatter(own_acc, 'rep', scatter_dimension=0, tiled=True)]
    concatenate x0 -> x2, other arithmetic: none -> 2.93 us  [the longest x1 1.48 us: body(): rows = jnp.concatenate([other_core(own), own]) if cores == 2 else own]
    reduce_sum x10 -> x0, other arithmetic: 2.16 us -> none  [the longest x9 1.96 us: pair_terms(): part_sq = jnp.sum(part_feat * part_feat, axis=1)]
  transfers between devices with their start and end apart: 26 -> 11, of which waited for: 10 -> 2; matrix products, arithmetic and copies ran while one was open for 35% -> 2% of each run, Pallas kernels for 0% -> 55%
where the time goes in v1:
time: 89.3 us; the launch traced here: 88.9 us
  Pallas kernels  53.5 us (60%)
  waiting for transfers between devices  16.5 us (18%)
  starting transfers between devices  11.2 us (13%)
  other arithmetic  5.61 us (6%)
  local copies, waits for them, and re-layouts  2.15 us (2%)
    pallas_call x7, Pallas kernels, pairs(): pl.pallas_call(functools.partial(pair_kernel, len(units), has_acc), grid=...  49.6 us
    ppermute x8, waiting for transfers between devices, ring(): return lax.ppermute(x, 'blk', moves)  12.5 us
    ppermute x8, starting transfers between devices, ring(): return lax.ppermute(x, 'blk', moves)  9.06 us
    ppermute x1, waiting for transfers between devices, body(): lax.ppermute(part, 'rep', [(r, (r + k) % replicas) for r in range(replica...  3.96 us
    pallas_call x1, Pallas kernels, prep(): pl.pallas_call(prep_kernel, grid=(count // block,), in_specs=[spec], out_...  3.86 us
    unnamed x18, local copies, waits for them, and re-layouts  2.08 us
  transfers between devices with their start and end apart: 11, of which 2 were waited for; matrix products, arithmetic and copies ran while one was open for 2% of the time, Pallas kernels for 55%

profile of v1, /device:TPU:0, one launch (start us, length us, event | category | flops | bytes accessed | tf_op | source)
XLA Modules:
  0.0 88.9 jit_solution(13213666300360550031)
XLA Ops:
  0.0 1.5 %fusion.1 = f32[1024,256]{1,0:T(8,128)S(1)} fusion(s32[]{:T(128)S(6)} %select_n.11, f32[1024,128]{1,0:T(8,128)} %param.2, f32[1024,128]{1,0:T(8,128)} %param.3), kind=kLoop, calls=%fused_computation.6 | loop fusion | flops 786432 | bytes 2097156 | tf_op jit(solution)/shard_map/concatenate | solution.py:165
  1.5 0.5 collective-permute-start
  2.0 0.0 copy-start.2
  2.0 2.6 %collective-permute-start.1 = (f32[512,256]{1,0:T(8,128)S(1)}, f32[512,256]{1,0:T(8,128)S(1)}, u32[]{:S(2)}, u32[]{:S(2)}) collective-permute-start(f32[512,256]{1,0:T(8,128)S(1)} %slice.20.refs_2_), channel_id=1, source_target_pairs={{0,8},{2,10},{8,16},{10,18},{16,24},{18,26},{24,28},{26,30},{28,20... | collective-permute-start | bytes 1572872 | tf_op jit(solution)/shard_map/ppermute | solution.py:159
  4.7 0.0 collective-permute-start.5
  4.7 12.5 %collective-permute-done.1.refs_2_ = f32[512,256]{1,0:T(8,128)S(1)} collective-permute-done((f32[512,256]{1,0:T(8,128)S(1)}, f32[512,256]{1,0:T(8,128)S(1)}, u32[]{:S(2)}, u32[]{:S(2)}) %collective-permute-start.1) | collective-permute-done | bytes 524320 | tf_op jit(solution)/shard_map/ppermute | solution.py:159
  17.2 0.0 copy-start.7
  17.2 1.8 %collective-permute-start.2 = (f32[512,256]{1,0:T(8,128)S(1)}, f32[512,256]{1,0:T(8,128)S(1)}, u32[]{:S(2)}, u32[]{:S(2)}) collective-permute-start(f32[512,256]{1,0:T(8,128)S(1)} %collective-permute-done.1.refs_2_), channel_id=1, source_target_pairs={{0,8},{2,10},{8,16},{10,18},{16,24},{18,26},{24,28},{26,30},{28,20... | collective-permute-start | bytes 1572872 | tf_op jit(solution)/shard_map/ppermute | solution.py:159
  19.0 0.0 collective-permute-done.5.refs_3_
  19.0 0.0 copy-start.8
  19.0 0.2 collective-permute-start.6
  19.2 0.0 collective-permute-done
  19.2 1.5 %pad_maximum_fusion.rows_ref = f32[2048,256]{1,0:T(8,128)} fusion(f32[1024,256]{1,0:T(8,128)S(1)} %fusion.1, f32[1024,256]{1,0:T(8,128)S(1)} %collective-permute-done), kind=kLoop, calls=%fused_computation.4 | loop fusion | flops 524288 | bytes 4194304 | tf_op jit(solution)/shard_map/concatenate | solution.py:182
  20.7 0.0 copy-done.2
  20.7 0.0 copy-done.7
  20.7 0.0 copy-done.8
  20.7 3.9 %prep_rows.1 = (bf16[2048,256]{1,0:T(8,128)(2,1)}, bf16[2048,256]{1,0:T(8,128)(2,1)}) custom-call(f32[2048,256]{1,0:T(8,128)} %pad_maximum_fusion.rows_ref), custom_call_target="tpu_custom_call" | custom-call | tf_op jit(solution)/shard_map/prep_rows/pallas_call | solution.py:42
  24.6 6.6 %pair_terms.7.refs_4_ = f32[2048,128]{1,0:T(8,128)} custom-call(bf16[2048,256]{1,0:T(8,128)(2,1)} %get-tuple-element.7.refs_0_, bf16[2048,256]{1,0:T(8,128)(2,1)} %get-tuple-element.8.refs_1_, f32[512,256]{1,0:T(8,128)} %copy-done.2), custom_call_target="tpu_custom_call" | custom-call | flops 3221225472 | bytes 2621440 | tf_op jit(solution)/shard_map/pair_terms/pallas_call | solution.py:119
  31.2 0.0 collective-permute-done.2.refs_2_
  31.2 0.0 copy-start.6
  31.2 1.8 %collective-permute-start.3 = (f32[512,256]{1,0:T(8,128)S(1)}, f32[512,256]{1,0:T(8,128)S(1)}, u32[]{:S(2)}, u32[]{:S(2)}) collective-permute-start(f32[512,256]{1,0:T(8,128)S(1)} %collective-permute-done.2.refs_2_), channel_id=1, source_target_pairs={{0,8},{2,10},{8,16},{10,18},{16,24},{18,26},{24,28},{26,30},{28,20... | collective-permute-start | bytes 1572872 | tf_op jit(solution)/shard_map/ppermute | solution.py:159
  33.0 10.7 %pair_terms.8.refs_4_ = f32[2048,128]{1,0:T(8,128)} custom-call(bf16[2048,256]{1,0:T(8,128)(2,1)} %get-tuple-element.7.refs_0_, bf16[2048,256]{1,0:T(8,128)(2,1)} %get-tuple-element.8.refs_1_, f32[512,256]{1,0:T(8,128)} %copy-done.7, f32[512,256]{1,0:T(8,128)} %copy-done.8, f32[2048,128]{1,0:T(8,128)} %pair_terms.7.refs_4_), custom_call_target="tpu_custom_call", output_to_operand_aliasing={{}: (4, {})} | custom-call | flops 6442450944 | bytes 3145728 | tf_op jit(solution)/shard_map/pair_terms/pallas_call | solution.py:119
  43.7 0.0 copy-done.6
  43.7 0.0 collective-permute-done.6.refs_3_
  43.7 0.0 copy-start.5
  43.7 0.3 collective-permute-start.7
  44.0 0.5 copy-done.5
  44.5 10.7 %pair_terms.9.refs_4_ = f32[2048,128]{1,0:T(8,128)} custom-call(bf16[2048,256]{1,0:T(8,128)(2,1)} %get-tuple-element.7.refs_0_, bf16[2048,256]{1,0:T(8,128)(2,1)} %get-tuple-element.8.refs_1_, f32[512,256]{1,0:T(8,128)} %copy-done.6, f32[512,256]{1,0:T(8,128)} %copy-done.5, f32[2048,128]{1,0:T(8,128)} %pair_terms.8.refs_4_), custom_call_target="tpu_custom_call", output_to_operand_aliasing={{}: (4, {})} | custom-call | flops 6442450944 | bytes 3145728 | tf_op jit(solution)/shard_map/pair_terms/pallas_call | solution.py:119
  55.2 0.0 collective-permute-done.3.refs_2_
  55.2 1.6 %collective-permute-start.4 = (f32[256,256]{1,0:T(8,128)S(1)}, f32[256,256]{1,0:T(8,128)S(1)}, u32[]{:S(2)}, u32[]{:S(2)}) collective-permute-start(f32[256,256]{1,0:T(8,128)S(1)} %slice.21), channel_id=1, source_target_pairs={{0,8},{2,10},{8,16},{10,18},{16,24},{18,26},{24,28},{26,30},{28,20... | collective-permute-start | bytes 786440 | tf_op jit(solution)/shard_map/ppermute | solution.py:159
  56.8 0.0 collective-permute-done.7.refs_3_
  56.8 0.7 collective-permute-start.8
  57.5 0.0 copy-done.3
  57.5 0.1 copy-done.4
  57.6 10.7 %pair_terms.10.refs_4_ = f32[2048,128]{1,0:T(8,128)} custom-call(bf16[2048,256]{1,0:T(8,128)(2,1)} %get-tuple-element.7.refs_0_, bf16[2048,256]{1,0:T(8,128)(2,1)} %get-tuple-element.8.refs_1_, f32[512,256]{1,0:T(8,128)} %copy-done.3, f32[512,256]{1,0:T(8,128)} %copy-done.4, f32[2048,128]{1,0:T(8,128)} %pair_terms.9.refs_4_), custom_call_target="tpu_custom_call", output_to_operand_aliasing={{}: (4, {})} | custom-call | flops 6442450944 | bytes 3145728 | tf_op jit(solution)/shard_map/pair_terms/pallas_call | solution.py:119
  68.3 0.0 collective-permute-done.4.refs_2_
  68.3 0.0 collective-permute-done.8.refs_3_
  68.3 0.7 copy-done
  69.0 0.7 copy-done.1
  69.7 4.5 %pair_terms.12 = f32[1024,128]{1,0:T(8,128)} custom-call(bf16[2048,256]{1,0:T(8,128)(2,1)} %get-tuple-element.7.refs_0_, bf16[2048,256]{1,0:T(8,128)(2,1)} %get-tuple-element.8.refs_1_, f32[256,256]{1,0:T(8,128)} %copy-done, f32[256,256]{1,0:T(8,128)} %copy-done.1, f32[2048,128]{1,0:T(8,128)} %pair_terms.10.refs_4_), custom_call_target="tpu_custom_call" | custom-call | flops 1610612736 | bytes 1572864 | tf_op jit(solution)/shard_map/pair_terms/pallas_call | solution.py:119
  74.2 0.0 collective-permute-start.9
  74.2 3.2 %pair_terms.13 = f32[512,128]{1,0:T(8,128)} custom-call(bf16[2048,256]{1,0:T(8,128)(2,1)} %get-tuple-element.7.refs_0_, bf16[2048,256]{1,0:T(8,128)(2,1)} %get-tuple-element.8.refs_1_, f32[256,256]{1,0:T(8,128)} %copy-done, f32[256,256]{1,0:T(8,128)} %copy-done.1, f32[2048,128]{1,0:T(8,128)} %pair_terms.10.refs_4_), custom_call_target="tpu_custom_call" | custom-call | flops 805306368 | bytes 1048576 | tf_op jit(solution)/shard_map/pair_terms/pallas_call | solution.py:119
  77.5 0.0 collective-permute-done.9
  77.5 1.0 %slice_add_fusion = f32[512,128]{1,0:T(8,128)S(1)} fusion(f32[512,128]{1,0:T(8,128)} %pair_terms.13, f32[1024,128]{1,0:T(8,128)S(1)} %collective-permute-done.9), kind=kLoop, calls=%fused_computation.8 | loop fusion | flops 65536 | bytes 786432 | tf_op jit(solution)/shard_map/add | solution.py:200
  78.4 1.6 %collective-permute-start.10 = (f32[512,128]{1,0:T(8,128)S(1)}, f32[512,128]{1,0:T(8,128)S(1)}, u32[]{:S(2)}, u32[]{:S(2)}) collective-permute-start(f32[512,128]{1,0:T(8,128)S(1)} %slice_add_fusion), channel_id=1, source_target_pairs={{0,1},{1,0},{2,3},{3,2},{4,5},{5,4},{6,7},{7,6},{8,9},{9,8},{10,11... | collective-permute-start | bytes 786440 | tf_op jit(solution)/shard_map/ppermute | solution.py:201
  80.0 3.2 %pair_terms.11 = f32[512,128]{1,0:T(8,128)} custom-call(bf16[2048,256]{1,0:T(8,128)(2,1)} %get-tuple-element.7.refs_0_, bf16[2048,256]{1,0:T(8,128)(2,1)} %get-tuple-element.8.refs_1_, f32[256,256]{1,0:T(8,128)} %copy-done, f32[256,256]{1,0:T(8,128)} %copy-done.1, f32[2048,128]{1,0:T(8,128)} %pair_terms.10.refs_4_), custom_call_target="tpu_custom_call" | custom-call | flops 805306368 | bytes 1048576 | tf_op jit(solution)/shard_map/pair_terms/pallas_call | solution.py:119
  83.3 4.0 %collective-permute-done.10 = f32[512,128]{1,0:T(8,128)S(1)} collective-permute-done((f32[512,128]{1,0:T(8,128)S(1)}, f32[512,128]{1,0:T(8,128)S(1)}, u32[]{:S(2)}, u32[]{:S(2)}) %collective-permute-start.10) | collective-permute-done | bytes 262176 | tf_op jit(solution)/shard_map/ppermute | solution.py:201
  87.2 1.7 %fusion.4 = f32[512,128]{1,0:T(8,128)} fusion(f32[512,128]{1,0:T(8,128)S(1)} %collective-permute-done.10, f32[512,128]{1,0:T(8,128)} %pair_terms.11, f32[1024,128]{1,0:T(8,128)S(1)} %collective-permute-done.9), kind=kLoop, calls=%fused_computation.11 | loop fusion | flops 196608 | bytes 1048576 | tf_op jit(solution)/shard_map/mul | solution.py:208
  (7 shorter events, 0.1 us)
Async XLA Ops:
  1.5 17.8 %collective-permute-start = (f32[1024,256]{1,0:T(8,128)S(1)}, f32[1024,256]{1,0:T(8,128)S(1)}, u32[]{:S(2)}, u32[]{:S(2)}) collective-permute-start(f32[1024,256]{1,0:T(8,128)S(1)} %fusion.1), channel_id=1, source_target_pairs={{0,2},{2,0},{4,6},{6,4},{8,10},{10,8},{12,14},{14,12},{16,18},{18,... | collective-permute-start | bytes 3145736 | tf_op jit(solution)/shard_map/ppermute | solution.py:162
  2.0 18.7 %copy-start.2 = (f32[512,256]{1,0:T(8,128)}, f32[512,256]{1,0:T(8,128)S(1)}, u32[]{:S(2)}) copy-start(f32[512,256]{1,0:T(8,128)S(1)} %slice.20.refs_2_) | copy-start | bytes 1572868
  2.0 15.2 %collective-permute-start.1 = (f32[512,256]{1,0:T(8,128)S(1)}, f32[512,256]{1,0:T(8,128)S(1)}, u32[]{:S(2)}, u32[]{:S(2)}) collective-permute-start(f32[512,256]{1,0:T(8,128)S(1)} %slice.20.refs_2_), channel_id=1, source_target_pairs={{0,8},{2,10},{8,16},{10,18},{16,24},{18,26},{24,28},{26,30},{28,20... | collective-permute-start | bytes 1572872 | tf_op jit(solution)/shard_map/ppermute | solution.py:159
  4.7 14.3 %collective-permute-start.5 = (f32[512,256]{1,0:T(8,128)S(1)}, f32[512,256]{1,0:T(8,128)S(1)}, u32[]{:S(2)}, u32[]{:S(2)}) collective-permute-start(f32[512,256]{1,0:T(8,128)S(1)} %slice.20.refs_2_), channel_id=1, source_target_pairs={{0,4},{2,6},{8,0},{10,2},{16,8},{18,10},{24,16},{26,18},{28,24},{3... | collective-permute-start | bytes 1572872 | tf_op jit(solution)/shard_map/ppermute | solution.py:159
  17.2 3.5 %copy-start.7 = (f32[512,256]{1,0:T(8,128)}, f32[512,256]{1,0:T(8,128)S(1)}, u32[]{:S(2)}) copy-start(f32[512,256]{1,0:T(8,128)S(1)} %collective-permute-done.1.refs_2_) | copy-start | bytes 1572868
  17.2 14.0 %collective-permute-start.2 = (f32[512,256]{1,0:T(8,128)S(1)}, f32[512,256]{1,0:T(8,128)S(1)}, u32[]{:S(2)}, u32[]{:S(2)}) collective-permute-start(f32[512,256]{1,0:T(8,128)S(1)} %collective-permute-done.1.refs_2_), channel_id=1, source_target_pairs={{0,8},{2,10},{8,16},{10,18},{16,24},{18,26},{24,28},{26,30},{28,20... | collective-permute-start | bytes 1572872 | tf_op jit(solution)/shard_map/ppermute | solution.py:159
  19.0 1.7 %copy-start.8 = (f32[512,256]{1,0:T(8,128)}, f32[512,256]{1,0:T(8,128)S(1)}, u32[]{:S(2)}) copy-start(f32[512,256]{1,0:T(8,128)S(1)} %collective-permute-done.5.refs_3_) | copy-start | bytes 1572868
  19.0 24.7 %collective-permute-start.6 = (f32[512,256]{1,0:T(8,128)S(1)}, f32[512,256]{1,0:T(8,128)S(1)}, u32[]{:S(2)}, u32[]{:S(2)}) collective-permute-start(f32[512,256]{1,0:T(8,128)S(1)} %collective-permute-done.5.refs_3_), channel_id=1, source_target_pairs={{0,4},{2,6},{8,0},{10,2},{16,8},{18,10},{24,16},{26,18},{28,24},{3... | collective-permute-start | bytes 1572872 | tf_op jit(solution)/shard_map/ppermute | solution.py:159
  31.2 12.5 %copy-start.6 = (f32[512,256]{1,0:T(8,128)}, f32[512,256]{1,0:T(8,128)S(1)}, u32[]{:S(2)}) copy-start(f32[512,256]{1,0:T(8,128)S(1)} %collective-permute-done.2.refs_2_) | copy-start | bytes 1572868
  31.2 23.9 %collective-permute-start.3 = (f32[512,256]{1,0:T(8,128)S(1)}, f32[512,256]{1,0:T(8,128)S(1)}, u32[]{:S(2)}, u32[]{:S(2)}) collective-permute-start(f32[512,256]{1,0:T(8,128)S(1)} %collective-permute-done.2.refs_2_), channel_id=1, source_target_pairs={{0,8},{2,10},{8,16},{10,18},{16,24},{18,26},{24,28},{26,30},{28,20... | collective-permute-start | bytes 1572872 | tf_op jit(solution)/shard_map/ppermute | solution.py:159
  43.7 0.8 copy-start.5
  43.7 13.1 %collective-permute-start.7 = (f32[512,256]{1,0:T(8,128)S(1)}, f32[512,256]{1,0:T(8,128)S(1)}, u32[]{:S(2)}, u32[]{:S(2)}) collective-permute-start(f32[512,256]{1,0:T(8,128)S(1)} %collective-permute-done.6.refs_3_), channel_id=1, source_target_pairs={{0,4},{2,6},{8,0},{10,2},{16,8},{18,10},{24,16},{26,18},{28,24},{3... | collective-permute-start | bytes 1572872 | tf_op jit(solution)/shard_map/ppermute | solution.py:159
  55.2 2.4 %copy-start.3 = (f32[512,256]{1,0:T(8,128)}, f32[512,256]{1,0:T(8,128)S(1)}, u32[]{:S(2)}) copy-start(f32[512,256]{1,0:T(8,128)S(1)} %collective-permute-done.3.refs_2_) | copy-start | bytes 1572868
  55.2 13.1 %collective-permute-start.4 = (f32[256,256]{1,0:T(8,128)S(1)}, f32[256,256]{1,0:T(8,128)S(1)}, u32[]{:S(2)}, u32[]{:S(2)}) collective-permute-start(f32[256,256]{1,0:T(8,128)S(1)} %slice.21), channel_id=1, source_target_pairs={{0,8},{2,10},{8,16},{10,18},{16,24},{18,26},{24,28},{26,30},{28,20... | collective-permute-start | bytes 786440 | tf_op jit(solution)/shard_map/ppermute | solution.py:159
  56.8 0.8 copy-start.4
  56.8 11.5 %collective-permute-start.8 = (f32[256,256]{1,0:T(8,128)S(1)}, f32[256,256]{1,0:T(8,128)S(1)}, u32[]{:S(2)}, u32[]{:S(2)}) collective-permute-start(f32[256,256]{1,0:T(8,128)S(1)} %slice.22), channel_id=1, source_target_pairs={{0,4},{2,6},{8,0},{10,2},{16,8},{18,10},{24,16},{26,18},{28,24},{3... | collective-permute-start | bytes 786440 | tf_op jit(solution)/shard_map/ppermute | solution.py:159
  68.3 0.7 copy-start
  69.0 0.7 copy-start.1
  74.2 3.3 %collective-permute-start.9 = (f32[1024,128]{1,0:T(8,128)}, f32[1024,128]{1,0:T(8,128)S(1)}, u32[]{:S(2)}, u32[]{:S(2)}) collective-permute-start(f32[1024,128]{1,0:T(8,128)} %pair_terms.12), channel_id=1, source_target_pairs={{0,2},{2,0},{4,6},{6,4},{8,10},{10,8},{12,14},{14,12},{16,18},{18,... | collective-permute-start | bytes 1572872 | tf_op jit(solution)/shard_map/ppermute | solution.py:162
  78.4 8.8 %collective-permute-start.10 = (f32[512,128]{1,0:T(8,128)S(1)}, f32[512,128]{1,0:T(8,128)S(1)}, u32[]{:S(2)}, u32[]{:S(2)}) collective-permute-start(f32[512,128]{1,0:T(8,128)S(1)} %slice_add_fusion), channel_id=1, source_target_pairs={{0,1},{1,0},{2,3},{3,2},{4,5},{5,4},{6,7},{7,6},{8,9},{9,8},{10,11... | collective-permute-start | bytes 786440 | tf_op jit(solution)/shard_map/ppermute | solution.py:201

commit v2 on v1

v2 whole, which is shorter than its diff:
```python
import functools
import math

import jax
import jax.numpy as jnp
from jax import lax
from jax.experimental import pallas as pl
from jax.experimental.pallas import tpu as pltpu
from jax.sharding import PartitionSpec as P

F32, BF16 = jnp.float32, jnp.bfloat16
NT = (((1,), (1,)), ((), ()))
VMEM_LIMIT = 16 << 20
IN_VMEM = pl.BlockSpec(memory_space=pltpu.VMEM)


def split(x):
    high = x.astype(BF16)
    low = (x - high.astype(F32)).astype(BF16)
    return high, low


def call(kernel, name, out, *args, scratch=(), pairs=0, aliases=None):
    width = 128
    return pl.pallas_call(
        kernel,
        in_specs=[IN_VMEM] * len(args),
        out_specs=jax.tree.map(lambda _: IN_VMEM, out),
        out_shape=out,
        scratch_shapes=scratch,
        input_output_aliases=aliases or {},
        compiler_params=pltpu.CompilerParams(vmem_limit_bytes=VMEM_LIMIT),
        cost_estimate=pl.CostEstimate(flops=2 * pairs * 12 * width, bytes_accessed=4 << 20, transcendentals=pairs),
        name=name,
    )(*args)


def scale_kernel(feat_ref, fac_ref, out_ref):
    width = feat_ref.shape[1]
    feat = feat_ref[...] * math.sqrt(math.log2(math.e) / width)
    norm = jnp.sum(feat * feat, axis=1, keepdims=True)
    out_ref[:, :width] = feat
    out_ref[:, width:] = fac_ref[...] * jnp.exp2(-0.5 * norm)


def split_kernel(rows_ref, feat_ref, fac_ref):
    width = rows_ref.shape[1] // 2
    for out, at in ((feat_ref, 0), (fac_ref, width)):
        high, low = split(rows_ref[:, at : at + width])
        out[:, :width] = high
        out[:, width:] = low


def split_rows(rows):
    shape = jax.ShapeDtypeStruct(rows.shape, BF16)
    return call(split_kernel, "split_rows", (shape, shape), rows)


def pair_kernel(n_units, has_acc, start, *refs):
    feat_ref, fac_ref = refs[:2]
    units = refs[2 : 2 + n_units]
    acc_ref = refs[2 + n_units] if has_acc else None
    out_ref, cross_rhs, coup_rhs, value = refs[2 + n_units + has_acc :]
    width = out_ref.shape[1]
    first = 0
    for unit in units:
        here = pl.ds(first, unit.shape[0])
        high, low = split(unit[:, :width])
        cross_rhs[here, :] = jnp.concatenate([high, high, low, low], axis=1)
        value[here, :] = jnp.concatenate([high, low, high, jnp.ones_like(high)], axis=1)
        fac = unit[:, width:]
        high, low = split(jnp.concatenate([fac[:, width // 2 :], fac[:, : width // 2]], axis=1))
        coup_rhs[here, :] = jnp.concatenate([high, high, low, low], axis=1)
        first += unit.shape[0]
    count = first
    tile = math.gcd(256, count)
    rows = math.gcd(1024, out_ref.shape[0])

    def dot_nt(a, b):
        return lax.dot_general(a, b, NT, preferred_element_type=F32)

    def chunk(i, _):
        at = pl.ds(pl.multiple_of(i * rows, rows), rows)
        own = pl.ds(pl.multiple_of(start + i * rows, math.gcd(start, rows)), rows)
        feat, fac = feat_ref[own, :], fac_ref[own, :]
        high_sum, low_sum, sums = None, None, None
        for j in range(0, count, tile):
            here = slice(j, j + tile)
            cross = dot_nt(feat, cross_rhs[here, : 2 * width]) + dot_nt(feat, cross_rhs[here, 2 * width :])
            coup = dot_nt(fac, coup_rhs[here, : 2 * width]) + dot_nt(fac, coup_rhs[here, 2 * width :])
            weight = jnp.exp2(cross) * coup
            high = weight.astype(BF16)
            back = high.astype(F32)
            low = (weight - back).astype(BF16)
            a = jnp.dot(high, value[here, : 2 * width], preferred_element_type=F32)
            b = jnp.dot(low, value[here, 2 * width :], preferred_element_type=F32)
            high_sum = a if high_sum is None else high_sum + a
            low_sum = b if low_sum is None else low_sum + b
            for k in range(0, tile, width):
                sums = back[:, k : k + width] if sums is None else sums + back[:, k : k + width]
        total = high_sum[:, :width] + high_sum[:, width:] + low_sum[:, :width]
        own_high, own_low = feat[:, :width].astype(F32), feat[:, width:].astype(F32)
        total = total - jnp.sum(sums, axis=1, keepdims=True) * (own_high + own_low) - low_sum[:, width:] * own_high
        out_ref[at, :] = total if acc_ref is None else acc_ref[at, :] + total
        return 0

    lax.fori_loop(0, out_ref.shape[0] // rows, chunk, 0)


def pairs(feat, fac, units, acc=None, start=0, rows=None):
    width = feat.shape[1] // 2
    rows = feat.shape[0] if rows is None else rows
    count = sum(u.shape[0] for u in units)
    has_acc = acc is not None
    return call(
        functools.partial(pair_kernel, len(units), has_acc, start),
        "pair_terms",
        jax.ShapeDtypeStruct((rows, width), F32),
        feat,
        fac,
        *units,
        *([acc] if has_acc else []),
        scratch=[pltpu.VMEM((count, 4 * width), BF16)] * 3,
        pairs=rows * count,
        aliases={2 + len(units): 0} if has_acc else None,
    )


def ring_order(homes):
    if homes % 2:
        return list(range(homes))
    return list(range(0, homes, 2)) + list(range(homes - 1, 0, -2))


def body(features, factors):
    count, width = features.shape
    replicas = lax.axis_size("rep")
    blocks = lax.axis_size("blk")
    cores = 2 if blocks % 2 == 0 else 1
    homes = blocks // cores
    share = count // replicas
    rep = lax.axis_index("rep")
    order = ring_order(homes)
    after = lax.optimization_barrier

    def ring(x, by):
        moves = [
            (order[p] * cores + c, order[(p + by) % homes] * cores + c) for p in range(homes) for c in range(cores)
        ]
        return lax.ppermute(x, "blk", moves)

    def other_core(x):
        return lax.ppermute(x, "blk", [(b, b ^ 1) for b in range(blocks)])

    own = call(scale_kernel, "scale", jax.ShapeDtypeStruct((count, 2 * width), F32), features, factors)
    unit = lax.dynamic_slice_in_dim(own, rep * share, share, 0)
    full = (homes - 1) // 2
    halves = homes % 2 == 0 and homes > 1
    rows = lax.dynamic_slice_in_dim(jnp.concatenate([own, own]), (rep + 1) % replicas * share, count, 0)

    ahead = behind = unit
    if homes > 1:
        ahead, behind = ring(unit, 1), ring(unit, -1)
    if cores == 2:
        rows = jnp.concatenate([other_core(rows), rows])
    feat, fac = split_rows(rows)
    acc = pairs(feat, fac, [unit])
    last = []
    for step in range(1, full + 1):
        ahead, behind, acc = after((ahead, behind, acc))
        now = [ahead, behind]
        if step < full:
            ahead, behind = ring(ahead, 1), ring(behind, -1)
        elif halves:
            last = [ring(ahead[: share // 2], 1), ring(behind[share // 2 :], -1)]
        acc = pairs(feat, fac, now, acc)
    if halves and not last:
        last = [ahead[: share // 2], behind[share // 2 :]]
    if last:
        *last, acc = after((*last, acc))

    def finish(start, size):
        part = acc[start : start + size]
        return pairs(feat, fac, last, part, start, size) if last else part

    at = 0
    carried = None
    if cores == 2:
        carried = other_core(finish(0, count))
        at = count
    arrived = []
    for k in range(1, replicas):
        part = finish(at, share)
        if carried is not None:
            part = part + carried[(k - 1) * share : k * share]
        arrived.append(lax.ppermute(part, "rep", [(r, (r + k) % replicas) for r in range(replicas)]))
        at += share
    mine = finish(at, share)
    if carried is not None:
        mine = mine + carried[count - share :]
    for part in arrived:
        mine = mine + part
    return mine * (1.0 / (width * math.sqrt(math.log2(math.e) / width)))


def solution(mesh):
    placed = (P("blk", None), P("blk", None))
    return jax.shard_map(
        body, mesh=mesh, in_specs=placed, out_specs=P(("blk", "rep"), None), check_vma=False
    )
```

time: 89.3 us -> 71 us (0.80)
  Pallas kernels: 53.5 us -> 30.9 us
  waiting for transfers between devices: 16.5 us -> 25 us
  other arithmetic: 5.61 us -> 1.41 us
    pallas_call x8 -> x9, Pallas kernels: 53.5 us -> 30.9 us  [call(): pl.pallas_call(kernel, in_specs=[IN_VMEM] * len(args), out_specs=jax.tree...]
    ppermute x8, waiting for transfers between devices: 12.5 us -> 18.5 us  [ring(): return lax.ppermute(x, 'blk', moves)]
    ppermute x1, waiting for transfers between devices: 3.96 us -> 5.75 us  [body(): lax.ppermute(part, 'rep', [(r, (r + k) % replicas) for r in range(replica...]
    concatenate x1, other arithmetic: 1.48 us -> 0.14 us  [body(): rows = jnp.concatenate([other_core(rows), rows])]
    concatenate x1, other arithmetic: 1.45 us -> 0.5 us  [body(): jnp.concatenate([own, own])]
    add x1, other arithmetic: 0.98 us -> 0.03 us  [body(): part = part + carried[(k - 1) * share:k * share]]
    mul x1, other arithmetic: 1.69 us -> 0.75 us  [body(): return mine * (1.0 / (width * math.sqrt(math.log2(math.e) / width)))]
    unnamed x18 -> x4, local copies, waits for them, and re-layouts: 2.08 us -> 2.08 us
  transfers between devices with their start and end apart: 11 -> 11, of which waited for: 2 -> 8; matrix products, arithmetic and copies ran while one was open for 2% -> 0% of each run, Pallas kernels for 55% -> 41%
where the time goes in v2:
time: 71 us; the launch traced here: 70.8 us
  Pallas kernels  30.9 us (44%)
  waiting for transfers between devices  25 us (35%)
  starting transfers between devices  11.2 us (16%)
  local copies, waits for them, and re-layouts  2.22 us (3%)
  other arithmetic  1.41 us (2%)
    pallas_call x9, Pallas kernels, call(): pl.pallas_call(kernel, in_specs=[IN_VMEM] * len(args), out_specs=jax.tree...  30.9 us
    ppermute x8, waiting for transfers between devices, ring(): return lax.ppermute(x, 'blk', moves)  18.5 us
    ppermute x8, starting transfers between devices, ring(): return lax.ppermute(x, 'blk', moves)  9.02 us
    ppermute x1, waiting for transfers between devices, body(): lax.ppermute(part, 'rep', [(r, (r + k) % replicas) for r in range(replica...  5.75 us
    unnamed x4, local copies, waits for them, and re-layouts  2.08 us
    ppermute x1, starting transfers between devices, body(): lax.ppermute(part, 'rep', [(r, (r + k) % replicas) for r in range(replica...  1.57 us
  transfers between devices with their start and end apart: 11, of which 8 were waited for; matrix products, arithmetic and copies ran while one was open for 0% of the time, Pallas kernels for 41%

profile of v2, /device:TPU:0, one launch (start us, length us, event | category | flops | bytes accessed | tf_op | source)
XLA Modules:
  0.0 70.8 jit_solution(15076298730016126048)
XLA Ops:
  0.0 0.0 copy-start
  0.0 1.0 %copy-done = f32[1024,128]{1,0:T(8,128)S(1)} copy-done((f32[1024,128]{1,0:T(8,128)S(1)}, f32[1024,128]{1,0:T(8,128)}, u32[]{:S(2)}) %copy-start) | copy-done | bytes 524312
  1.0 0.0 copy-start.1
  1.0 1.0 %copy-done.1 = f32[1024,128]{1,0:T(8,128)S(1)} copy-done((f32[1024,128]{1,0:T(8,128)S(1)}, f32[1024,128]{1,0:T(8,128)}, u32[]{:S(2)}) %copy-start.1) | copy-done | bytes 524312
  2.1 0.2 scale.1
  2.3 0.5 fusion
  2.8 0.5 collective-permute-start
  3.4 2.7 %collective-permute-start.1 = (f32[512,256]{1,0:T(8,128)S(1)}, f32[512,256]{1,0:T(8,128)S(1)}, u32[]{:S(2)}, u32[]{:S(2)}) collective-permute-start(f32[512,256]{1,0:T(8,128)S(1)} %constant_dynamic-slice_fusion.refs_2_), channel_id=1, source_target_pairs={{0,8},{2,10},{8,16},{10,18},{16,24},{18,26},{24,28},{26,30},{28,20... | collective-permute-start | bytes 1572872 | tf_op jit(solution)/shard_map/ppermute | solution.py:150
  6.0 0.0 collective-permute-start.2
  6.0 0.0 collective-permute-done
  6.0 0.1 pad_maximum_fusion.rows_ref
  6.2 0.4 split_rows.1
  6.6 3.9 %pair_terms.7.refs_4_ = f32[2048,128]{1,0:T(8,128)S(1)} custom-call(bf16[2048,256]{1,0:T(8,128)(2,1)S(1)} %get-tuple-element.19.refs_0_, bf16[2048,256]{1,0:T(8,128)(2,1)S(1)} %get-tuple-element.20.refs_1_, f32[512,256]{1,0:T(8,128)S(1)} %constant_dynamic-slice_fusion.refs_2_), custom_call_target="tpu_custom_call" | custom-call | flops 3221225472 | bytes 4194304 | tf_op jit(solution)/shard_map/pair_terms/pallas_call | solution.py:25
  10.5 8.1 %collective-permute-done.1.refs_2_ = f32[512,256]{1,0:T(8,128)S(1)} collective-permute-done((f32[512,256]{1,0:T(8,128)S(1)}, f32[512,256]{1,0:T(8,128)S(1)}, u32[]{:S(2)}, u32[]{:S(2)}) %collective-permute-start.1) | collective-permute-done | bytes 524320 | tf_op jit(solution)/shard_map/ppermute | solution.py:150
  18.5 1.5 %collective-permute-done.2.refs_3_ = f32[512,256]{1,0:T(8,128)S(1)} collective-permute-done((f32[512,256]{1,0:T(8,128)S(1)}, f32[512,256]{1,0:T(8,128)S(1)}, u32[]{:S(2)}, u32[]{:S(2)}) %collective-permute-start.2) | collective-permute-done | bytes 524320 | tf_op jit(solution)/shard_map/ppermute | solution.py:150
  20.1 1.6 %collective-permute-start.3 = (f32[512,256]{1,0:T(8,128)S(1)}, f32[512,256]{1,0:T(8,128)S(1)}, u32[]{:S(2)}, u32[]{:S(2)}) collective-permute-start(f32[512,256]{1,0:T(8,128)S(1)} %collective-permute-done.1.refs_2_), channel_id=1, source_target_pairs={{0,8},{2,10},{8,16},{10,18},{16,24},{18,26},{24,28},{26,30},{28,20... | collective-permute-start | bytes 1572872 | tf_op jit(solution)/shard_map/ppermute | solution.py:150
  21.6 0.4 collective-permute-start.4
  22.1 7.4 %pair_terms.8.refs_4_ = f32[2048,128]{1,0:T(8,128)S(1)} custom-call(bf16[2048,256]{1,0:T(8,128)(2,1)S(1)} %get-tuple-element.19.refs_0_, bf16[2048,256]{1,0:T(8,128)(2,1)S(1)} %get-tuple-element.20.refs_1_, f32[512,256]{1,0:T(8,128)S(1)} %collective-permute-done.1.refs_2_, ...), custom_call_target="tpu_custom_call", output_to_operand_aliasing={{}: (4, {})} | custom-call | flops 6442450944 | bytes 4194304 | tf_op jit(solution)/shard_map/pair_terms/pallas_call | solution.py:25
  29.5 3.7 %collective-permute-done.3.refs_2_ = f32[512,256]{1,0:T(8,128)S(1)} collective-permute-done((f32[512,256]{1,0:T(8,128)S(1)}, f32[512,256]{1,0:T(8,128)S(1)}, u32[]{:S(2)}, u32[]{:S(2)}) %collective-permute-start.3) | collective-permute-done | bytes 524320 | tf_op jit(solution)/shard_map/ppermute | solution.py:150
  33.3 1.3 %collective-permute-done.4.refs_3_ = f32[512,256]{1,0:T(8,128)S(1)} collective-permute-done((f32[512,256]{1,0:T(8,128)S(1)}, f32[512,256]{1,0:T(8,128)S(1)}, u32[]{:S(2)}, u32[]{:S(2)}) %collective-permute-start.4) | collective-permute-done | bytes 524320 | tf_op jit(solution)/shard_map/ppermute | solution.py:150
  34.6 1.6 %collective-permute-start.5 = (f32[512,256]{1,0:T(8,128)S(1)}, f32[512,256]{1,0:T(8,128)S(1)}, u32[]{:S(2)}, u32[]{:S(2)}) collective-permute-start(f32[512,256]{1,0:T(8,128)S(1)} %collective-permute-done.3.refs_2_), channel_id=1, source_target_pairs={{0,8},{2,10},{8,16},{10,18},{16,24},{18,26},{24,28},{26,30},{28,20... | collective-permute-start | bytes 1572872 | tf_op jit(solution)/shard_map/ppermute | solution.py:150
  36.1 0.4 collective-permute-start.6
  36.6 7.4 %pair_terms.9.refs_4_ = f32[2048,128]{1,0:T(8,128)S(1)} custom-call(bf16[2048,256]{1,0:T(8,128)(2,1)S(1)} %get-tuple-element.19.refs_0_, bf16[2048,256]{1,0:T(8,128)(2,1)S(1)} %get-tuple-element.20.refs_1_, f32[512,256]{1,0:T(8,128)S(1)} %collective-permute-done.3.refs_2_, ...), custom_call_target="tpu_custom_call", output_to_operand_aliasing={{}: (4, {})} | custom-call | flops 6442450944 | bytes 4194304 | tf_op jit(solution)/shard_map/pair_terms/pallas_call | solution.py:25
  44.0 2.5 %collective-permute-done.5.refs_2_ = f32[512,256]{1,0:T(8,128)S(1)} collective-permute-done((f32[512,256]{1,0:T(8,128)S(1)}, f32[512,256]{1,0:T(8,128)S(1)}, u32[]{:S(2)}, u32[]{:S(2)}) %collective-permute-start.5) | collective-permute-done | bytes 524320 | tf_op jit(solution)/shard_map/ppermute | solution.py:150
  46.6 1.3 %collective-permute-done.6.refs_3_ = f32[512,256]{1,0:T(8,128)S(1)} collective-permute-done((f32[512,256]{1,0:T(8,128)S(1)}, f32[512,256]{1,0:T(8,128)S(1)}, u32[]{:S(2)}, u32[]{:S(2)}) %collective-permute-start.6) | collective-permute-done | bytes 524320 | tf_op jit(solution)/shard_map/ppermute | solution.py:150
  47.9 1.6 %collective-permute-start.7 = (f32[256,256]{1,0:T(8,128)S(1)}, f32[256,256]{1,0:T(8,128)S(1)}, u32[]{:S(2)}, u32[]{:S(2)}) collective-permute-start(f32[256,256]{1,0:T(8,128)S(1)} %slice.21), channel_id=1, source_target_pairs={{0,8},{2,10},{8,16},{10,18},{16,24},{18,26},{24,28},{26,30},{28,20... | collective-permute-start | bytes 786440 | tf_op jit(solution)/shard_map/ppermute | solution.py:150
  49.5 0.7 %collective-permute-start.8 = (f32[256,256]{1,0:T(8,128)S(1)}, f32[256,256]{1,0:T(8,128)S(1)}, u32[]{:S(2)}, u32[]{:S(2)}) collective-permute-start(f32[256,256]{1,0:T(8,128)S(1)} %slice.22), channel_id=1, source_target_pairs={{0,4},{2,6},{8,0},{10,2},{16,8},{18,10},{24,16},{26,18},{28,24},{3... | collective-permute-start | bytes 786440 | tf_op jit(solution)/shard_map/ppermute | solution.py:150
  50.2 7.4 %pair_terms.10 = f32[2048,128]{1,0:T(8,128)S(1)} custom-call(bf16[2048,256]{1,0:T(8,128)(2,1)S(1)} %get-tuple-element.19.refs_0_, bf16[2048,256]{1,0:T(8,128)(2,1)S(1)} %get-tuple-element.20.refs_1_, f32[512,256]{1,0:T(8,128)S(1)} %collective-permute-done.5.refs_2_, f32[512,256]{1,0:T(8,128)S(1)} %collective-permute-done.6.refs_3_, ...), custom_call_target="tpu_custom_call", output_to_operand_aliasing={{}: (4, {})} | custom-call | flops 6442450944 | bytes 4194304 | tf_op jit(solution)/shard_map/pair_terms/pallas_call | solution.py:25
  57.6 0.0 collective-permute-done.7.refs_2_
  57.7 0.0 collective-permute-done.8.refs_3_
  57.7 2.0 %pair_terms.12 = f32[1024,128]{1,0:T(8,128)S(1)} custom-call(bf16[2048,256]{1,0:T(8,128)(2,1)S(1)} %get-tuple-element.19.refs_0_, bf16[2048,256]{1,0:T(8,128)(2,1)S(1)} %get-tuple-element.20.refs_1_, f32[256,256]{1,0:T(8,128)S(1)} %collective-permute-done.7.refs_2_, f32[256,256]{1,0:T(8,128)S(1)} %collective-permute-done.8.refs_3_, ...), custom_call_target="tpu_custom_call", output_to_operand_aliasing={{}: (4, {})} | custom-call | flops 1610612736 | bytes 4194304 | tf_op jit(solution)/shard_map/pair_terms/pallas_call | solution.py:25
  59.7 0.1 collective-permute-start.9
  59.8 1.1 %pair_terms.13 = f32[512,128]{1,0:T(8,128)S(1)} custom-call(bf16[2048,256]{1,0:T(8,128)(2,1)S(1)} %get-tuple-element.19.refs_0_, bf16[2048,256]{1,0:T(8,128)(2,1)S(1)} %get-tuple-element.20.refs_1_, f32[256,256]{1,0:T(8,128)S(1)} %collective-permute-done.7.refs_2_, f32[256,256]{1,0:T(8,128)S(1)} %collective-permute-done.8.refs_3_, ...), custom_call_target="tpu_custom_call", output_to_operand_aliasing={{}: (4, {})} | custom-call | flops 805306368 | bytes 4194304 | tf_op jit(solution)/shard_map/pair_terms/pallas_call | solution.py:25
  60.9 0.8 %collective-permute-done.9 = f32[1024,128]{1,0:T(8,128)S(1)} collective-permute-done((f32[1024,128]{1,0:T(8,128)S(1)}, f32[1024,128]{1,0:T(8,128)S(1)}, u32[]{:S(2)}, u32[]{:S(2)}) %collective-permute-start.9) | collective-permute-done | bytes 524320 | tf_op jit(solution)/shard_map/ppermute | solution.py:153
  61.7 1.6 %collective-permute-start.10 = (f32[512,128]{1,0:T(8,128)S(1)}, f32[512,128]{1,0:T(8,128)S(1)}, u32[]{:S(2)}, u32[]{:S(2)}) collective-permute-start(f32[512,128]{1,0:T(8,128)S(1)} %slice_add_fusion), channel_id=1, source_target_pairs={{0,1},{1,0},{2,3},{3,2},{4,5},{5,4},{6,7},{7,6},{8,9},{9,8},{10,11... | collective-permute-start | bytes 786440 | tf_op jit(solution)/shard_map/ppermute | solution.py:196
  63.2 1.1 %pair_terms.11 = f32[512,128]{1,0:T(8,128)S(1)} custom-call(bf16[2048,256]{1,0:T(8,128)(2,1)S(1)} %get-tuple-element.19.refs_0_, bf16[2048,256]{1,0:T(8,128)(2,1)S(1)} %get-tuple-element.20.refs_1_, f32[256,256]{1,0:T(8,128)S(1)} %collective-permute-done.7.refs_2_, f32[256,256]{1,0:T(8,128)S(1)} %collective-permute-done.8.refs_3_, ...), custom_call_target="tpu_custom_call", output_to_operand_aliasing={{}: (4, {})} | custom-call | flops 805306368 | bytes 4194304 | tf_op jit(solution)/shard_map/pair_terms/pallas_call | solution.py:25
  64.3 5.7 %collective-permute-done.10 = f32[512,128]{1,0:T(8,128)S(1)} collective-permute-done((f32[512,128]{1,0:T(8,128)S(1)}, f32[512,128]{1,0:T(8,128)S(1)}, u32[]{:S(2)}, u32[]{:S(2)}) %collective-permute-start.10) | collective-permute-done | bytes 262176 | tf_op jit(solution)/shard_map/ppermute | solution.py:196
  70.1 0.7 %fusion.2 = f32[512,128]{1,0:T(8,128)} fusion(f32[512,128]{1,0:T(8,128)S(1)} %collective-permute-done.10, f32[512,128]{1,0:T(8,128)S(1)} %pair_terms.11, f32[1024,128]{1,0:T(8,128)S(1)} %collective-permute-done.9), kind=kLoop, calls=%fused_computation.7 | loop fusion | flops 196608 | bytes 1048576 | tf_op jit(solution)/shard_map/mul | solution.py:203
  (6 shorter events, 0.2 us)
Async XLA Ops:
  0.0 1.0 %copy-start = (f32[1024,128]{1,0:T(8,128)S(1)}, f32[1024,128]{1,0:T(8,128)}, u32[]{:S(2)}) copy-start(f32[1024,128]{1,0:T(8,128)} %feat_ref.1) | copy-start | bytes 1572868
  1.0 1.0 %copy-start.1 = (f32[1024,128]{1,0:T(8,128)S(1)}, f32[1024,128]{1,0:T(8,128)}, u32[]{:S(2)}) copy-start(f32[1024,128]{1,0:T(8,128)} %fac_ref.1) | copy-start | bytes 1572868
  2.8 3.2 %collective-permute-start = (f32[1024,256]{1,0:T(8,128)S(1)}, f32[1024,256]{1,0:T(8,128)S(1)}, u32[]{:S(2)}, u32[]{:S(2)}) collective-permute-start(f32[1024,256]{1,0:T(8,128)S(1)} %fusion), channel_id=1, source_target_pairs={{0,2},{2,0},{4,6},{6,4},{8,10},{10,8},{12,14},{14,12},{16,18},{18,... | collective-permute-start | bytes 3145736 | tf_op jit(solution)/shard_map/ppermute | solution.py:153
  3.4 15.2 %collective-permute-start.1 = (f32[512,256]{1,0:T(8,128)S(1)}, f32[512,256]{1,0:T(8,128)S(1)}, u32[]{:S(2)}, u32[]{:S(2)}) collective-permute-start(f32[512,256]{1,0:T(8,128)S(1)} %constant_dynamic-slice_fusion.refs_2_), channel_id=1, source_target_pairs={{0,8},{2,10},{8,16},{10,18},{16,24},{18,26},{24,28},{26,30},{28,20... | collective-permute-start | bytes 1572872 | tf_op jit(solution)/shard_map/ppermute | solution.py:150
  6.0 14.0 %collective-permute-start.2 = (f32[512,256]{1,0:T(8,128)S(1)}, f32[512,256]{1,0:T(8,128)S(1)}, u32[]{:S(2)}, u32[]{:S(2)}) collective-permute-start(f32[512,256]{1,0:T(8,128)S(1)} %constant_dynamic-slice_fusion.refs_2_), channel_id=1, source_target_pairs={{0,4},{2,6},{8,0},{10,2},{16,8},{18,10},{24,16},{26,18},{28,24},{3... | collective-permute-start | bytes 1572872 | tf_op jit(solution)/shard_map/ppermute | solution.py:150
  20.1 13.2 %collective-permute-start.3 = (f32[512,256]{1,0:T(8,128)S(1)}, f32[512,256]{1,0:T(8,128)S(1)}, u32[]{:S(2)}, u32[]{:S(2)}) collective-permute-start(f32[512,256]{1,0:T(8,128)S(1)} %collective-permute-done.1.refs_2_), channel_id=1, source_target_pairs={{0,8},{2,10},{8,16},{10,18},{16,24},{18,26},{24,28},{26,30},{28,20... | collective-permute-start | bytes 1572872 | tf_op jit(solution)/shard_map/ppermute | solution.py:150
  21.6 12.9 %collective-permute-start.4 = (f32[512,256]{1,0:T(8,128)S(1)}, f32[512,256]{1,0:T(8,128)S(1)}, u32[]{:S(2)}, u32[]{:S(2)}) collective-permute-start(f32[512,256]{1,0:T(8,128)S(1)} %collective-permute-done.2.refs_3_), channel_id=1, source_target_pairs={{0,4},{2,6},{8,0},{10,2},{16,8},{18,10},{24,16},{26,18},{28,24},{3... | collective-permute-start | bytes 1572872 | tf_op jit(solution)/shard_map/ppermute | solution.py:150
  34.6 12.0 %collective-permute-start.5 = (f32[512,256]{1,0:T(8,128)S(1)}, f32[512,256]{1,0:T(8,128)S(1)}, u32[]{:S(2)}, u32[]{:S(2)}) collective-permute-start(f32[512,256]{1,0:T(8,128)S(1)} %collective-permute-done.3.refs_2_), channel_id=1, source_target_pairs={{0,8},{2,10},{8,16},{10,18},{16,24},{18,26},{24,28},{26,30},{28,20... | collective-permute-start | bytes 1572872 | tf_op jit(solution)/shard_map/ppermute | solution.py:150
  36.1 11.7 %collective-permute-start.6 = (f32[512,256]{1,0:T(8,128)S(1)}, f32[512,256]{1,0:T(8,128)S(1)}, u32[]{:S(2)}, u32[]{:S(2)}) collective-permute-start(f32[512,256]{1,0:T(8,128)S(1)} %collective-permute-done.4.refs_3_), channel_id=1, source_target_pairs={{0,4},{2,6},{8,0},{10,2},{16,8},{18,10},{24,16},{26,18},{28,24},{3... | collective-permute-start | bytes 1572872 | tf_op jit(solution)/shard_map/ppermute | solution.py:150
  47.9 9.8 %collective-permute-start.7 = (f32[256,256]{1,0:T(8,128)S(1)}, f32[256,256]{1,0:T(8,128)S(1)}, u32[]{:S(2)}, u32[]{:S(2)}) collective-permute-start(f32[256,256]{1,0:T(8,128)S(1)} %slice.21), channel_id=1, source_target_pairs={{0,8},{2,10},{8,16},{10,18},{16,24},{18,26},{24,28},{26,30},{28,20... | collective-permute-start | bytes 786440 | tf_op jit(solution)/shard_map/ppermute | solution.py:150
  49.5 8.2 %collective-permute-start.8 = (f32[256,256]{1,0:T(8,128)S(1)}, f32[256,256]{1,0:T(8,128)S(1)}, u32[]{:S(2)}, u32[]{:S(2)}) collective-permute-start(f32[256,256]{1,0:T(8,128)S(1)} %slice.22), channel_id=1, source_target_pairs={{0,4},{2,6},{8,0},{10,2},{16,8},{18,10},{24,16},{26,18},{28,24},{3... | collective-permute-start | bytes 786440 | tf_op jit(solution)/shard_map/ppermute | solution.py:150
  59.7 2.0 %collective-permute-start.9 = (f32[1024,128]{1,0:T(8,128)S(1)}, f32[1024,128]{1,0:T(8,128)S(1)}, u32[]{:S(2)}, u32[]{:S(2)}) collective-permute-start(f32[1024,128]{1,0:T(8,128)S(1)} %pair_terms.12), channel_id=1, source_target_pairs={{0,2},{2,0},{4,6},{6,4},{8,10},{10,8},{12,14},{14,12},{16,18},{18,... | collective-permute-start | bytes 1572872 | tf_op jit(solution)/shard_map/ppermute | solution.py:153
  61.7 8.4 %collective-permute-start.10 = (f32[512,128]{1,0:T(8,128)S(1)}, f32[512,128]{1,0:T(8,128)S(1)}, u32[]{:S(2)}, u32[]{:S(2)}) collective-permute-start(f32[512,128]{1,0:T(8,128)S(1)} %slice_add_fusion), channel_id=1, source_target_pairs={{0,1},{1,0},{2,3},{3,2},{4,5},{5,4},{6,7},{7,6},{8,9},{9,8},{10,11... | collective-permute-start | bytes 786440 | tf_op jit(solution)/shard_map/ppermute | solution.py:196

commit v3 on v2

--- a/solution.py
+++ b/solution.py
@@ -35,25 +35,73 @@
     )(*args)
 
 
-def scale_kernel(feat_ref, fac_ref, out_ref):
-    width = feat_ref.shape[1]
-    feat = feat_ref[...] * math.sqrt(math.log2(math.e) / width)
+def scale(feat, fac):
+    width = feat.shape[1]
+    feat = feat * math.sqrt(math.log2(math.e) / width)
     norm = jnp.sum(feat * feat, axis=1, keepdims=True)
-    out_ref[:, :width] = feat
-    out_ref[:, width:] = fac_ref[...] * jnp.exp2(-0.5 * norm)
-
-
-def split_kernel(rows_ref, feat_ref, fac_ref):
-    width = rows_ref.shape[1] // 2
-    for out, at in ((feat_ref, 0), (fac_ref, width)):
-        high, low = split(rows_ref[:, at : at + width])
-        out[:, :width] = high
-        out[:, width:] = low
-
-
-def split_rows(rows):
-    shape = jax.ShapeDtypeStruct(rows.shape, BF16)
-    return call(split_kernel, "split_rows", (shape, shape), rows)
+    return feat, fac * jnp.exp2(-0.5 * norm)
+
+
+def unit_kernel(rep_ref, feat_hbm, fac_hbm, *refs):
+    outs, (feat_ref, fac_ref, sem) = refs[:-3], refs[-3:]
+    share, width = feat_ref.shape
+    here = pl.ds(pl.multiple_of(rep_ref[0] * share, share), share)
+    copies = [
+        pltpu.make_async_copy(src.at[here, :], dst, sem.at[k])
+        for k, (src, dst) in enumerate(((feat_hbm, feat_ref), (fac_hbm, fac_ref)))
+    ]
+    for copy in copies:
+        copy.start()
+    for copy in copies:
+        copy.wait()
+    part = share // len(outs)
+    for k, out in enumerate(outs):
+        feat, fac = scale(feat_ref[k * part : (k + 1) * part, :], fac_ref[k * part : (k + 1) * part, :])
+        out[:, :width] = feat
+        out[:, width:] = fac
+
+
+def own_units(rep, features, factors, share, parts):
+    width = features.shape[1]
+    out = jax.ShapeDtypeStruct((share // parts, 2 * width), F32)
+    return pl.pallas_call(
+        unit_kernel,
+        in_specs=[pl.BlockSpec(memory_space=pltpu.SMEM)] + [pl.BlockSpec(memory_space=pltpu.HBM)] * 2,
+        out_specs=[IN_VMEM] * parts,
+        out_shape=[out] * parts,
+        scratch_shapes=[pltpu.VMEM((share, width), F32)] * 2 + [pltpu.SemaphoreType.DMA((2,))],
+        compiler_params=pltpu.CompilerParams(vmem_limit_bytes=VMEM_LIMIT),
+        name="own_units",
+    )(rep, features, factors)
+
+
+def rows_kernel(replicas, rep_ref, *refs):
+    sources, (feat_out, fac_out) = refs[:-2], refs[-2:]
+    count, width = sources[0].shape
+    share = count // replicas
+    for block in range(len(sources) // 2):
+        feat_ref, fac_ref = sources[2 * block : 2 * block + 2]
+        for k in range(replicas):
+            place = lax.rem(k - rep_ref[0] - 1 + replicas, replicas) * share + block * count
+            at = pl.ds(pl.multiple_of(place, share), share)
+            here = slice(k * share, (k + 1) * share)
+            for out, x in zip((feat_out, fac_out), scale(feat_ref[here, :], fac_ref[here, :]), strict=True):
+                high, low = split(x)
+                out[at, :width] = high
+                out[at, width:] = low
+
+
+def split_rows(rep, replicas, *blocks):
+    count, width = blocks[0].shape
+    out = jax.ShapeDtypeStruct((count * len(blocks) // 2, 2 * width), BF16)
+    return pl.pallas_call(
+        functools.partial(rows_kernel, replicas),
+        in_specs=[pl.BlockSpec(memory_space=pltpu.SMEM)] + [IN_VMEM] * len(blocks),
+        out_specs=[IN_VMEM] * 2,
+        out_shape=[out] * 2,
+        compiler_params=pltpu.CompilerParams(vmem_limit_bytes=VMEM_LIMIT),
+        name="split_rows",
+    )(rep, *blocks)
 
 
 def pair_kernel(n_units, has_acc, start, *refs):
@@ -101,7 +149,7 @@
         total = high_sum[:, :width] + high_sum[:, width:] + low_sum[:, :width]
         own_high, own_low = feat[:, :width].astype(F32), feat[:, width:].astype(F32)
         total = total - jnp.sum(sums, axis=1, keepdims=True) * (own_high + own_low) - low_sum[:, width:] * own_high
-        out_ref[at, :] = total if acc_ref is None else acc_ref[at, :] + total
+        out_ref[at, :] = total if acc_ref is None else acc_ref[own, :] + total
         return 0
 
     lax.fori_loop(0, out_ref.shape[0] // rows, chunk, 0)
@@ -122,7 +170,7 @@
         *([acc] if has_acc else []),
         scratch=[pltpu.VMEM((count, 4 * width), BF16)] * 3,
         pairs=rows * count,
-        aliases={2 + len(units): 0} if has_acc else None,
+        aliases={2 + len(units): 0} if has_acc and rows == feat.shape[0] else None,
     )
 
 
@@ -152,52 +200,52 @@
     def other_core(x):
         return lax.ppermute(x, "blk", [(b, b ^ 1) for b in range(blocks)])
 
-    own = call(scale_kernel, "scale", jax.ShapeDtypeStruct((count, 2 * width), F32), features, factors)
-    unit = lax.dynamic_slice_in_dim(own, rep * share, share, 0)
+    rep_ref = rep.astype(jnp.int32).reshape(1)
+    parts = 2 if share % 32 == 0 else 1
     full = (homes - 1) // 2
     halves = homes % 2 == 0 and homes > 1
-    rows = lax.dynamic_slice_in_dim(jnp.concatenate([own, own]), (rep + 1) % replicas * share, count, 0)
-
-    ahead = behind = unit
+
+    ahead = list(own_units(rep_ref, features, factors, share, parts))
+    behind = list(ahead)
+    own = list(ahead)
     if homes > 1:
-        ahead, behind = ring(unit, 1), ring(unit, -1)
+        for p in range(parts):
+            ahead[p], behind[p] = ring(ahead[p], 1), ring(behind[p], -1)
     if cores == 2:
-        rows = jnp.concatenate([other_core(rows), rows])
-    feat, fac = split_rows(rows)
-    acc = pairs(feat, fac, [unit])
+        feat, fac = split_rows(rep_ref, replicas, other_core(features), other_core(factors), features, factors)
+    else:
+        feat, fac = split_rows(rep_ref, replicas, features, factors)
+    acc = pairs(feat, fac, own)
     last = []
     for step in range(1, full + 1):
-        ahead, behind, acc = after((ahead, behind, acc))
-        now = [ahead, behind]
-        if step < full:
-            ahead, behind = ring(ahead, 1), ring(behind, -1)
-        elif halves:
-            last = [ring(ahead[: share // 2], 1), ring(behind[share // 2 :], -1)]
-        acc = pairs(feat, fac, now, acc)
-    if halves and not last:
-        last = [ahead[: share // 2], behind[share // 2 :]]
+        for p in range(parts):
+            ahead[p], behind[p], acc = after((ahead[p], behind[p], acc))
+            now = [ahead[p], behind[p]]
+            if step < full:
+                ahead[p], behind[p] = ring(ahead[p], 1), ring(behind[p], -1)
+            elif halves and parts == 2:
+                last.append(ring(ahead[p], 1) if p == 0 else ring(behind[p], -1))
+            elif halves:
+                last = [ring(ahead[p][: share // 2], 1), ring(behind[p][share // 2 :], -1)]
+            acc = pairs(feat, fac, now, acc)
+    if halves and not full:
+        last = [ahead[0], behind[1]] if parts == 2 else [ahead[0][: share // 2], behind[0][share // 2 :]]
     if last:
         *last, acc = after((*last, acc))
 
     def finish(start, size):
-        part = acc[start : start + size]
-        return pairs(feat, fac, last, part, start, size) if last else part
-
-    at = 0
-    carried = None
-    if cores == 2:
-        carried = other_core(finish(0, count))
-        at = count
+        return pairs(feat, fac, last, acc, start, size) if last else acc[start : start + size]
+
+    base = count if cores == 2 else 0
     arrived = []
-    for k in range(1, replicas):
-        part = finish(at, share)
-        if carried is not None:
-            part = part + carried[(k - 1) * share : k * share]
-        arrived.append(lax.ppermute(part, "rep", [(r, (r + k) % replicas) for r in range(replicas)]))
-        at += share
-    mine = finish(at, share)
-    if carried is not None:
-        mine = mine + carried[count - share :]
+    for k in range(replicas):
+        at = k * share
+        theirs = other_core(finish(at, share)) if cores == 2 else None
+        mine = finish(base + at, share)
+        if cores == 2:
+            mine = mine + theirs
+        if k < replicas - 1:
+            arrived.append(lax.ppermute(mine, "rep", [(r, (r + k + 1) % replicas) for r in range(replicas)]))
     for part in arrived:
         mine = mine + part
     return mine * (1.0 / (width * math.sqrt(math.log2(math.e) / width)))

time: 71 us -> 63.3 us (0.89)
  waiting for transfers between devices: 25 us -> 8.56 us
  starting transfers between devices: 11.2 us -> 18.9 us
  Pallas kernels: 30.9 us -> 32.6 us
    ppermute x8 -> x14, waiting for transfers between devices: 18.5 us -> 3.16 us  [ring(): return lax.ppermute(x, 'blk', moves)]
    ppermute x8 -> x14, starting transfers between devices: 9.02 us -> 15.7 us  [ring(): return lax.ppermute(x, 'blk', moves)]
    pallas_call x9 -> x11, Pallas kernels: 30.9 us -> 31.9 us  [call(): pl.pallas_call(kernel, in_specs=[IN_VMEM] * len(args), out_specs=jax.tree...]
    ppermute x2 -> x4, waiting for transfers between devices: 0.75 us -> 0.01 us  [other_core(): return lax.ppermute(x, 'blk', [(b, b ^ 1) for b in range(blocks)])]
    pallas_call x0 -> x2, Pallas kernels: none -> 0.72 us  [the longest x1 0.51 us: split_rows(): pl.pallas_call(functools.partial(rows_kernel, replicas), in_specs=[pl.Blo...]
    unnamed x4 -> x8, local copies, waits for them, and re-layouts: 2.08 us -> 2.09 us
  transfers between devices with their start and end apart: 11 -> 19, of which waited for: 8 -> 4; matrix products, arithmetic and copies ran while one was open for 0% -> 0% of each run, Pallas kernels for 41% -> 50%
where the time goes in v3:
time: 63.3 us; the launch traced here: 63.1 us
  Pallas kernels  32.6 us (52%)
  starting transfers between devices  18.9 us (30%)
  waiting for transfers between devices  8.56 us (14%)
  local copies, waits for them, and re-layouts  2.09 us (3%)
  other arithmetic  0.78 us (1%)
    pallas_call x11, Pallas kernels, call(): pl.pallas_call(kernel, in_specs=[IN_VMEM] * len(args), out_specs=jax.tree...  31.9 us
    ppermute x14, starting transfers between devices, ring(): return lax.ppermute(x, 'blk', moves)  15.7 us
    ppermute x1, waiting for transfers between devices, body(): lax.ppermute(mine, 'rep', [(r, (r + k + 1) % replicas) for r in range(rep...  5.38 us
    ppermute x14, waiting for transfers between devices, ring(): return lax.ppermute(x, 'blk', moves)  3.16 us
    unnamed x8, local copies, waits for them, and re-layouts  2.09 us
    ppermute x1, starting transfers between devices, body(): lax.ppermute(mine, 'rep', [(r, (r + k + 1) % replicas) for r in range(rep...  1.98 us
  transfers between devices with their start and end apart: 19, of which 4 were waited for; matrix products, arithmetic and copies ran while one was open for 0% of the time, Pallas kernels for 50%

profile of v3, /device:TPU:0, one launch (start us, length us, event | category | flops | bytes accessed | tf_op | source)
XLA Modules:
  0.0 63.1 jit_solution(15825258982168855461)
XLA Ops:
  0.0 0.5 collective-permute-start
  0.5 0.1 collective-permute-start.1
  0.5 1.0 %copy-done = f32[1024,128]{1,0:T(8,128)S(1)} copy-done((f32[1024,128]{1,0:T(8,128)S(1)}, f32[1024,128]{1,0:T(8,128)}, u32[]{:S(2)}) %copy-start) | copy-done | bytes 524312
  1.6 1.0 %copy-done.2 = f32[1024,128]{1,0:T(8,128)S(1)} copy-done((f32[1024,128]{1,0:T(8,128)S(1)}, f32[1024,128]{1,0:T(8,128)}, u32[]{:S(2)}) %copy-start.2) | copy-done | bytes 524312
  2.6 0.2 own_units.1
  2.8 3.0 %collective-permute-start.3 = (f32[256,256]{1,0:T(8,128)S(1)}, f32[256,256]{1,0:T(8,128)S(1)}, u32[]{:S(2)}, u32[]{:S(2)}) collective-permute-start(f32[256,256]{1,0:T(8,128)S(1)} %get-tuple-element.32.refs_2_), channel_id=1, source_target_pairs={{0,4},{2,6},{8,0},{10,2},{16,8},{18,10},{24,16},{26,18},{28,24},{3... | collective-permute-start | bytes 786440 | tf_op jit(solution)/shard_map/ppermute | solution.py:198
  5.8 0.1 collective-permute-start.2
  6.0 1.9 %collective-permute-start.7 = (f32[256,256]{1,0:T(8,128)S(1)}, f32[256,256]{1,0:T(8,128)S(1)}, u32[]{:S(2)}, u32[]{:S(2)}) collective-permute-start(f32[256,256]{1,0:T(8,128)S(1)} %get-tuple-element.33.refs_3_), channel_id=1, source_target_pairs={{0,4},{2,6},{8,0},{10,2},{16,8},{18,10},{24,16},{26,18},{28,24},{3... | collective-permute-start | bytes 786440 | tf_op jit(solution)/shard_map/ppermute | solution.py:198
  7.9 0.1 collective-permute-start.6
  8.0 0.0 collective-permute-done.1.refs_1_
  8.0 0.5 split_rows.1
  8.5 3.9 %pair_terms.11.refs_4_ = f32[2048,128]{1,0:T(8,128)S(1)} custom-call(bf16[2048,256]{1,0:T(8,128)(2,1)S(1)} %get-tuple-element.30.refs_0_, bf16[2048,256]{1,0:T(8,128)(2,1)S(1)} %get-tuple-element.31.refs_1_, f32[256,256]{1,0:T(8,128)S(1)} %get-tuple-element.32.refs_2_, f32[256,256]{1,0:T(8,128)S(1)} %get-tuple-element.33.refs_3_), custom_call_target="tpu_custom_call" | custom-call | flops 3221225472 | bytes 4194304 | tf_op jit(solution)/shard_map/pair_terms/pallas_call | solution.py:25
  12.4 0.6 collective-permute-done.3.refs_3_
  13.0 2.0 %collective-permute-done.2.refs_2_ = f32[256,256]{1,0:T(8,128)S(1)} collective-permute-done((f32[256,256]{1,0:T(8,128)S(1)}, f32[256,256]{1,0:T(8,128)S(1)}, u32[]{:S(2)}, u32[]{:S(2)}) %collective-permute-start.2) | collective-permute-done | bytes 262176 | tf_op jit(solution)/shard_map/ppermute | solution.py:198
  15.1 0.1 collective-permute-start.4
  15.1 1.9 %collective-permute-start.5 = (f32[256,256]{1,0:T(8,128)S(1)}, f32[256,256]{1,0:T(8,128)S(1)}, u32[]{:S(2)}, u32[]{:S(2)}) collective-permute-start(f32[256,256]{1,0:T(8,128)S(1)} %collective-permute-done.3.refs_3_), channel_id=1, source_target_pairs={{0,4},{2,6},{8,0},{10,2},{16,8},{18,10},{24,16},{26,18},{28,24},{3... | collective-permute-start | bytes 786440 | tf_op jit(solution)/shard_map/ppermute | solution.py:198
  17.1 3.9 %pair_terms.12.refs_4_ = f32[2048,128]{1,0:T(8,128)S(1)} custom-call(bf16[2048,256]{1,0:T(8,128)(2,1)S(1)} %get-tuple-element.30.refs_0_, bf16[2048,256]{1,0:T(8,128)(2,1)S(1)} %get-tuple-element.31.refs_1_, f32[256,256]{1,0:T(8,128)S(1)} %collective-permute-done.2.refs_2_, ...), custom_call_target="tpu_custom_call", output_to_operand_aliasing={{}: (4, {})} | custom-call | flops 3221225472 | bytes 4194304 | tf_op jit(solution)/shard_map/pair_terms/pallas_call | solution.py:25
  21.0 0.0 collective-permute-done.7.refs_3_
  21.0 0.0 collective-permute-done.6.refs_2_
  21.0 0.1 collective-permute-start.10
  21.2 1.9 %collective-permute-start.11 = (f32[256,256]{1,0:T(8,128)S(1)}, f32[256,256]{1,0:T(8,128)S(1)}, u32[]{:S(2)}, u32[]{:S(2)}) collective-permute-start(f32[256,256]{1,0:T(8,128)S(1)} %collective-permute-done.7.refs_3_), channel_id=1, source_target_pairs={{0,4},{2,6},{8,0},{10,2},{16,8},{18,10},{24,16},{26,18},{28,24},{3... | collective-permute-start | bytes 786440 | tf_op jit(solution)/shard_map/ppermute | solution.py:198
  23.1 3.9 %pair_terms.13.refs_4_ = f32[2048,128]{1,0:T(8,128)S(1)} custom-call(bf16[2048,256]{1,0:T(8,128)(2,1)S(1)} %get-tuple-element.30.refs_0_, bf16[2048,256]{1,0:T(8,128)(2,1)S(1)} %get-tuple-element.31.refs_1_, f32[256,256]{1,0:T(8,128)S(1)} %collective-permute-done.6.refs_2_, ...), custom_call_target="tpu_custom_call", output_to_operand_aliasing={{}: (4, {})} | custom-call | flops 3221225472 | bytes 4194304 | tf_op jit(solution)/shard_map/pair_terms/pallas_call | solution.py:25
  27.1 0.0 collective-permute-done.5.refs_3_
  27.1 0.1 collective-permute-start.8
  27.2 1.9 %collective-permute-start.9 = (f32[256,256]{1,0:T(8,128)S(1)}, f32[256,256]{1,0:T(8,128)S(1)}, u32[]{:S(2)}, u32[]{:S(2)}) collective-permute-start(f32[256,256]{1,0:T(8,128)S(1)} %collective-permute-done.5.refs_3_), channel_id=1, source_target_pairs={{0,4},{2,6},{8,0},{10,2},{16,8},{18,10},{24,16},{26,18},{28,24},{3... | collective-permute-start | bytes 786440 | tf_op jit(solution)/shard_map/ppermute | solution.py:198
  29.2 3.9 %pair_terms.14.refs_4_ = f32[2048,128]{1,0:T(8,128)S(1)} custom-call(bf16[2048,256]{1,0:T(8,128)(2,1)S(1)} %get-tuple-element.30.refs_0_, bf16[2048,256]{1,0:T(8,128)(2,1)S(1)} %get-tuple-element.31.refs_1_, f32[256,256]{1,0:T(8,128)S(1)} %collective-permute-done.4.refs_2_, ...), custom_call_target="tpu_custom_call", output_to_operand_aliasing={{}: (4, {})} | custom-call | flops 3221225472 | bytes 4194304 | tf_op jit(solution)/shard_map/pair_terms/pallas_call | solution.py:25
  33.1 0.0 collective-permute-done.11.refs_3_
  33.1 0.1 collective-permute-start.13
  33.3 1.9 %collective-permute-start.14 = (f32[256,256]{1,0:T(8,128)S(1)}, f32[256,256]{1,0:T(8,128)S(1)}, u32[]{:S(2)}, u32[]{:S(2)}) collective-permute-start(f32[256,256]{1,0:T(8,128)S(1)} %collective-permute-done.11.refs_3_), channel_id=1, source_target_pairs={{0,4},{2,6},{8,0},{10,2},{16,8},{18,10},{24,16},{26,18},{28,24},{3... | collective-permute-start | bytes 786440 | tf_op jit(solution)/shard_map/ppermute | solution.py:198
  35.2 3.9 %pair_terms.15.refs_4_ = f32[2048,128]{1,0:T(8,128)S(1)} custom-call(bf16[2048,256]{1,0:T(8,128)(2,1)S(1)} %get-tuple-element.30.refs_0_, bf16[2048,256]{1,0:T(8,128)(2,1)S(1)} %get-tuple-element.31.refs_1_, f32[256,256]{1,0:T(8,128)S(1)} %collective-permute-done.10.refs_2_, ...), custom_call_target="tpu_custom_call", output_to_operand_aliasing={{}: (4, {})} | custom-call | flops 3221225472 | bytes 4194304 | tf_op jit(solution)/shard_map/pair_terms/pallas_call | solution.py:25
  39.2 0.0 collective-permute-done.9.refs_3_
  39.2 0.3 collective-permute-start.12
  39.5 3.9 %pair_terms.16.refs_4_ = f32[2048,128]{1,0:T(8,128)S(1)} custom-call(bf16[2048,256]{1,0:T(8,128)(2,1)S(1)} %get-tuple-element.30.refs_0_, bf16[2048,256]{1,0:T(8,128)(2,1)S(1)} %get-tuple-element.31.refs_1_, f32[256,256]{1,0:T(8,128)S(1)} %collective-permute-done.8.refs_2_, ...), custom_call_target="tpu_custom_call", output_to_operand_aliasing={{}: (4, {})} | custom-call | flops 3221225472 | bytes 4194304 | tf_op jit(solution)/shard_map/pair_terms/pallas_call | solution.py:25
  43.4 0.0 collective-permute-done.13.refs_2_
  43.4 0.0 collective-permute-done.14.refs_3_
  43.4 2.0 %collective-permute-start.15 = (f32[256,256]{1,0:T(8,128)S(1)}, f32[256,256]{1,0:T(8,128)S(1)}, u32[]{:S(2)}, u32[]{:S(2)}) collective-permute-start(f32[256,256]{1,0:T(8,128)S(1)} %collective-permute-done.14.refs_3_), channel_id=1, source_target_pairs={{0,4},{2,6},{8,0},{10,2},{16,8},{18,10},{24,16},{26,18},{28,24},{3... | collective-permute-start | bytes 786440 | tf_op jit(solution)/shard_map/ppermute | solution.py:198
  45.4 3.9 %pair_terms.17.refs_4_ = f32[2048,128]{1,0:T(8,128)S(1)} custom-call(bf16[2048,256]{1,0:T(8,128)(2,1)S(1)} %get-tuple-element.30.refs_0_, bf16[2048,256]{1,0:T(8,128)(2,1)S(1)} %get-tuple-element.31.refs_1_, f32[256,256]{1,0:T(8,128)S(1)} %collective-permute-done.13.refs_2_, ...), custom_call_target="tpu_custom_call", output_to_operand_aliasing={{}: (4, {})} | custom-call | flops 3221225472 | bytes 4194304 | tf_op jit(solution)/shard_map/pair_terms/pallas_call | solution.py:25
  49.4 0.5 collective-permute-done.15.refs_3_
  49.9 1.1 %pair_terms.21 = f32[512,128]{1,0:T(8,128)S(1)} custom-call(bf16[2048,256]{1,0:T(8,128)(2,1)S(1)} %get-tuple-element.30.refs_0_, bf16[2048,256]{1,0:T(8,128)(2,1)S(1)} %get-tuple-element.31.refs_1_, f32[256,256]{1,0:T(8,128)S(1)} %collective-permute-done.12.refs_2_, f32[256,256]{1,0:T(8,128)S(1)} %collective-permute-done.15.refs_3_, ...), custom_call_target="tpu_custom_call" | custom-call | flops 805306368 | bytes 4194304 | tf_op jit(solution)/shard_map/pair_terms/pallas_call | solution.py:25
  51.0 0.1 collective-permute-start.17
  51.1 1.1 %pair_terms.19 = f32[512,128]{1,0:T(8,128)S(1)} custom-call(bf16[2048,256]{1,0:T(8,128)(2,1)S(1)} %get-tuple-element.30.refs_0_, bf16[2048,256]{1,0:T(8,128)(2,1)S(1)} %get-tuple-element.31.refs_1_, f32[256,256]{1,0:T(8,128)S(1)} %collective-permute-done.12.refs_2_, f32[256,256]{1,0:T(8,128)S(1)} %collective-permute-done.15.refs_3_, ...), custom_call_target="tpu_custom_call" | custom-call | flops 805306368 | bytes 4194304 | tf_op jit(solution)/shard_map/pair_terms/pallas_call | solution.py:25
  52.1 0.6 collective-permute-start.16
  52.7 1.1 %pair_terms.20 = f32[512,128]{1,0:T(8,128)S(1)} custom-call(bf16[2048,256]{1,0:T(8,128)(2,1)S(1)} %get-tuple-element.30.refs_0_, bf16[2048,256]{1,0:T(8,128)(2,1)S(1)} %get-tuple-element.31.refs_1_, f32[256,256]{1,0:T(8,128)S(1)} %collective-permute-done.12.refs_2_, f32[256,256]{1,0:T(8,128)S(1)} %collective-permute-done.15.refs_3_, ...), custom_call_target="tpu_custom_call" | custom-call | flops 805306368 | bytes 4194304 | tf_op jit(solution)/shard_map/pair_terms/pallas_call | solution.py:25
  53.9 2.0 %collective-permute-start.18 = (f32[512,128]{1,0:T(8,128)S(1)}, f32[512,128]{1,0:T(8,128)S(1)}, u32[]{:S(2)}, u32[]{:S(2)}) collective-permute-start(f32[512,128]{1,0:T(8,128)S(1)} %add.10), channel_id=1, source_target_pairs={{0,1},{1,0},{2,3},{3,2},{4,5},{5,4},{6,7},{7,6},{8,9},{9,8},{10,11... | collective-permute-start | bytes 786440 | tf_op jit(solution)/shard_map/ppermute | solution.py:248
  55.8 1.1 %pair_terms.18 = f32[512,128]{1,0:T(8,128)S(1)} custom-call(bf16[2048,256]{1,0:T(8,128)(2,1)S(1)} %get-tuple-element.30.refs_0_, bf16[2048,256]{1,0:T(8,128)(2,1)S(1)} %get-tuple-element.31.refs_1_, f32[256,256]{1,0:T(8,128)S(1)} %collective-permute-done.12.refs_2_, f32[256,256]{1,0:T(8,128)S(1)} %collective-permute-done.15.refs_3_, ...), custom_call_target="tpu_custom_call" | custom-call | flops 805306368 | bytes 4194304 | tf_op jit(solution)/shard_map/pair_terms/pallas_call | solution.py:25
  56.9 0.0 collective-permute-done.16
  56.9 5.4 %collective-permute-done.18 = f32[512,128]{1,0:T(8,128)S(1)} collective-permute-done((f32[512,128]{1,0:T(8,128)S(1)}, f32[512,128]{1,0:T(8,128)S(1)}, u32[]{:S(2)}, u32[]{:S(2)}) %collective-permute-start.18) | collective-permute-done | bytes 262176 | tf_op jit(solution)/shard_map/ppermute | solution.py:248
  62.3 0.7 %add_multiply_fusion = f32[512,128]{1,0:T(8,128)} fusion(f32[512,128]{1,0:T(8,128)S(1)} %collective-permute-done.18, f32[512,128]{1,0:T(8,128)S(1)} %pair_terms.18, f32[512,128]{1,0:T(8,128)S(1)} %collective-permute-done.16), kind=kLoop, calls=%fused_computation | loop fusion | flops 196608 | bytes 1048576 | tf_op jit(solution)/shard_map/mul | solution.py:251
  (13 shorter events, 0.1 us)
Async XLA Ops:
  0.0 7.9 %collective-permute-start = (f32[1024,128]{1,0:T(8,128)}, f32[1024,128]{1,0:T(8,128)S(1)}, u32[]{:S(2)}, u32[]{:S(2)}) collective-permute-start(f32[1024,128]{1,0:T(8,128)} %feat_hbm.1), channel_id=1, source_target_pairs={{0,2},{2,0},{4,6},{6,4},{8,10},{10,8},{12,14},{14,12},{16,18},{18,... | collective-permute-start | bytes 1572872 | tf_op jit(solution)/shard_map/ppermute | solution.py:201
  0.5 7.5 %collective-permute-start.1 = (f32[1024,128]{1,0:T(8,128)}, f32[1024,128]{1,0:T(8,128)S(1)}, u32[]{:S(2)}, u32[]{:S(2)}) collective-permute-start(f32[1024,128]{1,0:T(8,128)} %fac_hbm.1), channel_id=1, source_target_pairs={{0,2},{2,0},{4,6},{6,4},{8,10},{10,8},{12,14},{14,12},{16,18},{18,... | collective-permute-start | bytes 1572872 | tf_op jit(solution)/shard_map/ppermute | solution.py:201
  0.5 1.0 %copy-start = (f32[1024,128]{1,0:T(8,128)S(1)}, f32[1024,128]{1,0:T(8,128)}, u32[]{:S(2)}) copy-start(f32[1024,128]{1,0:T(8,128)} %feat_hbm.1) | copy-start | bytes 1572868
  1.6 1.0 %copy-start.2 = (f32[1024,128]{1,0:T(8,128)S(1)}, f32[1024,128]{1,0:T(8,128)}, u32[]{:S(2)}) copy-start(f32[1024,128]{1,0:T(8,128)} %fac_hbm.1) | copy-start | bytes 1572868
  2.6 5.4 %copy-start.1 = (f32[1024,128]{1,0:T(8,128)S(1)}, f32[1024,128]{1,0:T(8,128)}, u32[]{:S(2)}) copy-start(f32[1024,128]{1,0:T(8,128)} %feat_hbm.1) | copy-start | bytes 1572868
  2.6 5.4 %copy-start.3 = (f32[1024,128]{1,0:T(8,128)S(1)}, f32[1024,128]{1,0:T(8,128)}, u32[]{:S(2)}) copy-start(f32[1024,128]{1,0:T(8,128)} %fac_hbm.1) | copy-start | bytes 1572868
  2.8 10.2 %collective-permute-start.3 = (f32[256,256]{1,0:T(8,128)S(1)}, f32[256,256]{1,0:T(8,128)S(1)}, u32[]{:S(2)}, u32[]{:S(2)}) collective-permute-start(f32[256,256]{1,0:T(8,128)S(1)} %get-tuple-element.32.refs_2_), channel_id=1, source_target_pairs={{0,4},{2,6},{8,0},{10,2},{16,8},{18,10},{24,16},{26,18},{28,24},{3... | collective-permute-start | bytes 786440 | tf_op jit(solution)/shard_map/ppermute | solution.py:198
  5.8 9.2 %collective-permute-start.2 = (f32[256,256]{1,0:T(8,128)S(1)}, f32[256,256]{1,0:T(8,128)S(1)}, u32[]{:S(2)}, u32[]{:S(2)}) collective-permute-start(f32[256,256]{1,0:T(8,128)S(1)} %get-tuple-element.32.refs_2_), channel_id=1, source_target_pairs={{0,8},{2,10},{8,16},{10,18},{16,24},{18,26},{24,28},{26,30},{28,20... | collective-permute-start | bytes 786440 | tf_op jit(solution)/shard_map/ppermute | solution.py:198
  6.0 15.1 %collective-permute-start.7 = (f32[256,256]{1,0:T(8,128)S(1)}, f32[256,256]{1,0:T(8,128)S(1)}, u32[]{:S(2)}, u32[]{:S(2)}) collective-permute-start(f32[256,256]{1,0:T(8,128)S(1)} %get-tuple-element.33.refs_3_), channel_id=1, source_target_pairs={{0,4},{2,6},{8,0},{10,2},{16,8},{18,10},{24,16},{26,18},{28,24},{3... | collective-permute-start | bytes 786440 | tf_op jit(solution)/shard_map/ppermute | solution.py:198
  7.9 13.2 %collective-permute-start.6 = (f32[256,256]{1,0:T(8,128)S(1)}, f32[256,256]{1,0:T(8,128)S(1)}, u32[]{:S(2)}, u32[]{:S(2)}) collective-permute-start(f32[256,256]{1,0:T(8,128)S(1)} %get-tuple-element.33.refs_3_), channel_id=1, source_target_pairs={{0,8},{2,10},{8,16},{10,18},{16,24},{18,26},{24,28},{26,30},{28,20... | collective-permute-start | bytes 786440 | tf_op jit(solution)/shard_map/ppermute | solution.py:198
  15.1 12.0 %collective-permute-start.4 = (f32[256,256]{1,0:T(8,128)S(1)}, f32[256,256]{1,0:T(8,128)S(1)}, u32[]{:S(2)}, u32[]{:S(2)}) collective-permute-start(f32[256,256]{1,0:T(8,128)S(1)} %collective-permute-done.2.refs_2_), channel_id=1, source_target_pairs={{0,8},{2,10},{8,16},{10,18},{16,24},{18,26},{24,28},{26,30},{28,20... | collective-permute-start | bytes 786440 | tf_op jit(solution)/shard_map/ppermute | solution.py:198
  15.1 11.9 %collective-permute-start.5 = (f32[256,256]{1,0:T(8,128)S(1)}, f32[256,256]{1,0:T(8,128)S(1)}, u32[]{:S(2)}, u32[]{:S(2)}) collective-permute-start(f32[256,256]{1,0:T(8,128)S(1)} %collective-permute-done.3.refs_3_), channel_id=1, source_target_pairs={{0,4},{2,6},{8,0},{10,2},{16,8},{18,10},{24,16},{26,18},{28,24},{3... | collective-permute-start | bytes 786440 | tf_op jit(solution)/shard_map/ppermute | solution.py:198
  21.0 12.1 %collective-permute-start.10 = (f32[256,256]{1,0:T(8,128)S(1)}, f32[256,256]{1,0:T(8,128)S(1)}, u32[]{:S(2)}, u32[]{:S(2)}) collective-permute-start(f32[256,256]{1,0:T(8,128)S(1)} %collective-permute-done.6.refs_2_), channel_id=1, source_target_pairs={{0,8},{2,10},{8,16},{10,18},{16,24},{18,26},{24,28},{26,30},{28,20... | collective-permute-start | bytes 786440 | tf_op jit(solution)/shard_map/ppermute | solution.py:198
  21.2 11.9 %collective-permute-start.11 = (f32[256,256]{1,0:T(8,128)S(1)}, f32[256,256]{1,0:T(8,128)S(1)}, u32[]{:S(2)}, u32[]{:S(2)}) collective-permute-start(f32[256,256]{1,0:T(8,128)S(1)} %collective-permute-done.7.refs_3_), channel_id=1, source_target_pairs={{0,4},{2,6},{8,0},{10,2},{16,8},{18,10},{24,16},{26,18},{28,24},{3... | collective-permute-start | bytes 786440 | tf_op jit(solution)/shard_map/ppermute | solution.py:198
  27.1 12.1 %collective-permute-start.8 = (f32[256,256]{1,0:T(8,128)S(1)}, f32[256,256]{1,0:T(8,128)S(1)}, u32[]{:S(2)}, u32[]{:S(2)}) collective-permute-start(f32[256,256]{1,0:T(8,128)S(1)} %collective-permute-done.4.refs_2_), channel_id=1, source_target_pairs={{0,8},{2,10},{8,16},{10,18},{16,24},{18,26},{24,28},{26,30},{28,20... | collective-permute-start | bytes 786440 | tf_op jit(solution)/shard_map/ppermute | solution.py:198
  27.2 11.9 %collective-permute-start.9 = (f32[256,256]{1,0:T(8,128)S(1)}, f32[256,256]{1,0:T(8,128)S(1)}, u32[]{:S(2)}, u32[]{:S(2)}) collective-permute-start(f32[256,256]{1,0:T(8,128)S(1)} %collective-permute-done.5.refs_3_), channel_id=1, source_target_pairs={{0,4},{2,6},{8,0},{10,2},{16,8},{18,10},{24,16},{26,18},{28,24},{3... | collective-permute-start | bytes 786440 | tf_op jit(solution)/shard_map/ppermute | solution.py:198
  33.1 10.3 %collective-permute-start.13 = (f32[256,256]{1,0:T(8,128)S(1)}, f32[256,256]{1,0:T(8,128)S(1)}, u32[]{:S(2)}, u32[]{:S(2)}) collective-permute-start(f32[256,256]{1,0:T(8,128)S(1)} %collective-permute-done.10.refs_2_), channel_id=1, source_target_pairs={{0,8},{2,10},{8,16},{10,18},{16,24},{18,26},{24,28},{26,30},{28,20... | collective-permute-start | bytes 786440 | tf_op jit(solution)/shard_map/ppermute | solution.py:198
  33.3 10.2 %collective-permute-start.14 = (f32[256,256]{1,0:T(8,128)S(1)}, f32[256,256]{1,0:T(8,128)S(1)}, u32[]{:S(2)}, u32[]{:S(2)}) collective-permute-start(f32[256,256]{1,0:T(8,128)S(1)} %collective-permute-done.11.refs_3_), channel_id=1, source_target_pairs={{0,4},{2,6},{8,0},{10,2},{16,8},{18,10},{24,16},{26,18},{28,24},{3... | collective-permute-start | bytes 786440 | tf_op jit(solution)/shard_map/ppermute | solution.py:198
  39.2 10.7 %collective-permute-start.12 = (f32[256,256]{1,0:T(8,128)S(1)}, f32[256,256]{1,0:T(8,128)S(1)}, u32[]{:S(2)}, u32[]{:S(2)}) collective-permute-start(f32[256,256]{1,0:T(8,128)S(1)} %collective-permute-done.8.refs_2_), channel_id=1, source_target_pairs={{0,8},{2,10},{8,16},{10,18},{16,24},{18,26},{24,28},{26,30},{28,20... | collective-permute-start | bytes 786440 | tf_op jit(solution)/shard_map/ppermute | solution.py:198
  43.4 6.4 %collective-permute-start.15 = (f32[256,256]{1,0:T(8,128)S(1)}, f32[256,256]{1,0:T(8,128)S(1)}, u32[]{:S(2)}, u32[]{:S(2)}) collective-permute-start(f32[256,256]{1,0:T(8,128)S(1)} %collective-permute-done.14.refs_3_), channel_id=1, source_target_pairs={{0,4},{2,6},{8,0},{10,2},{16,8},{18,10},{24,16},{26,18},{28,24},{3... | collective-permute-start | bytes 786440 | tf_op jit(solution)/shard_map/ppermute | solution.py:198
  51.0 2.8 %collective-permute-start.17 = (f32[512,128]{1,0:T(8,128)S(1)}, f32[512,128]{1,0:T(8,128)S(1)}, u32[]{:S(2)}, u32[]{:S(2)}) collective-permute-start(f32[512,128]{1,0:T(8,128)S(1)} %pair_terms.21), channel_id=1, source_target_pairs={{0,2},{2,0},{4,6},{6,4},{8,10},{10,8},{12,14},{14,12},{16,18},{18,... | collective-permute-start | bytes 786440 | tf_op jit(solution)/shard_map/ppermute | solution.py:201
  52.1 4.8 %collective-permute-start.16 = (f32[512,128]{1,0:T(8,128)S(1)}, f32[512,128]{1,0:T(8,128)S(1)}, u32[]{:S(2)}, u32[]{:S(2)}) collective-permute-start(f32[512,128]{1,0:T(8,128)S(1)} %pair_terms.19), channel_id=1, source_target_pairs={{0,2},{2,0},{4,6},{6,4},{8,10},{10,8},{12,14},{14,12},{16,18},{18,... | collective-permute-start | bytes 786440 | tf_op jit(solution)/shard_map/ppermute | solution.py:201
  53.9 8.5 %collective-permute-start.18 = (f32[512,128]{1,0:T(8,128)S(1)}, f32[512,128]{1,0:T(8,128)S(1)}, u32[]{:S(2)}, u32[]{:S(2)}) collective-permute-start(f32[512,128]{1,0:T(8,128)S(1)} %add.10), channel_id=1, source_target_pairs={{0,1},{1,0},{2,3},{3,2},{4,5},{5,4},{6,7},{7,6},{8,9},{9,8},{10,11... | collective-permute-start | bytes 786440 | tf_op jit(solution)/shard_map/ppermute | solution.py:248

commit v4 on v2

v4 whole, which is shorter than its diff:
```python
import functools
import math

import jax
import jax.numpy as jnp
from jax import lax
from jax.experimental import pallas as pl
from jax.experimental.pallas import tpu as pltpu
from jax.sharding import PartitionSpec as P

F32, BF16 = jnp.float32, jnp.bfloat16
NT = (((1,), (1,)), ((), ()))
VMEM_LIMIT = 16 << 20
IN_VMEM = pl.BlockSpec(memory_space=pltpu.VMEM)


def split(x):
    high = x.astype(BF16)
    low = (x - high.astype(F32)).astype(BF16)
    return high, low


def call(kernel, name, out, *args, scratch=(), pairs=0, aliases=None):
    width = 128
    return pl.pallas_call(
        kernel,
        in_specs=[IN_VMEM] * len(args),
        out_specs=jax.tree.map(lambda _: IN_VMEM, out),
        out_shape=out,
        scratch_shapes=scratch,
        input_output_aliases=aliases or {},
        compiler_params=pltpu.CompilerParams(vmem_limit_bytes=VMEM_LIMIT),
        cost_estimate=pl.CostEstimate(flops=2 * pairs * 12 * width, bytes_accessed=4 << 20, transcendentals=pairs),
        name=name,
    )(*args)


def scale(feat, fac):
    width = feat.shape[1]
    feat = feat * math.sqrt(math.log2(math.e) / width)
    norm = jnp.sum(feat * feat, axis=1, keepdims=True)
    return feat, fac * jnp.exp2(-0.5 * norm)


def rows_kernel(replicas, blocks, block, rep_ref, feat_ref, fac_ref, *refs):
    feat_out, fac_out = refs[-2:]
    count, width = feat_ref.shape
    share = count // replicas
    for k in range(replicas):
        place = lax.rem(k - rep_ref[0] - 1 + replicas, replicas) * (blocks * share) + block * share
        at = pl.ds(pl.multiple_of(place, share), share)
        here = slice(k * share, (k + 1) * share)
        for out, x in zip((feat_out, fac_out), scale(feat_ref[here, :], fac_ref[here, :]), strict=True):
            high, low = split(x)
            out[at, :width] = high
            out[at, width:] = low


def split_rows(rep, replicas, blocks, block, feat, fac, filled=()):
    count, width = feat.shape
    out = jax.ShapeDtypeStruct((count * blocks, 2 * width), BF16)
    return pl.pallas_call(
        functools.partial(rows_kernel, replicas, blocks, block),
        in_specs=[pl.BlockSpec(memory_space=pltpu.SMEM)] + [IN_VMEM] * (2 + len(filled)),
        out_specs=[IN_VMEM] * 2,
        out_shape=[out] * 2,
        input_output_aliases={3: 0, 4: 1} if filled else {},
        compiler_params=pltpu.CompilerParams(vmem_limit_bytes=VMEM_LIMIT),
        name="split_rows",
    )(rep, feat, fac, *filled)


def pair_kernel(n_units, has_acc, start, acc_start, size, *refs):
    feat_ref, fac_ref = refs[:2]
    units = refs[2 : 2 + n_units]
    acc_ref = refs[2 + n_units] if has_acc else None
    out_ref, cross_rhs, coup_rhs, value = refs[2 + n_units + has_acc :]
    width = out_ref.shape[1]
    first = 0
    for unit in units:
        here = pl.ds(first, unit.shape[0])
        high, low = split(unit[:, :width])
        cross_rhs[here, :] = jnp.concatenate([high, high, low, low], axis=1)
        value[here, :] = jnp.concatenate([high, low, high, jnp.ones_like(high)], axis=1)
        fac = unit[:, width:]
        high, low = split(jnp.concatenate([fac[:, width // 2 :], fac[:, : width // 2]], axis=1))
        coup_rhs[here, :] = jnp.concatenate([high, high, low, low], axis=1)
        first += unit.shape[0]
    count = first
    tile = math.gcd(256, count)
    rows = math.gcd(1024, size)

    def dot_nt(a, b):
        return lax.dot_general(a, b, NT, preferred_element_type=F32)

    def chunk(i, _):
        at = pl.ds(pl.multiple_of(i * rows, rows), rows)
        own = pl.ds(pl.multiple_of(start + i * rows, math.gcd(start, rows)), rows)
        before = pl.ds(pl.multiple_of(acc_start + i * rows, math.gcd(acc_start, rows)), rows)
        feat, fac = feat_ref[own, :], fac_ref[own, :]
        high_sum, low_sum, sums = None, None, None
        for j in range(0, count, tile):
            here = slice(j, j + tile)
            cross = dot_nt(feat, cross_rhs[here, : 2 * width]) + dot_nt(feat, cross_rhs[here, 2 * width :])
            coup = dot_nt(fac, coup_rhs[here, : 2 * width]) + dot_nt(fac, coup_rhs[here, 2 * width :])
            weight = jnp.exp2(cross) * coup
            high = weight.astype(BF16)
            back = high.astype(F32)
            low = (weight - back).astype(BF16)
            a = jnp.dot(high, value[here, : 2 * width], preferred_element_type=F32)
            b = jnp.dot(low, value[here, 2 * width :], preferred_element_type=F32)
            high_sum = a if high_sum is None else high_sum + a
            low_sum = b if low_sum is None else low_sum + b
            for k in range(0, tile, width):
                sums = back[:, k : k + width] if sums is None else sums + back[:, k : k + width]
        total = high_sum[:, :width] + high_sum[:, width:] + low_sum[:, :width]
        own_high, own_low = feat[:, :width].astype(F32), feat[:, width:].astype(F32)
        total = total - jnp.sum(sums, axis=1, keepdims=True) * (own_high + own_low) - low_sum[:, width:] * own_high
        out_ref[at, :] = total if acc_ref is None else acc_ref[before, :] + total
        return 0

    lax.fori_loop(0, size // rows, chunk, 0)
    if size < out_ref.shape[0]:
        out_ref[size:, :] = jnp.zeros_like(out_ref[size:, :])


def pairs(feat, fac, units, acc=None, start=0, rows=None, acc_start=0, size=None):
    width = feat.shape[1] // 2
    rows = feat.shape[0] if rows is None else rows
    size = rows if size is None else size
    count = sum(u.shape[0] for u in units)
    has_acc = acc is not None
    return call(
        functools.partial(pair_kernel, len(units), has_acc, start, start - acc_start, size),
        "pair_terms",
        jax.ShapeDtypeStruct((rows, width), F32),
        feat,
        fac,
        *units,
        *([acc] if has_acc else []),
        scratch=[pltpu.VMEM((count, 4 * width), BF16)] * 3,
        pairs=size * count,
        aliases={2 + len(units): 0} if has_acc and rows == acc.shape[0] else None,
    )


def ring_order(homes):
    if homes % 2:
        return list(range(homes))
    return list(range(0, homes, 2)) + list(range(homes - 1, 0, -2))


def body(features, factors):
    replicas = lax.axis_size("rep")
    blocks = lax.axis_size("blk")
    count, width = features.shape
    share = count // replicas
    rep = lax.axis_index("rep")
    rep_ref = rep.astype(jnp.int32).reshape(1)
    homes = blocks // 2
    order = ring_order(homes)
    after = lax.optimization_barrier

    def ring(x):
        moves = []
        for p in range(homes):
            moves += [(order[p] * 2 + c, order[(p + 1 - 2 * c) % homes] * 2 + c) for c in range(2)]
        return lax.ppermute(x, "blk", moves)

    def other_core(x):
        return lax.ppermute(x, "blk", [(b, b ^ 1) for b in range(blocks)])

    def units_of(*blocks):
        return jnp.concatenate(scale(*(lax.dynamic_slice_in_dim(x, rep * share, share) for x in blocks)), axis=1)

    own = units_of(features, factors)
    first = ring(own)
    own, features, factors = after((own, features, factors))
    filled = split_rows(rep_ref, replicas, 2, 1, features, factors)
    *filled, features, factors = after((*filled, features, factors))
    features, factors = other_core(features), other_core(factors)
    second = ring(units_of(features, factors))
    feat, fac = split_rows(rep_ref, replicas, 2, 0, features, factors, filled)
    mine_at = 2 * share * (replicas - 1)
    acc = pairs(feat, fac, [own], size=mine_at) if mine_at else jnp.zeros((2 * count, width), F32)

    full = (homes - 1) // 2
    total = 2 * full + (homes + 1) % 2
    flying = [first, second]
    for step in range(total - 1):
        here, acc = after((flying[step % 2], acc))
        if step + 2 < total:
            flying[step % 2] = ring(here)
        acc = pairs(feat, fac, [here], acc)
    last, acc = after((flying[(total - 1) % 2], acc))

    arrived = []
    for k in range(replicas - 1):
        at = k * 2 * share
        received = other_core(pairs(feat, fac, [last], acc, at, share))
        part = pairs(feat, fac, [last], acc, at + share, share) + received
        arrived.append(lax.ppermute(part, "rep", [(r, (r + k + 1) % replicas) for r in range(replicas)]))
        acc, part = after((acc, part))
    part = pairs(feat, fac, [own, last], acc, mine_at, 2 * share)
    part = part[share:] + other_core(part[:share])
    for x in arrived:
        part = part + x
    return part * (1.0 / (width * math.sqrt(math.log2(math.e) / width)))


def solution(mesh):
    placed = (P("blk", None), P("blk", None))
    return jax.shard_map(
        body, mesh=mesh, in_specs=placed, out_specs=P(("blk", "rep"), None), check_vma=False
    )
```

time: 71 us -> 59.3 us (0.84)
  waiting for transfers between devices: 25 us -> 7.17 us
  starting transfers between devices: 11.2 us -> 16.8 us
  local copies, waits for them, and re-layouts: 2.22 us -> 1.02 us
  other arithmetic: 1.41 us -> 2.42 us
    ppermute x8 -> x7, waiting for transfers between devices: 18.5 us -> 3.78 us  [ring(): return lax.ppermute(x, 'blk', moves)]
    ppermute x8 -> x7, starting transfers between devices: 9.02 us -> 14 us  [ring(): return lax.ppermute(x, 'blk', moves)]
    ppermute x1, waiting for transfers between devices: 5.75 us -> 2.95 us  [body(): lax.ppermute(part, 'rep', [(r, (r + k + 1) % replicas) for r in range(rep...]
    reduce_sum x0 -> x2, other arithmetic: none -> 1.3 us  [scale(): norm = jnp.sum(feat * feat, axis=1, keepdims=True)]
    unnamed x4, local copies, waits for them, and re-layouts: 2.08 us -> 1 us
    pallas_call x9 -> x10, Pallas kernels: 30.9 us -> 31 us  [call(): pl.pallas_call(kernel, in_specs=[IN_VMEM] * len(args), out_specs=jax.tree...]
  transfers between devices with their start and end apart: 11 -> 12, of which waited for: 8 -> 4; matrix products, arithmetic and copies ran while one was open for 0% -> 1% of each run, Pallas kernels for 41% -> 51%
where the time goes in v4:
time: 59.3 us; the launch traced here: 59.2 us
  Pallas kernels  31.5 us (53%)
  starting transfers between devices  16.8 us (28%)
  waiting for transfers between devices  7.17 us (12%)
  other arithmetic  2.42 us (4%)
  local copies, waits for them, and re-layouts  1.02 us (2%)
    pallas_call x10, Pallas kernels, call(): pl.pallas_call(kernel, in_specs=[IN_VMEM] * len(args), out_specs=jax.tree...  31 us
    ppermute x7, starting transfers between devices, ring(): return lax.ppermute(x, 'blk', moves)  14 us
    ppermute x7, waiting for transfers between devices, ring(): return lax.ppermute(x, 'blk', moves)  3.78 us
    ppermute x1, waiting for transfers between devices, body(): lax.ppermute(part, 'rep', [(r, (r + k + 1) % replicas) for r in range(rep...  2.95 us
    ppermute x1, starting transfers between devices, body(): lax.ppermute(part, 'rep', [(r, (r + k + 1) % replicas) for r in range(rep...  2.06 us
    reduce_sum x2, other arithmetic, scale(): norm = jnp.sum(feat * feat, axis=1, keepdims=True)  1.3 us
  transfers between devices with their start and end apart: 12, of which 4 were waited for; matrix products, arithmetic and copies ran while one was open for 1% of the time, Pallas kernels for 51%

profile of v4, /device:TPU:0, one launch (start us, length us, event | category | flops | bytes accessed | tf_op | source)
XLA Modules:
  0.0 59.2 jit_solution(9491429156629104941)
XLA Ops:
  0.0 0.0 copy-start.1
  0.0 1.2 %multiply_reduce_fusion.1 = (f32[512]{0:T(512)S(1)}, f32[512,128]{1,0:T(8,128)S(1)}) fusion(f32[1024,128]{1,0:T(8,128)} %feat_ref, s32[]{:T(128)S(6)} %select_n.2), kind=kLoop, calls=%fused_computation.8 | loop fusion | flops 196096 | bytes 526340 | tf_op jit(solution)/shard_map/reduce_sum | solution.py:41
  1.2 0.0 copy-done.1
  1.2 0.1 dynamic-slice_multiply_fusion.2
  1.3 0.0 copy-start
  1.4 1.0 %copy-done = f32[1024,128]{1,0:T(8,128)S(1)} copy-done((f32[1024,128]{1,0:T(8,128)S(1)}, f32[1024,128]{1,0:T(8,128)}, u32[]{:S(2)}) %copy-start) | copy-done | bytes 524312
  2.4 0.3 split_rows.2
  2.6 0.5 collective-permute-start
  3.1 0.1 collective-permute-start.1
  3.2 3.0 %collective-permute-start.2 = (f32[512,256]{1,0:T(8,128)S(1)}, f32[512,256]{1,0:T(8,128)S(1)}, u32[]{:S(2)}, u32[]{:S(2)}) collective-permute-start(f32[512,256]{1,0:T(8,128)S(1)} %pad_maximum_fusion.refs_2_), channel_id=1, source_target_pairs={{0,8},{2,6},{8,16},{10,2},{16,24},{18,10},{24,28},{26,18},{28,20},... | collective-permute-start | bytes 1572872 | tf_op jit(solution)/shard_map/ppermute | solution.py:168
  6.2 0.0 collective-permute-done.feat_ref
  6.2 0.1 multiply_reduce_fusion
  6.4 0.0 collective-permute-done.1.fac_ref
  6.4 0.1 dynamic-slice_multiply_fusion
  6.6 2.0 %collective-permute-start.4 = (f32[512,256]{1,0:T(8,128)S(1)}, f32[512,256]{1,0:T(8,128)S(1)}, u32[]{:S(2)}, u32[]{:S(2)}) collective-permute-start(f32[512,256]{1,0:T(8,128)S(1)} %pad_maximum_fusion.1), channel_id=1, source_target_pairs={{0,8},{2,6},{8,16},{10,2},{16,24},{18,10},{24,28},{26,18},{28,20},... | collective-permute-start | bytes 1572872 | tf_op jit(solution)/shard_map/ppermute | solution.py:168
  8.6 0.3 split_rows.3
  8.9 1.9 %pair_terms.10.refs_3_ = f32[2048,128]{1,0:T(8,128)S(1)} custom-call(bf16[2048,256]{1,0:T(8,128)(2,1)S(1)} %get-tuple-element.39.refs_0_, bf16[2048,256]{1,0:T(8,128)(2,1)S(1)} %get-tuple-element.40.refs_1_, f32[512,256]{1,0:T(8,128)S(1)} %pad_maximum_fusion.refs_2_), custom_call_target="tpu_custom_call" | custom-call | flops 1610612736 | bytes 4194304 | tf_op jit(solution)/shard_map/pair_terms/pallas_call | solution.py:25
  10.8 2.6 %collective-permute-done.2.refs_2_ = f32[512,256]{1,0:T(8,128)S(1)} collective-permute-done((f32[512,256]{1,0:T(8,128)S(1)}, f32[512,256]{1,0:T(8,128)S(1)}, u32[]{:S(2)}, u32[]{:S(2)}) %collective-permute-start.2) | collective-permute-done | bytes 524320 | tf_op jit(solution)/shard_map/ppermute | solution.py:168
  13.3 2.1 %collective-permute-start.3 = (f32[512,256]{1,0:T(8,128)S(1)}, f32[512,256]{1,0:T(8,128)S(1)}, u32[]{:S(2)}, u32[]{:S(2)}) collective-permute-start(f32[512,256]{1,0:T(8,128)S(1)} %collective-permute-done.2.refs_2_), channel_id=1, source_target_pairs={{0,8},{2,6},{8,16},{10,2},{16,24},{18,10},{24,28},{26,18},{28,20},... | collective-permute-start | bytes 1572872 | tf_op jit(solution)/shard_map/ppermute | solution.py:168
  15.4 3.9 %pair_terms.11.refs_3_ = f32[2048,128]{1,0:T(8,128)S(1)} custom-call(bf16[2048,256]{1,0:T(8,128)(2,1)S(1)} %get-tuple-element.39.refs_0_, bf16[2048,256]{1,0:T(8,128)(2,1)S(1)} %get-tuple-element.40.refs_1_, f32[512,256]{1,0:T(8,128)S(1)} %collective-permute-done.2.refs_2_, f32[2048,128]{1,0:T(8,128)S(1)} %pair_terms.10.refs_3_), custom_call_target="tpu_custom_call", output_to_operand_aliasing={{}: (3, {})} | custom-call | flops 3221225472 | bytes 4194304 | tf_op jit(solution)/shard_map/pair_terms/pallas_call | solution.py:25
  19.3 0.0 collective-permute-done.4.refs_2_
  19.3 1.7 %collective-permute-start.6 = (f32[512,256]{1,0:T(8,128)S(1)}, f32[512,256]{1,0:T(8,128)S(1)}, u32[]{:S(2)}, u32[]{:S(2)}) collective-permute-start(f32[512,256]{1,0:T(8,128)S(1)} %collective-permute-done.4.refs_2_), channel_id=1, source_target_pairs={{0,8},{2,6},{8,16},{10,2},{16,24},{18,10},{24,28},{26,18},{28,20},... | collective-permute-start | bytes 1572872 | tf_op jit(solution)/shard_map/ppermute | solution.py:168
  21.0 3.9 %pair_terms.12.refs_3_ = f32[2048,128]{1,0:T(8,128)S(1)} custom-call(bf16[2048,256]{1,0:T(8,128)(2,1)S(1)} %get-tuple-element.39.refs_0_, bf16[2048,256]{1,0:T(8,128)(2,1)S(1)} %get-tuple-element.40.refs_1_, f32[512,256]{1,0:T(8,128)S(1)} %collective-permute-done.4.refs_2_, f32[2048,128]{1,0:T(8,128)S(1)} %pair_terms.11.refs_3_), custom_call_target="tpu_custom_call", output_to_operand_aliasing={{}: (3, {})} | custom-call | flops 3221225472 | bytes 4194304 | tf_op jit(solution)/shard_map/pair_terms/pallas_call | solution.py:25
  24.9 0.0 collective-permute-done.3.refs_2_
  24.9 1.7 %collective-permute-start.5 = (f32[512,256]{1,0:T(8,128)S(1)}, f32[512,256]{1,0:T(8,128)S(1)}, u32[]{:S(2)}, u32[]{:S(2)}) collective-permute-start(f32[512,256]{1,0:T(8,128)S(1)} %collective-permute-done.3.refs_2_), channel_id=1, source_target_pairs={{0,8},{2,6},{8,16},{10,2},{16,24},{18,10},{24,28},{26,18},{28,20},... | collective-permute-start | bytes 1572872 | tf_op jit(solution)/shard_map/ppermute | solution.py:168
  26.6 3.9 %pair_terms.13.refs_3_ = f32[2048,128]{1,0:T(8,128)S(1)} custom-call(bf16[2048,256]{1,0:T(8,128)(2,1)S(1)} %get-tuple-element.39.refs_0_, bf16[2048,256]{1,0:T(8,128)(2,1)S(1)} %get-tuple-element.40.refs_1_, f32[512,256]{1,0:T(8,128)S(1)} %collective-permute-done.3.refs_2_, f32[2048,128]{1,0:T(8,128)S(1)} %pair_terms.12.refs_3_), custom_call_target="tpu_custom_call", output_to_operand_aliasing={{}: (3, {})} | custom-call | flops 3221225472 | bytes 4194304 | tf_op jit(solution)/shard_map/pair_terms/pallas_call | solution.py:25
  30.6 0.0 collective-permute-done.6.refs_2_
  30.6 1.7 %collective-permute-start.8 = (f32[512,256]{1,0:T(8,128)S(1)}, f32[512,256]{1,0:T(8,128)S(1)}, u32[]{:S(2)}, u32[]{:S(2)}) collective-permute-start(f32[512,256]{1,0:T(8,128)S(1)} %collective-permute-done.6.refs_2_), channel_id=1, source_target_pairs={{0,8},{2,6},{8,16},{10,2},{16,24},{18,10},{24,28},{26,18},{28,20},... | collective-permute-start | bytes 1572872 | tf_op jit(solution)/shard_map/ppermute | solution.py:168
  32.3 3.9 %pair_terms.14.refs_3_ = f32[2048,128]{1,0:T(8,128)S(1)} custom-call(bf16[2048,256]{1,0:T(8,128)(2,1)S(1)} %get-tuple-element.39.refs_0_, bf16[2048,256]{1,0:T(8,128)(2,1)S(1)} %get-tuple-element.40.refs_1_, f32[512,256]{1,0:T(8,128)S(1)} %collective-permute-done.6.refs_2_, f32[2048,128]{1,0:T(8,128)S(1)} %pair_terms.13.refs_3_), custom_call_target="tpu_custom_call", output_to_operand_aliasing={{}: (3, {})} | custom-call | flops 3221225472 | bytes 4194304 | tf_op jit(solution)/shard_map/pair_terms/pallas_call | solution.py:25
  36.2 0.0 collective-permute-done.5.refs_2_
  36.2 1.8 %collective-permute-start.7 = (f32[512,256]{1,0:T(8,128)S(1)}, f32[512,256]{1,0:T(8,128)S(1)}, u32[]{:S(2)}, u32[]{:S(2)}) collective-permute-start(f32[512,256]{1,0:T(8,128)S(1)} %collective-permute-done.5.refs_2_), channel_id=1, source_target_pairs={{0,8},{2,6},{8,16},{10,2},{16,24},{18,10},{24,28},{26,18},{28,20},... | collective-permute-start | bytes 1572872 | tf_op jit(solution)/shard_map/ppermute | solution.py:168
  38.0 3.9 %pair_terms.15.refs_3_ = f32[2048,128]{1,0:T(8,128)S(1)} custom-call(bf16[2048,256]{1,0:T(8,128)(2,1)S(1)} %get-tuple-element.39.refs_0_, bf16[2048,256]{1,0:T(8,128)(2,1)S(1)} %get-tuple-element.40.refs_1_, f32[512,256]{1,0:T(8,128)S(1)} %collective-permute-done.5.refs_2_, f32[2048,128]{1,0:T(8,128)S(1)} %pair_terms.14.refs_3_), custom_call_target="tpu_custom_call", output_to_operand_aliasing={{}: (3, {})} | custom-call | flops 3221225472 | bytes 4194304 | tf_op jit(solution)/shard_map/pair_terms/pallas_call | solution.py:25
  41.9 0.0 collective-permute-done.8.refs_2_
  41.9 3.9 %pair_terms.16.refs_3_.refs_4_ = f32[2048,128]{1,0:T(8,128)S(1)} custom-call(bf16[2048,256]{1,0:T(8,128)(2,1)S(1)} %get-tuple-element.39.refs_0_, bf16[2048,256]{1,0:T(8,128)(2,1)S(1)} %get-tuple-element.40.refs_1_, f32[512,256]{1,0:T(8,128)S(1)} %collective-permute-done.8.refs_2_, f32[2048,128]{1,0:T(8,128)S(1)} %pair_terms.15.refs_3_), custom_call_target="tpu_custom_call", output_to_operand_aliasing={{}: (3, {})} | custom-call | flops 3221225472 | bytes 4194304 | tf_op jit(solution)/shard_map/pair_terms/pallas_call | solution.py:25
  45.8 1.2 %collective-permute-done.7.refs_2_.refs_3_ = f32[512,256]{1,0:T(8,128)S(1)} collective-permute-done((f32[512,256]{1,0:T(8,128)S(1)}, f32[512,256]{1,0:T(8,128)S(1)}, u32[]{:S(2)}, u32[]{:S(2)}) %collective-permute-start.7) | collective-permute-done | bytes 524320 | tf_op jit(solution)/shard_map/ppermute | solution.py:168
  47.0 1.1 %pair_terms.18 = f32[512,128]{1,0:T(8,128)S(1)} custom-call(bf16[2048,256]{1,0:T(8,128)(2,1)S(1)} %get-tuple-element.39.refs_0_, bf16[2048,256]{1,0:T(8,128)(2,1)S(1)} %get-tuple-element.40.refs_1_, f32[512,256]{1,0:T(8,128)S(1)} %collective-permute-done.7.refs_2_.refs_3_, f32[2048,128]{1,0:T(8,128)S(1)} %pair_terms.16.refs_3_.refs_4_), custom_call_target="tpu_custom_call" | custom-call | flops 805306368 | bytes 4194304 | tf_op jit(solution)/shard_map/pair_terms/pallas_call | solution.py:25
  48.1 0.1 collective-permute-start.9
  48.2 1.1 %pair_terms.17 = f32[512,128]{1,0:T(8,128)S(1)} custom-call(bf16[2048,256]{1,0:T(8,128)(2,1)S(1)} %get-tuple-element.39.refs_0_, bf16[2048,256]{1,0:T(8,128)(2,1)S(1)} %get-tuple-element.40.refs_1_, f32[512,256]{1,0:T(8,128)S(1)} %collective-permute-done.7.refs_2_.refs_3_, f32[2048,128]{1,0:T(8,128)S(1)} %pair_terms.16.refs_3_.refs_4_), custom_call_target="tpu_custom_call" | custom-call | flops 805306368 | bytes 4194304 | tf_op jit(solution)/shard_map/pair_terms/pallas_call | solution.py:25
  49.3 0.4 collective-permute-done.9
  49.8 2.1 %collective-permute-start.11 = (f32[512,128]{1,0:T(8,128)S(1)}, f32[512,128]{1,0:T(8,128)S(1)}, u32[]{:S(2)}, u32[]{:S(2)}) collective-permute-start(f32[512,128]{1,0:T(8,128)S(1)} %add.16), channel_id=1, source_target_pairs={{0,1},{1,0},{2,3},{3,2},{4,5},{5,4},{6,7},{7,6},{8,9},{9,8},{10,11... | collective-permute-start | bytes 786440 | tf_op jit(solution)/shard_map/ppermute | solution.py:202
  51.8 3.5 %pair_terms.19 = f32[1024,128]{1,0:T(8,128)S(1)} custom-call(bf16[2048,256]{1,0:T(8,128)(2,1)S(1)} %get-tuple-element.39.refs_0_, bf16[2048,256]{1,0:T(8,128)(2,1)S(1)} %get-tuple-element.40.refs_1_, f32[512,256]{1,0:T(8,128)S(1)} %pad_maximum_fusion.refs_2_, f32[512,256]{1,0:T(8,128)S(1)} %collective-permute-done.7.refs_2_.refs_3_, ...), custom_call_target="tpu_custom_call" | custom-call | flops 3221225472 | bytes 4194304 | tf_op jit(solution)/shard_map/pair_terms/pallas_call | solution.py:25
  55.4 0.1 collective-permute-start.10
  55.5 3.0 %collective-permute-done.11 = f32[512,128]{1,0:T(8,128)S(1)} collective-permute-done((f32[512,128]{1,0:T(8,128)S(1)}, f32[512,128]{1,0:T(8,128)S(1)}, u32[]{:S(2)}, u32[]{:S(2)}) %collective-permute-start.11) | collective-permute-done | bytes 262176 | tf_op jit(solution)/shard_map/ppermute | solution.py:202
  58.4 0.0 collective-permute-done.10
  58.4 0.7 %fusion.1 = f32[512,128]{1,0:T(8,128)} fusion(f32[512,128]{1,0:T(8,128)S(1)} %collective-permute-done.11, f32[512,128]{1,0:T(8,128)S(1)} %collective-permute-done.10, f32[1024,128]{1,0:T(8,128)S(1)} %pair_terms.19), kind=kLoop, calls=%fused_computation.4 | loop fusion | flops 196608 | bytes 1048576 | tf_op jit(solution)/shard_map/mul | solution.py:208
  (6 shorter events, 0.1 us)
Async XLA Ops:
  0.0 1.2 %copy-start.1 = (f32[1024,128]{1,0:T(8,128)S(1)}, f32[1024,128]{1,0:T(8,128)}, u32[]{:S(2)}) copy-start(f32[1024,128]{1,0:T(8,128)} %fac_ref) | copy-start | bytes 1572868
  1.3 1.0 %copy-start = (f32[1024,128]{1,0:T(8,128)S(1)}, f32[1024,128]{1,0:T(8,128)}, u32[]{:S(2)}) copy-start(f32[1024,128]{1,0:T(8,128)} %feat_ref) | copy-start | bytes 1572868
  2.6 3.6 %collective-permute-start = (f32[1024,128]{1,0:T(8,128)S(1)}, f32[1024,128]{1,0:T(8,128)S(1)}, u32[]{:S(2)}, u32[]{:S(2)}) collective-permute-start(f32[1024,128]{1,0:T(8,128)S(1)} %copy-done), channel_id=1, source_target_pairs={{0,2},{2,0},{4,6},{6,4},{8,10},{10,8},{12,14},{14,12},{16,18},{18,... | collective-permute-start | bytes 1572872 | tf_op jit(solution)/shard_map/ppermute | solution.py:171
  3.1 3.2 %collective-permute-start.1 = (f32[1024,128]{1,0:T(8,128)S(1)}, f32[1024,128]{1,0:T(8,128)S(1)}, u32[]{:S(2)}, u32[]{:S(2)}) collective-permute-start(f32[1024,128]{1,0:T(8,128)S(1)} %copy-done.1), channel_id=1, source_target_pairs={{0,2},{2,0},{4,6},{6,4},{8,10},{10,8},{12,14},{14,12},{16,18},{18,... | collective-permute-start | bytes 1572872 | tf_op jit(solution)/shard_map/ppermute | solution.py:171
  3.2 10.1 %collective-permute-start.2 = (f32[512,256]{1,0:T(8,128)S(1)}, f32[512,256]{1,0:T(8,128)S(1)}, u32[]{:S(2)}, u32[]{:S(2)}) collective-permute-start(f32[512,256]{1,0:T(8,128)S(1)} %pad_maximum_fusion.refs_2_), channel_id=1, source_target_pairs={{0,8},{2,6},{8,16},{10,2},{16,24},{18,10},{24,28},{26,18},{28,20},... | collective-permute-start | bytes 1572872 | tf_op jit(solution)/shard_map/ppermute | solution.py:168
  6.6 12.7 %collective-permute-start.4 = (f32[512,256]{1,0:T(8,128)S(1)}, f32[512,256]{1,0:T(8,128)S(1)}, u32[]{:S(2)}, u32[]{:S(2)}) collective-permute-start(f32[512,256]{1,0:T(8,128)S(1)} %pad_maximum_fusion.1), channel_id=1, source_target_pairs={{0,8},{2,6},{8,16},{10,2},{16,24},{18,10},{24,28},{26,18},{28,20},... | collective-permute-start | bytes 1572872 | tf_op jit(solution)/shard_map/ppermute | solution.py:168
  13.3 11.6 %collective-permute-start.3 = (f32[512,256]{1,0:T(8,128)S(1)}, f32[512,256]{1,0:T(8,128)S(1)}, u32[]{:S(2)}, u32[]{:S(2)}) collective-permute-start(f32[512,256]{1,0:T(8,128)S(1)} %collective-permute-done.2.refs_2_), channel_id=1, source_target_pairs={{0,8},{2,6},{8,16},{10,2},{16,24},{18,10},{24,28},{26,18},{28,20},... | collective-permute-start | bytes 1572872 | tf_op jit(solution)/shard_map/ppermute | solution.py:168
  19.3 11.2 %collective-permute-start.6 = (f32[512,256]{1,0:T(8,128)S(1)}, f32[512,256]{1,0:T(8,128)S(1)}, u32[]{:S(2)}, u32[]{:S(2)}) collective-permute-start(f32[512,256]{1,0:T(8,128)S(1)} %collective-permute-done.4.refs_2_), channel_id=1, source_target_pairs={{0,8},{2,6},{8,16},{10,2},{16,24},{18,10},{24,28},{26,18},{28,20},... | collective-permute-start | bytes 1572872 | tf_op jit(solution)/shard_map/ppermute | solution.py:168
  24.9 11.2 %collective-permute-start.5 = (f32[512,256]{1,0:T(8,128)S(1)}, f32[512,256]{1,0:T(8,128)S(1)}, u32[]{:S(2)}, u32[]{:S(2)}) collective-permute-start(f32[512,256]{1,0:T(8,128)S(1)} %collective-permute-done.3.refs_2_), channel_id=1, source_target_pairs={{0,8},{2,6},{8,16},{10,2},{16,24},{18,10},{24,28},{26,18},{28,20},... | collective-permute-start | bytes 1572872 | tf_op jit(solution)/shard_map/ppermute | solution.py:168
  30.6 11.3 %collective-permute-start.8 = (f32[512,256]{1,0:T(8,128)S(1)}, f32[512,256]{1,0:T(8,128)S(1)}, u32[]{:S(2)}, u32[]{:S(2)}) collective-permute-start(f32[512,256]{1,0:T(8,128)S(1)} %collective-permute-done.6.refs_2_), channel_id=1, source_target_pairs={{0,8},{2,6},{8,16},{10,2},{16,24},{18,10},{24,28},{26,18},{28,20},... | collective-permute-start | bytes 1572872 | tf_op jit(solution)/shard_map/ppermute | solution.py:168
  36.2 10.9 %collective-permute-start.7 = (f32[512,256]{1,0:T(8,128)S(1)}, f32[512,256]{1,0:T(8,128)S(1)}, u32[]{:S(2)}, u32[]{:S(2)}) collective-permute-start(f32[512,256]{1,0:T(8,128)S(1)} %collective-permute-done.5.refs_2_), channel_id=1, source_target_pairs={{0,8},{2,6},{8,16},{10,2},{16,24},{18,10},{24,28},{26,18},{28,20},... | collective-permute-start | bytes 1572872 | tf_op jit(solution)/shard_map/ppermute | solution.py:168
  48.1 1.6 %collective-permute-start.9 = (f32[512,128]{1,0:T(8,128)S(1)}, f32[512,128]{1,0:T(8,128)S(1)}, u32[]{:S(2)}, u32[]{:S(2)}) collective-permute-start(f32[512,128]{1,0:T(8,128)S(1)} %pair_terms.18), channel_id=1, source_target_pairs={{0,2},{2,0},{4,6},{6,4},{8,10},{10,8},{12,14},{14,12},{16,18},{18,... | collective-permute-start | bytes 786440 | tf_op jit(solution)/shard_map/ppermute | solution.py:171
  49.8 8.7 %collective-permute-start.11 = (f32[512,128]{1,0:T(8,128)S(1)}, f32[512,128]{1,0:T(8,128)S(1)}, u32[]{:S(2)}, u32[]{:S(2)}) collective-permute-start(f32[512,128]{1,0:T(8,128)S(1)} %add.16), channel_id=1, source_target_pairs={{0,1},{1,0},{2,3},{3,2},{4,5},{5,4},{6,7},{7,6},{8,9},{9,8},{10,11... | collective-permute-start | bytes 786440 | tf_op jit(solution)/shard_map/ppermute | solution.py:202
  55.4 3.0 %collective-permute-start.10 = (f32[512,128]{1,0:T(8,128)S(1)}, f32[512,128]{1,0:T(8,128)S(1)}, u32[]{:S(2)}, u32[]{:S(2)}) collective-permute-start(f32[512,128]{1,0:T(8,128)S(1)} %slice.9), channel_id=1, source_target_pairs={{0,2},{2,0},{4,6},{6,4},{8,10},{10,8},{12,14},{14,12},{16,18},{18,... | collective-permute-start | bytes 786440 | tf_op jit(solution)/shard_map/ppermute | solution.py:171

commit v5 on v4

--- a/solution.py
+++ b/solution.py
@@ -42,32 +42,59 @@
     return feat, fac * jnp.exp2(-0.5 * norm)
 
 
-def rows_kernel(replicas, blocks, block, rep_ref, feat_ref, fac_ref, *refs):
-    feat_out, fac_out = refs[-2:]
-    count, width = feat_ref.shape
+def store_split(out, at, x):
+    high, low = split(x)
+    out[at, : x.shape[1]] = high
+    out[at, x.shape[1] :] = low
+
+
+def own_rows_kernel(replicas, rep_ref, feat_ref, fac_ref, feat_out, fac_out, *parts):
+    count = feat_ref.shape[0]
     share = count // replicas
     for k in range(replicas):
-        place = lax.rem(k - rep_ref[0] - 1 + replicas, replicas) * (blocks * share) + block * share
-        at = pl.ds(pl.multiple_of(place, share), share)
-        here = slice(k * share, (k + 1) * share)
-        for out, x in zip((feat_out, fac_out), scale(feat_ref[here, :], fac_ref[here, :]), strict=True):
-            high, low = split(x)
-            out[at, :width] = high
-            out[at, width:] = low
-
-
-def split_rows(rep, replicas, blocks, block, feat, fac, filled=()):
+        here = pl.ds(pl.multiple_of(lax.rem(rep_ref[0] + 1 + k, replicas) * share, share), share)
+        values = scale(feat_ref[here, :], fac_ref[here, :])
+        part, first = divmod(k * share, parts[0].shape[0])
+        for out, x, raw in zip((feat_out, fac_out), values, parts[2 * part : 2 * part + 2], strict=True):
+            store_split(out, pl.ds((2 * k + 1) * share, share), x)
+            raw[first : first + share, :] = x
+
+
+def own_rows(rep, replicas, feat, fac, part):
     count, width = feat.shape
-    out = jax.ShapeDtypeStruct((count * blocks, 2 * width), BF16)
+    split_out = jax.ShapeDtypeStruct((2 * count, 2 * width), BF16)
+    outs = [split_out] * 2 + [jax.ShapeDtypeStruct((part, width), F32)] * (2 * (count // part))
     return pl.pallas_call(
-        functools.partial(rows_kernel, replicas, blocks, block),
-        in_specs=[pl.BlockSpec(memory_space=pltpu.SMEM)] + [IN_VMEM] * (2 + len(filled)),
+        functools.partial(own_rows_kernel, replicas),
+        in_specs=[pl.BlockSpec(memory_space=pltpu.SMEM)] + [IN_VMEM] * 2,
+        out_specs=[IN_VMEM] * len(outs),
+        out_shape=outs,
+        compiler_params=pltpu.CompilerParams(vmem_limit_bytes=VMEM_LIMIT),
+        name="own_rows",
+    )(rep, feat, fac)
+
+
+def other_rows_kernel(share, n_parts, *refs):
+    outs = refs[-2:]
+    rows = refs[0].shape[0]
+    for part in range(n_parts):
+        for first in range(0, rows, share):
+            k = (part * rows + first) // share
+            for out, x in zip(outs, refs[2 * part : 2 * part + 2], strict=True):
+                store_split(out, pl.ds(2 * k * share, share), x[first : first + share, :])
+
+
+def other_rows(share, parts, filled):
+    n_parts = len(parts) // 2
+    return pl.pallas_call(
+        functools.partial(other_rows_kernel, share, n_parts),
+        in_specs=[IN_VMEM] * (len(parts) + 2),
         out_specs=[IN_VMEM] * 2,
-        out_shape=[out] * 2,
-        input_output_aliases={3: 0, 4: 1} if filled else {},
+        out_shape=[jax.ShapeDtypeStruct(x.shape, x.dtype) for x in filled],
+        input_output_aliases={len(parts): 0, len(parts) + 1: 1},
         compiler_params=pltpu.CompilerParams(vmem_limit_bytes=VMEM_LIMIT),
-        name="split_rows",
-    )(rep, feat, fac, *filled)
+        name="other_rows",
+    )(*parts, *filled)
 
 
 def pair_kernel(n_units, has_acc, start, acc_start, size, *refs):
@@ -170,27 +197,28 @@
     def other_core(x):
         return lax.ppermute(x, "blk", [(b, b ^ 1) for b in range(blocks)])
 
-    def units_of(*blocks):
-        return jnp.concatenate(scale(*(lax.dynamic_slice_in_dim(x, rep * share, share) for x in blocks)), axis=1)
-
-    own = units_of(features, factors)
+    slices = (lax.dynamic_slice_in_dim(x, rep * share, share) for x in (features, factors))
+    own = jnp.concatenate(scale(*slices), axis=1)
     first = ring(own)
     own, features, factors = after((own, features, factors))
-    filled = split_rows(rep_ref, replicas, 2, 1, features, factors)
-    *filled, features, factors = after((*filled, features, factors))
-    features, factors = other_core(features), other_core(factors)
-    second = ring(units_of(features, factors))
-    feat, fac = split_rows(rep_ref, replicas, 2, 0, features, factors, filled)
+    part = share if replicas <= 4 else count
+    made = own_rows(rep_ref, replicas, features, factors, part)
+    filled, parts = made[:2], made[2:]
+    parts = [other_core(x) for x in parts]
+    second = ring(jnp.concatenate([x[part - share :] for x in parts[-2:]], axis=1))
+    feat, fac = other_rows(share, parts, filled)
     mine_at = 2 * share * (replicas - 1)
-    acc = pairs(feat, fac, [own], size=mine_at) if mine_at else jnp.zeros((2 * count, width), F32)
 
     full = (homes - 1) // 2
     total = 2 * full + (homes + 1) % 2
     flying = [first, second]
+    acc = None
     for step in range(total - 1):
-        here, acc = after((flying[step % 2], acc))
+        here, feat, fac, acc = after((flying[step % 2], feat, fac, acc))
         if step + 2 < total:
             flying[step % 2] = ring(here)
+        if acc is None:
+            acc = pairs(feat, fac, [own], size=mine_at)
         acc = pairs(feat, fac, [here], acc)
     last, acc = after((flying[(total - 1) % 2], acc))
 
@@ -202,7 +230,8 @@
         arrived.append(lax.ppermute(part, "rep", [(r, (r + k + 1) % replicas) for r in range(replicas)]))
         acc, part = after((acc, part))
     part = pairs(feat, fac, [own, last], acc, mine_at, 2 * share)
-    part = part[share:] + other_core(part[:share])
+    half = share // 2
+    part = part[share:] + jnp.concatenate([other_core(part[:half]), other_core(part[half:share])])
     for x in arrived:
         part = part + x
     return part * (1.0 / (width * math.sqrt(math.log2(math.e) / width)))

time: 59.3 us -> 57.6 us (0.971)
  starting transfers between devices: 16.8 us -> 15.8 us
  local copies, waits for them, and re-layouts: 1.02 us -> 0.03 us
  waiting for transfers between devices: 7.17 us -> 7.78 us
    ppermute x4 -> x7, waiting for transfers between devices: 0.44 us -> 2.35 us  [other_core(): return lax.ppermute(x, 'blk', [(b, b ^ 1) for b in range(blocks)])]
    ppermute x7, starting transfers between devices: 14 us -> 12.3 us  [ring(): return lax.ppermute(x, 'blk', moves)]
    ppermute x1, waiting for transfers between devices: 2.95 us -> 1.46 us  [body(): lax.ppermute(part, 'rep', [(r, (r + k + 1) % replicas) for r in range(rep...]
    unnamed x4, local copies, waits for them, and re-layouts: 1 us -> 0.01 us
    ppermute x4 -> x7, starting transfers between devices: 0.74 us -> 1.72 us  [other_core(): return lax.ppermute(x, 'blk', [(b, b ^ 1) for b in range(blocks)])]
    reduce_sum x2 -> x1, other arithmetic: 1.3 us -> 1.15 us  [scale(): norm = jnp.sum(feat * feat, axis=1, keepdims=True)]
  transfers between devices with their start and end apart: 12 -> 15, of which waited for: 4 -> 8; matrix products, arithmetic and copies ran while one was open for 1% -> 0% of each run, Pallas kernels for 51% -> 53%
where the time goes in v5:
time: 57.6 us; the launch traced here: 57.4 us
  Pallas kernels  31.5 us (55%)
  starting transfers between devices  15.8 us (27%)
  waiting for transfers between devices  7.78 us (14%)
  other arithmetic  2.14 us (4%)
    pallas_call x10, Pallas kernels, call(): pl.pallas_call(kernel, in_specs=[IN_VMEM] * len(args), out_specs=jax.tree...  31 us
    ppermute x7, starting transfers between devices, ring(): return lax.ppermute(x, 'blk', moves)  12.3 us
    ppermute x7, waiting for transfers between devices, ring(): return lax.ppermute(x, 'blk', moves)  3.97 us
    ppermute x7, waiting for transfers between devices, other_core(): return lax.ppermute(x, 'blk', [(b, b ^ 1) for b in range(blocks)])  2.35 us
    ppermute x1, starting transfers between devices, body(): lax.ppermute(part, 'rep', [(r, (r + k + 1) % replicas) for r in range(rep...  1.77 us
    ppermute x7, starting transfers between devices, other_core(): return lax.ppermute(x, 'blk', [(b, b ^ 1) for b in range(blocks)])  1.72 us
    ppermute x1, waiting for transfers between devices, body(): lax.ppermute(part, 'rep', [(r, (r + k + 1) % replicas) for r in range(rep...  1.46 us
    reduce_sum x1, other arithmetic, scale(): norm = jnp.sum(feat * feat, axis=1, keepdims=True)  1.15 us
  transfers between devices with their start and end apart: 15, of which 8 were waited for; matrix products, arithmetic and copies ran while one was open for 0% of the time, Pallas kernels for 53%

profile of v5, /device:TPU:0, one launch (start us, length us, event | category | flops | bytes accessed | tf_op | source)
XLA Modules:
  0.0 57.4 jit_solution(10998498562943366428)
XLA Ops:
  0.0 1.2 %multiply_reduce_fusion = (f32[512]{0:T(512)S(1)}, f32[512,128]{1,0:T(8,128)S(1)}) fusion(f32[1024,128]{1,0:T(8,128)} %feat_ref, s32[]{:T(128)S(6)} %select_n.4), kind=kLoop, calls=%fused_computation.5 | loop fusion | flops 196096 | bytes 526340 | tf_op jit(solution)/shard_map/reduce_sum | solution.py:41
  1.2 0.0 copy-done.1
  1.2 0.1 dynamic-slice_multiply_fusion
  1.3 0.0 copy-start
  1.4 3.1 %collective-permute-start.3 = (f32[512,256]{1,0:T(8,128)S(1)}, f32[512,256]{1,0:T(8,128)S(1)}, u32[]{:S(2)}, u32[]{:S(2)}) collective-permute-start(f32[512,256]{1,0:T(8,128)S(1)} %pad_maximum_fusion.refs_2_), channel_id=1, source_target_pairs={{0,8},{2,6},{8,16},{10,2},{16,24},{18,10},{24,28},{26,18},{28,20},... | collective-permute-start | bytes 1572872 | tf_op jit(solution)/shard_map/ppermute | solution.py:195
  4.5 0.0 copy-done
  4.5 0.3 own_rows.1
  4.7 0.1 collective-permute-start
  4.8 0.5 collective-permute-start.1
  5.3 0.1 collective-permute-start.4
  5.4 0.4 collective-permute-start.5
  5.8 0.5 collective-permute-done.refs_2_
  6.3 0.4 collective-permute-done.1.refs_3_
  6.7 1.6 %collective-permute-start.2 = (f32[512,256]{1,0:T(8,128)S(1)}, f32[512,256]{1,0:T(8,128)S(1)}, u32[]{:S(2)}, u32[]{:S(2)}) collective-permute-start(f32[512,256]{1,0:T(8,128)S(1)} %pad_maximum_fusion.1), channel_id=1, source_target_pairs={{0,8},{2,6},{8,16},{10,2},{16,24},{18,10},{24,28},{26,18},{28,20},... | collective-permute-start | bytes 1572872 | tf_op jit(solution)/shard_map/ppermute | solution.py:195
  8.4 0.0 collective-permute-done.4.refs_0_
  8.4 0.0 collective-permute-done.5.refs_1_
  8.4 0.2 other_rows.1
  8.6 3.0 %collective-permute-done.3.refs_2_ = f32[512,256]{1,0:T(8,128)S(1)} collective-permute-done((f32[512,256]{1,0:T(8,128)S(1)}, f32[512,256]{1,0:T(8,128)S(1)}, u32[]{:S(2)}, u32[]{:S(2)}) %collective-permute-start.3) | collective-permute-done | bytes 524320 | tf_op jit(solution)/shard_map/ppermute | solution.py:195
  11.6 2.1 %collective-permute-start.7 = (f32[512,256]{1,0:T(8,128)S(1)}, f32[512,256]{1,0:T(8,128)S(1)}, u32[]{:S(2)}, u32[]{:S(2)}) collective-permute-start(f32[512,256]{1,0:T(8,128)S(1)} %collective-permute-done.3.refs_2_), channel_id=1, source_target_pairs={{0,8},{2,6},{8,16},{10,2},{16,24},{18,10},{24,28},{26,18},{28,20},... | collective-permute-start | bytes 1572872 | tf_op jit(solution)/shard_map/ppermute | solution.py:195
  13.6 1.9 %pair_terms.10.refs_3_ = f32[2048,128]{1,0:T(8,128)S(1)} custom-call(bf16[2048,256]{1,0:T(8,128)(2,1)S(1)} %get-tuple-element.72.refs_0_, bf16[2048,256]{1,0:T(8,128)(2,1)S(1)} %get-tuple-element.73.refs_1_, f32[512,256]{1,0:T(8,128)S(1)} %pad_maximum_fusion.refs_2_), custom_call_target="tpu_custom_call" | custom-call | flops 1610612736 | bytes 4194304 | tf_op jit(solution)/shard_map/pair_terms/pallas_call | solution.py:25
  15.5 3.9 %pair_terms.11.refs_3_ = f32[2048,128]{1,0:T(8,128)S(1)} custom-call(bf16[2048,256]{1,0:T(8,128)(2,1)S(1)} %get-tuple-element.72.refs_0_, bf16[2048,256]{1,0:T(8,128)(2,1)S(1)} %get-tuple-element.73.refs_1_, f32[512,256]{1,0:T(8,128)S(1)} %collective-permute-done.3.refs_2_, f32[2048,128]{1,0:T(8,128)S(1)} %pair_terms.10.refs_3_), custom_call_target="tpu_custom_call", output_to_operand_aliasing={{}: (3, {})} | custom-call | flops 3221225472 | bytes 4194304 | tf_op jit(solution)/shard_map/pair_terms/pallas_call | solution.py:25
  19.5 0.0 collective-permute-done.2.refs_2_
  19.5 1.6 %collective-permute-start.6 = (f32[512,256]{1,0:T(8,128)S(1)}, f32[512,256]{1,0:T(8,128)S(1)}, u32[]{:S(2)}, u32[]{:S(2)}) collective-permute-start(f32[512,256]{1,0:T(8,128)S(1)} %collective-permute-done.2.refs_2_), channel_id=1, source_target_pairs={{0,8},{2,6},{8,16},{10,2},{16,24},{18,10},{24,28},{26,18},{28,20},... | collective-permute-start | bytes 1572872 | tf_op jit(solution)/shard_map/ppermute | solution.py:195
  21.1 3.9 %pair_terms.12.refs_3_ = f32[2048,128]{1,0:T(8,128)S(1)} custom-call(bf16[2048,256]{1,0:T(8,128)(2,1)S(1)} %get-tuple-element.72.refs_0_, bf16[2048,256]{1,0:T(8,128)(2,1)S(1)} %get-tuple-element.73.refs_1_, f32[512,256]{1,0:T(8,128)S(1)} %collective-permute-done.2.refs_2_, f32[2048,128]{1,0:T(8,128)S(1)} %pair_terms.11.refs_3_), custom_call_target="tpu_custom_call", output_to_operand_aliasing={{}: (3, {})} | custom-call | flops 3221225472 | bytes 4194304 | tf_op jit(solution)/shard_map/pair_terms/pallas_call | solution.py:25
  25.0 0.0 collective-permute-done.7.refs_2_
  25.0 1.6 %collective-permute-start.9 = (f32[512,256]{1,0:T(8,128)S(1)}, f32[512,256]{1,0:T(8,128)S(1)}, u32[]{:S(2)}, u32[]{:S(2)}) collective-permute-start(f32[512,256]{1,0:T(8,128)S(1)} %collective-permute-done.7.refs_2_), channel_id=1, source_target_pairs={{0,8},{2,6},{8,16},{10,2},{16,24},{18,10},{24,28},{26,18},{28,20},... | collective-permute-start | bytes 1572872 | tf_op jit(solution)/shard_map/ppermute | solution.py:195
  26.6 3.9 %pair_terms.13.refs_3_ = f32[2048,128]{1,0:T(8,128)S(1)} custom-call(bf16[2048,256]{1,0:T(8,128)(2,1)S(1)} %get-tuple-element.72.refs_0_, bf16[2048,256]{1,0:T(8,128)(2,1)S(1)} %get-tuple-element.73.refs_1_, f32[512,256]{1,0:T(8,128)S(1)} %collective-permute-done.7.refs_2_, f32[2048,128]{1,0:T(8,128)S(1)} %pair_terms.12.refs_3_), custom_call_target="tpu_custom_call", output_to_operand_aliasing={{}: (3, {})} | custom-call | flops 3221225472 | bytes 4194304 | tf_op jit(solution)/shard_map/pair_terms/pallas_call | solution.py:25
  30.6 0.0 collective-permute-done.6.refs_2_
  30.6 1.6 %collective-permute-start.8 = (f32[512,256]{1,0:T(8,128)S(1)}, f32[512,256]{1,0:T(8,128)S(1)}, u32[]{:S(2)}, u32[]{:S(2)}) collective-permute-start(f32[512,256]{1,0:T(8,128)S(1)} %collective-permute-done.6.refs_2_), channel_id=1, source_target_pairs={{0,8},{2,6},{8,16},{10,2},{16,24},{18,10},{24,28},{26,18},{28,20},... | collective-permute-start | bytes 1572872 | tf_op jit(solution)/shard_map/ppermute | solution.py:195
  32.1 3.9 %pair_terms.14.refs_3_ = f32[2048,128]{1,0:T(8,128)S(1)} custom-call(bf16[2048,256]{1,0:T(8,128)(2,1)S(1)} %get-tuple-element.72.refs_0_, bf16[2048,256]{1,0:T(8,128)(2,1)S(1)} %get-tuple-element.73.refs_1_, f32[512,256]{1,0:T(8,128)S(1)} %collective-permute-done.6.refs_2_, f32[2048,128]{1,0:T(8,128)S(1)} %pair_terms.13.refs_3_), custom_call_target="tpu_custom_call", output_to_operand_aliasing={{}: (3, {})} | custom-call | flops 3221225472 | bytes 4194304 | tf_op jit(solution)/shard_map/pair_terms/pallas_call | solution.py:25
  36.0 0.0 collective-permute-done.9.refs_2_
  36.1 0.7 %collective-permute-start.10 = (f32[512,256]{1,0:T(8,128)S(1)}, f32[512,256]{1,0:T(8,128)S(1)}, u32[]{:S(2)}, u32[]{:S(2)}) collective-permute-start(f32[512,256]{1,0:T(8,128)S(1)} %collective-permute-done.9.refs_2_), channel_id=1, source_target_pairs={{0,8},{2,6},{8,16},{10,2},{16,24},{18,10},{24,28},{26,18},{28,20},... | collective-permute-start | bytes 1572872 | tf_op jit(solution)/shard_map/ppermute | solution.py:195
  36.7 3.9 %pair_terms.15.refs_3_ = f32[2048,128]{1,0:T(8,128)S(1)} custom-call(bf16[2048,256]{1,0:T(8,128)(2,1)S(1)} %get-tuple-element.72.refs_0_, bf16[2048,256]{1,0:T(8,128)(2,1)S(1)} %get-tuple-element.73.refs_1_, f32[512,256]{1,0:T(8,128)S(1)} %collective-permute-done.9.refs_2_, f32[2048,128]{1,0:T(8,128)S(1)} %pair_terms.14.refs_3_), custom_call_target="tpu_custom_call", output_to_operand_aliasing={{}: (3, {})} | custom-call | flops 3221225472 | bytes 4194304 | tf_op jit(solution)/shard_map/pair_terms/pallas_call | solution.py:25
  40.6 0.0 collective-permute-done.8.refs_2_
  40.7 3.9 %pair_terms.16.refs_3_.refs_4_ = f32[2048,128]{1,0:T(8,128)S(1)} custom-call(bf16[2048,256]{1,0:T(8,128)(2,1)S(1)} %get-tuple-element.72.refs_0_, bf16[2048,256]{1,0:T(8,128)(2,1)S(1)} %get-tuple-element.73.refs_1_, f32[512,256]{1,0:T(8,128)S(1)} %collective-permute-done.8.refs_2_, f32[2048,128]{1,0:T(8,128)S(1)} %pair_terms.15.refs_3_), custom_call_target="tpu_custom_call", output_to_operand_aliasing={{}: (3, {})} | custom-call | flops 3221225472 | bytes 4194304 | tf_op jit(solution)/shard_map/pair_terms/pallas_call | solution.py:25
  44.6 1.0 %collective-permute-done.10.refs_2_.refs_3_ = f32[512,256]{1,0:T(8,128)S(1)} collective-permute-done((f32[512,256]{1,0:T(8,128)S(1)}, f32[512,256]{1,0:T(8,128)S(1)}, u32[]{:S(2)}, u32[]{:S(2)}) %collective-permute-start.10) | collective-permute-done | bytes 524320 | tf_op jit(solution)/shard_map/ppermute | solution.py:195
  45.6 1.1 %pair_terms.18 = f32[512,128]{1,0:T(8,128)S(1)} custom-call(bf16[2048,256]{1,0:T(8,128)(2,1)S(1)} %get-tuple-element.72.refs_0_, bf16[2048,256]{1,0:T(8,128)(2,1)S(1)} %get-tuple-element.73.refs_1_, f32[512,256]{1,0:T(8,128)S(1)} %collective-permute-done.10.refs_2_.refs_3_, f32[2048,128]{1,0:T(8,128)S(1)} %pair_terms.16.refs_3_.refs_4_), custom_call_target="tpu_custom_call" | custom-call | flops 805306368 | bytes 4194304 | tf_op jit(solution)/shard_map/pair_terms/pallas_call | solution.py:25
  46.6 0.1 collective-permute-start.11
  46.7 1.1 %pair_terms.17 = f32[512,128]{1,0:T(8,128)S(1)} custom-call(bf16[2048,256]{1,0:T(8,128)(2,1)S(1)} %get-tuple-element.72.refs_0_, bf16[2048,256]{1,0:T(8,128)(2,1)S(1)} %get-tuple-element.73.refs_1_, f32[512,256]{1,0:T(8,128)S(1)} %collective-permute-done.10.refs_2_.refs_3_, f32[2048,128]{1,0:T(8,128)S(1)} %pair_terms.16.refs_3_.refs_4_), custom_call_target="tpu_custom_call" | custom-call | flops 805306368 | bytes 4194304 | tf_op jit(solution)/shard_map/pair_terms/pallas_call | solution.py:25
  47.8 0.4 collective-permute-done.11
  48.3 1.8 %collective-permute-start.14 = (f32[512,128]{1,0:T(8,128)S(1)}, f32[512,128]{1,0:T(8,128)S(1)}, u32[]{:S(2)}, u32[]{:S(2)}) collective-permute-start(f32[512,128]{1,0:T(8,128)S(1)} %add.14), channel_id=1, source_target_pairs={{0,1},{1,0},{2,3},{3,2},{4,5},{5,4},{6,7},{7,6},{8,9},{9,8},{10,11... | collective-permute-start | bytes 786440 | tf_op jit(solution)/shard_map/ppermute | solution.py:230
  50.0 3.5 %pair_terms.19 = f32[1024,128]{1,0:T(8,128)S(1)} custom-call(bf16[2048,256]{1,0:T(8,128)(2,1)S(1)} %get-tuple-element.72.refs_0_, bf16[2048,256]{1,0:T(8,128)(2,1)S(1)} %get-tuple-element.73.refs_1_, f32[512,256]{1,0:T(8,128)S(1)} %pad_maximum_fusion.refs_2_, f32[512,256]{1,0:T(8,128)S(1)} %collective-permute-done.10.refs_2_.refs_3_, ...), custom_call_target="tpu_custom_call" | custom-call | flops 3221225472 | bytes 4194304 | tf_op jit(solution)/shard_map/pair_terms/pallas_call | solution.py:25
  53.6 0.1 collective-permute-start.12
  53.7 0.5 collective-permute-start.13
  54.2 0.8 %collective-permute-done.12 = f32[256,128]{1,0:T(8,128)S(1)} collective-permute-done((f32[256,128]{1,0:T(8,128)S(1)}, f32[256,128]{1,0:T(8,128)S(1)}, u32[]{:S(2)}, u32[]{:S(2)}) %collective-permute-start.12) | collective-permute-done | bytes 131104 | tf_op jit(solution)/shard_map/ppermute | solution.py:198
  55.0 0.2 collective-permute-done.13
  55.2 1.5 %collective-permute-done.14 = f32[512,128]{1,0:T(8,128)S(1)} collective-permute-done((f32[512,128]{1,0:T(8,128)S(1)}, f32[512,128]{1,0:T(8,128)S(1)}, u32[]{:S(2)}, u32[]{:S(2)}) %collective-permute-start.14) | collective-permute-done | bytes 262176 | tf_op jit(solution)/shard_map/ppermute | solution.py:230
  56.7 0.7 %fusion.1 = f32[512,128]{1,0:T(8,128)} fusion(f32[512,128]{1,0:T(8,128)S(1)} %collective-permute-done.14, f32[1024,128]{1,0:T(8,128)S(1)} %pair_terms.19, f32[256,128]{1,0:T(8,128)S(1)} %collective-permute-done.13, f32[256,128]{1,0:T(8,128)S(1)} %collective-permute-done.12), kind=kLoop, calls=%fused_computation.4 | loop fusion | flops 262144 | bytes 1048576 | tf_op jit(solution)/shard_map/mul | solution.py:237
  (6 shorter events, 0.1 us)
Async XLA Ops:
  0.0 1.2 %copy-start.1 = (f32[1024,128]{1,0:T(8,128)S(1)}, f32[1024,128]{1,0:T(8,128)}, u32[]{:S(2)}) copy-start(f32[1024,128]{1,0:T(8,128)} %fac_ref) | copy-start | bytes 1572868
  1.3 3.1 %copy-start = (f32[1024,128]{1,0:T(8,128)S(1)}, f32[1024,128]{1,0:T(8,128)}, u32[]{:S(2)}) copy-start(f32[1024,128]{1,0:T(8,128)} %feat_ref) | copy-start | bytes 1572868
  1.4 10.2 %collective-permute-start.3 = (f32[512,256]{1,0:T(8,128)S(1)}, f32[512,256]{1,0:T(8,128)S(1)}, u32[]{:S(2)}, u32[]{:S(2)}) collective-permute-start(f32[512,256]{1,0:T(8,128)S(1)} %pad_maximum_fusion.refs_2_), channel_id=1, source_target_pairs={{0,8},{2,6},{8,16},{10,2},{16,24},{18,10},{24,28},{26,18},{28,20},... | collective-permute-start | bytes 1572872 | tf_op jit(solution)/shard_map/ppermute | solution.py:195
  4.7 1.6 %collective-permute-start = (f32[512,128]{1,0:T(8,128)S(1)}, f32[512,128]{1,0:T(8,128)S(1)}, u32[]{:S(2)}, u32[]{:S(2)}) collective-permute-start(f32[512,128]{1,0:T(8,128)S(1)} %get-tuple-element.44), channel_id=1, source_target_pairs={{0,2},{2,0},{4,6},{6,4},{8,10},{10,8},{12,14},{14,12},{16,18},{18,... | collective-permute-start | bytes 786440 | tf_op jit(solution)/shard_map/ppermute | solution.py:198
  4.8 1.9 %collective-permute-start.1 = (f32[512,128]{1,0:T(8,128)S(1)}, f32[512,128]{1,0:T(8,128)S(1)}, u32[]{:S(2)}, u32[]{:S(2)}) collective-permute-start(f32[512,128]{1,0:T(8,128)S(1)} %get-tuple-element.45), channel_id=1, source_target_pairs={{0,2},{2,0},{4,6},{6,4},{8,10},{10,8},{12,14},{14,12},{16,18},{18,... | collective-permute-start | bytes 786440 | tf_op jit(solution)/shard_map/ppermute | solution.py:198
  5.3 3.1 %collective-permute-start.4 = (f32[512,128]{1,0:T(8,128)S(1)}, f32[512,128]{1,0:T(8,128)S(1)}, u32[]{:S(2)}, u32[]{:S(2)}) collective-permute-start(f32[512,128]{1,0:T(8,128)S(1)} %get-tuple-element.46), channel_id=1, source_target_pairs={{0,2},{2,0},{4,6},{6,4},{8,10},{10,8},{12,14},{14,12},{16,18},{18,... | collective-permute-start | bytes 786440 | tf_op jit(solution)/shard_map/ppermute | solution.py:198
  5.4 3.0 %collective-permute-start.5 = (f32[512,128]{1,0:T(8,128)S(1)}, f32[512,128]{1,0:T(8,128)S(1)}, u32[]{:S(2)}, u32[]{:S(2)}) collective-permute-start(f32[512,128]{1,0:T(8,128)S(1)} %get-tuple-element.47), channel_id=1, source_target_pairs={{0,2},{2,0},{4,6},{6,4},{8,10},{10,8},{12,14},{14,12},{16,18},{18,... | collective-permute-start | bytes 786440 | tf_op jit(solution)/shard_map/ppermute | solution.py:198
  6.7 12.7 %collective-permute-start.2 = (f32[512,256]{1,0:T(8,128)S(1)}, f32[512,256]{1,0:T(8,128)S(1)}, u32[]{:S(2)}, u32[]{:S(2)}) collective-permute-start(f32[512,256]{1,0:T(8,128)S(1)} %pad_maximum_fusion.1), channel_id=1, source_target_pairs={{0,8},{2,6},{8,16},{10,2},{16,24},{18,10},{24,28},{26,18},{28,20},... | collective-permute-start | bytes 1572872 | tf_op jit(solution)/shard_map/ppermute | solution.py:195
  11.6 13.4 %collective-permute-start.7 = (f32[512,256]{1,0:T(8,128)S(1)}, f32[512,256]{1,0:T(8,128)S(1)}, u32[]{:S(2)}, u32[]{:S(2)}) collective-permute-start(f32[512,256]{1,0:T(8,128)S(1)} %collective-permute-done.3.refs_2_), channel_id=1, source_target_pairs={{0,8},{2,6},{8,16},{10,2},{16,24},{18,10},{24,28},{26,18},{28,20},... | collective-permute-start | bytes 1572872 | tf_op jit(solution)/shard_map/ppermute | solution.py:195
  19.5 11.1 %collective-permute-start.6 = (f32[512,256]{1,0:T(8,128)S(1)}, f32[512,256]{1,0:T(8,128)S(1)}, u32[]{:S(2)}, u32[]{:S(2)}) collective-permute-start(f32[512,256]{1,0:T(8,128)S(1)} %collective-permute-done.2.refs_2_), channel_id=1, source_target_pairs={{0,8},{2,6},{8,16},{10,2},{16,24},{18,10},{24,28},{26,18},{28,20},... | collective-permute-start | bytes 1572872 | tf_op jit(solution)/shard_map/ppermute | solution.py:195
  25.0 11.0 %collective-permute-start.9 = (f32[512,256]{1,0:T(8,128)S(1)}, f32[512,256]{1,0:T(8,128)S(1)}, u32[]{:S(2)}, u32[]{:S(2)}) collective-permute-start(f32[512,256]{1,0:T(8,128)S(1)} %collective-permute-done.7.refs_2_), channel_id=1, source_target_pairs={{0,8},{2,6},{8,16},{10,2},{16,24},{18,10},{24,28},{26,18},{28,20},... | collective-permute-start | bytes 1572872 | tf_op jit(solution)/shard_map/ppermute | solution.py:195
  30.6 10.1 %collective-permute-start.8 = (f32[512,256]{1,0:T(8,128)S(1)}, f32[512,256]{1,0:T(8,128)S(1)}, u32[]{:S(2)}, u32[]{:S(2)}) collective-permute-start(f32[512,256]{1,0:T(8,128)S(1)} %collective-permute-done.6.refs_2_), channel_id=1, source_target_pairs={{0,8},{2,6},{8,16},{10,2},{16,24},{18,10},{24,28},{26,18},{28,20},... | collective-permute-start | bytes 1572872 | tf_op jit(solution)/shard_map/ppermute | solution.py:195
  36.1 9.5 %collective-permute-start.10 = (f32[512,256]{1,0:T(8,128)S(1)}, f32[512,256]{1,0:T(8,128)S(1)}, u32[]{:S(2)}, u32[]{:S(2)}) collective-permute-start(f32[512,256]{1,0:T(8,128)S(1)} %collective-permute-done.9.refs_2_), channel_id=1, source_target_pairs={{0,8},{2,6},{8,16},{10,2},{16,24},{18,10},{24,28},{26,18},{28,20},... | collective-permute-start | bytes 1572872 | tf_op jit(solution)/shard_map/ppermute | solution.py:195
  46.6 1.6 %collective-permute-start.11 = (f32[512,128]{1,0:T(8,128)S(1)}, f32[512,128]{1,0:T(8,128)S(1)}, u32[]{:S(2)}, u32[]{:S(2)}) collective-permute-start(f32[512,128]{1,0:T(8,128)S(1)} %pair_terms.18), channel_id=1, source_target_pairs={{0,2},{2,0},{4,6},{6,4},{8,10},{10,8},{12,14},{14,12},{16,18},{18,... | collective-permute-start | bytes 786440 | tf_op jit(solution)/shard_map/ppermute | solution.py:198
  48.3 8.4 %collective-permute-start.14 = (f32[512,128]{1,0:T(8,128)S(1)}, f32[512,128]{1,0:T(8,128)S(1)}, u32[]{:S(2)}, u32[]{:S(2)}) collective-permute-start(f32[512,128]{1,0:T(8,128)S(1)} %add.14), channel_id=1, source_target_pairs={{0,1},{1,0},{2,3},{3,2},{4,5},{5,4},{6,7},{7,6},{8,9},{9,8},{10,11... | collective-permute-start | bytes 786440 | tf_op jit(solution)/shard_map/ppermute | solution.py:230
  53.6 1.4 %collective-permute-start.12 = (f32[256,128]{1,0:T(8,128)S(1)}, f32[256,128]{1,0:T(8,128)S(1)}, u32[]{:S(2)}, u32[]{:S(2)}) collective-permute-start(f32[256,128]{1,0:T(8,128)S(1)} %get-tuple-element.81), channel_id=1, source_target_pairs={{0,2},{2,0},{4,6},{6,4},{8,10},{10,8},{12,14},{14,12},{16,18},{18,... | collective-permute-start | bytes 393224 | tf_op jit(solution)/shard_map/ppermute | solution.py:198
  53.7 1.5 %collective-permute-start.13 = (f32[256,128]{1,0:T(8,128)S(1)}, f32[256,128]{1,0:T(8,128)S(1)}, u32[]{:S(2)}, u32[]{:S(2)}) collective-permute-start(f32[256,128]{1,0:T(8,128)S(1)} %get-tuple-element.82), channel_id=1, source_target_pairs={{0,2},{2,0},{4,6},{6,4},{8,10},{10,8},{12,14},{14,12},{16,18},{18,... | collective-permute-start | bytes 393224 | tf_op jit(solution)/shard_map/ppermute | solution.py:198

commit v6 on v5

v6 whole, which is shorter than its diff:
```python
import functools
import math

import jax
import jax.numpy as jnp
from jax import lax
from jax.experimental import pallas as pl
from jax.experimental.pallas import tpu as pltpu
from jax.sharding import PartitionSpec as P

F32, BF16 = jnp.float32, jnp.bfloat16
NT = (((1,), (1,)), ((), ()))
VMEM_LIMIT = 16 << 20
IN_VMEM = pl.BlockSpec(memory_space=pltpu.VMEM)


def split(x):
    high = x.astype(BF16)
    low = (x - high.astype(F32)).astype(BF16)
    return high, low


def call(kernel, name, out, *args, scratch=(), pairs=0, aliases=None):
    width = 128
    return pl.pallas_call(
        kernel,
        in_specs=[IN_VMEM] * len(args),
        out_specs=jax.tree.map(lambda _: IN_VMEM, out),
        out_shape=out,
        scratch_shapes=scratch,
        input_output_aliases=aliases or {},
        compiler_params=pltpu.CompilerParams(vmem_limit_bytes=VMEM_LIMIT),
        cost_estimate=pl.CostEstimate(flops=2 * pairs * 12 * width, bytes_accessed=4 << 20, transcendentals=pairs),
        name=name,
    )(*args)


def scale(feat, fac):
    width = feat.shape[1]
    feat = feat * math.sqrt(math.log2(math.e) / width)
    norm = jnp.sum(feat * feat, axis=1, keepdims=True)
    return feat, fac * jnp.exp2(-0.5 * norm)


def store_split(out, at, x):
    parts = split(x)
    for k in range(4):
        out[at, k * x.shape[1] : (k + 1) * x.shape[1]] = parts[k // 2]


def own_rows_kernel(replicas, rep_ref, feat_ref, fac_ref, feat_out, fac_out, *parts):
    count = feat_ref.shape[0]
    share = count // replicas
    for k in range(replicas):
        here = pl.ds(pl.multiple_of(lax.rem(rep_ref[0] + 1 + k, replicas) * share, share), share)
        values = scale(feat_ref[here, :], fac_ref[here, :])
        for x, out, held in zip(values, (feat_out, fac_out), (parts[::2], parts[1::2]), strict=True):
            store_split(out, pl.ds((2 * k + 1) * share, share), x)
            rows = min(share, held[0].shape[0])
            for first in range(0, share, rows):
                part, at = divmod(k * share + first, held[0].shape[0])
                held[part][at : at + rows, :] = x[first : first + rows, :]


def own_rows(rep, replicas, feat, fac, part):
    count, width = feat.shape
    split_out = jax.ShapeDtypeStruct((2 * count, 4 * width), BF16)
    outs = [split_out] * 2 + [jax.ShapeDtypeStruct((part, width), F32)] * (2 * (count // part))
    return pl.pallas_call(
        functools.partial(own_rows_kernel, replicas),
        in_specs=[pl.BlockSpec(memory_space=pltpu.SMEM)] + [IN_VMEM] * 2,
        out_specs=[IN_VMEM] * len(outs),
        out_shape=outs,
        compiler_params=pltpu.CompilerParams(vmem_limit_bytes=VMEM_LIMIT),
        name="own_rows",
    )(rep, feat, fac)


def other_rows_kernel(share, n_parts, *refs):
    outs = refs[-2:]
    held = refs[0].shape[0]
    rows = min(share, held)
    for part in range(n_parts):
        for first in range(0, held, rows):
            k, at = divmod(part * held + first, share)
            for out, x in zip(outs, refs[2 * part : 2 * part + 2], strict=True):
                store_split(out, pl.ds(2 * k * share + at, rows), x[first : first + rows, :])


def other_rows(share, parts, filled):
    n_parts = len(parts) // 2
    return pl.pallas_call(
        functools.partial(other_rows_kernel, share, n_parts),
        in_specs=[IN_VMEM] * (len(parts) + 2),
        out_specs=[IN_VMEM] * 2,
        out_shape=[jax.ShapeDtypeStruct(x.shape, x.dtype) for x in filled],
        input_output_aliases={len(parts): 0, len(parts) + 1: 1},
        compiler_params=pltpu.CompilerParams(vmem_limit_bytes=VMEM_LIMIT),
        name="other_rows",
    )(*parts, *filled)


def pair_kernel(kinds, has_acc, has_more, start, acc_start, *refs):
    feat_ref, fac_ref, *refs = refs
    value, coup_rhs = refs[-2:]
    out_ref = refs[-3]
    more_ref = refs[-4] if has_more else None
    acc_ref = refs[-4 - has_more] if has_acc else None
    width = out_ref.shape[1]
    tiles = []
    for pair in kinds:
        feat, fac, refs = (refs[0], refs[1], refs[2:]) if pair else (refs[0], refs[0], refs[1:])
        tile = math.gcd(256, feat.shape[0])
        tiles += [(feat, fac, at, tile, pair) for at in range(0, feat.shape[0], tile)]
    rows = math.gcd(1024, out_ref.shape[0])

    def dot_nt(a, b):
        return lax.dot_general(a, b, NT, preferred_element_type=F32)

    def place(k):
        first = sum(t[3] for t in tiles[:k])
        return slice(first, first + tiles[k][3])

    def prepare(k):
        feat, fac, at, tile, pair = tiles[k]
        here, at = place(k), slice(at, at + tile)
        high, low = split(feat[at, :width])
        value[here, :] = jnp.concatenate([high, low, high, jnp.ones_like(high)], axis=1)
        fac = fac[at, :] if pair else fac[at, width:]
        high, low = split(jnp.concatenate([fac[:, width // 2 :], fac[:, : width // 2]], axis=1))
        coup_rhs[here, :] = jnp.concatenate([high, low], axis=1)

    def chunk(i, first):
        own = pl.ds(start + i * rows, rows)
        feat, fac = feat_ref[own, :], fac_ref[own, :]
        high_sum, low_sum, sums = None, None, None
        for k in range(len(tiles)):
            if first:
                prepare(k)
            here = place(k)
            both, other = value[here, : 2 * width], coup_rhs[here, :]
            cross = dot_nt(feat[:, : 2 * width], both) + dot_nt(feat[:, 2 * width :], both)
            coup = dot_nt(fac[:, : 2 * width], other) + dot_nt(fac[:, 2 * width :], other)
            weight = jnp.exp2(cross) * coup
            high = weight.astype(BF16)
            back = high.astype(F32)
            low = (weight - back).astype(BF16)
            a = jnp.dot(high, both, preferred_element_type=F32)
            b = jnp.dot(low, value[here, 2 * width :], preferred_element_type=F32)
            high_sum = a if high_sum is None else high_sum + a
            low_sum = b if low_sum is None else low_sum + b
            for k in range(0, weight.shape[1], width):
                sums = back[:, k : k + width] if sums is None else sums + back[:, k : k + width]
        total = high_sum[:, :width] + high_sum[:, width:] + low_sum[:, :width]
        own_high, own_low = feat[:, :width].astype(F32), feat[:, 2 * width : 3 * width].astype(F32)
        total = total - jnp.sum(sums, axis=1, keepdims=True) * (own_high + own_low) - low_sum[:, width:] * own_high
        if acc_ref is not None:
            total = acc_ref[pl.ds(acc_start + i * rows, rows), :] + total
        if more_ref is not None:
            total = more_ref[pl.ds(i * rows, rows), :] + total
        out_ref[pl.ds(i * rows, rows), :] = total

    for i in range(out_ref.shape[0] // rows):
        chunk(i, i == 0)


def pairs(feat, fac, units, acc=None, start=0, rows=None, acc_start=0, more=None):
    width = feat.shape[1] // 4
    rows = feat.shape[0] if rows is None else rows
    kinds = [isinstance(x, tuple) for x in units]
    arrays = [y for x in units for y in (x if isinstance(x, tuple) else (x,))]
    count = sum((x[0] if isinstance(x, tuple) else x).shape[0] for x in units)
    has_acc = acc is not None
    return call(
        functools.partial(pair_kernel, kinds, has_acc, more is not None, start, start - acc_start),
        "pair_terms",
        jax.ShapeDtypeStruct((rows, width), F32),
        feat,
        fac,
        *arrays,
        *([acc] if has_acc else []),
        *([more] if more is not None else []),
        scratch=[pltpu.VMEM((count, 4 * width), BF16), pltpu.VMEM((count, 2 * width), BF16)],
        pairs=rows * count,
        aliases={2 + len(arrays): 0} if has_acc and rows == acc.shape[0] else None,
    )


def ring_order(homes):
    if homes % 2:
        return list(range(homes))
    return list(range(0, homes, 2)) + list(range(homes - 1, 0, -2))


def body(features, factors):
    replicas = lax.axis_size("rep")
    blocks = lax.axis_size("blk")
    count, width = features.shape
    share = count // replicas
    rep = lax.axis_index("rep")
    rep_ref = rep.astype(jnp.int32).reshape(1)
    homes = blocks // 2
    order = ring_order(homes)
    after = lax.optimization_barrier

    def ring(x):
        moves = []
        for p in range(homes):
            moves += [(order[p] * 2 + c, order[(p + 1 - 2 * c) % homes] * 2 + c) for c in range(2)]
        return lax.ppermute(x, "blk", moves)

    def other_core(x):
        return lax.ppermute(x, "blk", [(b, b ^ 1) for b in range(blocks)])

    slices = after([lax.dynamic_slice_in_dim(x, rep * share, share) for x in (features, factors)])
    own = jnp.concatenate(scale(*slices), axis=1)
    first = ring(own)
    own, features, factors = after((own, features, factors))
    part = share // 2 if replicas <= 2 and share % 32 == 0 else count
    made = own_rows(rep_ref, replicas, features, factors, part)
    filled, parts = made[:2], made[2:]
    own_block = list(zip(parts[::2], parts[1::2], strict=True))
    parts = [other_core(x) for x in parts]
    if part < share:
        beside = [jnp.concatenate(parts[k - 2 * (share // part) :: 2]) for k in (0, 1)]
    else:
        beside = [x[part - share :] for x in parts[-2:]]
    second = ring(jnp.concatenate(beside, axis=1))
    feat, fac = other_rows(share, parts, filled)
    mine_at = 2 * share * (replicas - 1)

    full = (homes - 1) // 2
    total = 2 * full + (homes + 1) % 2
    cut = share // 2 if total > 2 and share % (2 * width) == 0 else 0
    flying, last = [first, second], []
    acc = None
    early = len(own_block) // 2
    mine = pairs(feat, fac, own_block[:early], None, mine_at, 2 * share) if early else None
    for step in range(total - 1):
        here, feat, fac, acc, mine = after((flying[step % 2], feat, fac, acc, mine))
        if step + 2 < total:
            if cut and step + 3 == total:
                last = [ring(here[:cut]), ring(here[cut:])]
            else:
                flying[step % 2] = ring(here)
        if step + 2 < total:
            acc = pairs(feat, fac, [here], acc)
        if step == 0:
            acc, mine = after((acc, mine))
            mine = pairs(feat, fac, own_block[early:], mine, mine_at, 2 * share, mine_at)
    if total < 2:
        mine = pairs(feat, fac, own_block[early:], mine, mine_at, 2 * share, mine_at)
    last = last or [flying[(total - 1) % 2]]
    late = [here, *last] if total > 1 else last

    theirs = acc
    for x in late[:-1] if mine_at else []:
        x, theirs = after((x, theirs))
        theirs = pairs(feat, fac, [x], theirs, 0, mine_at)
    end, theirs, acc = after((late[-1], theirs, acc))
    late = [*late[:-1], end]
    arrived = []
    for k in range(replicas - 1):
        at = k * 2 * share
        received = other_core(pairs(feat, fac, [end], theirs, at, share))
        part = pairs(feat, fac, [end], theirs, at + share, share) + received
        arrived.append(lax.ppermute(part, "rep", [(r, (r + k + 1) % replicas) for r in range(replicas)]))
        acc, part = after((acc, part))
    part = pairs(feat, fac, late, acc, mine_at, 2 * share, 0, mine)
    half = share // 2
    part = part[share:] + jnp.concatenate([other_core(part[:half]), other_core(part[half:share])])
    for x in arrived:
        part = part + x
    return part * (1.0 / (width * math.sqrt(math.log2(math.e) / width)))


def solution(mesh):
    placed = (P("blk", None), P("blk", None))
    return jax.shard_map(
        body, mesh=mesh, in_specs=placed, out_specs=P(("blk", "rep"), None), check_vma=False
    )
```

time: 57.6 us -> 57.3 us (level)
  starting transfers between devices: 15.8 us -> 19 us
  waiting for transfers between devices: 7.78 us -> 5.1 us
  local copies, waits for them, and re-layouts: 0.03 us -> 1.22 us
  other arithmetic: 2.14 us -> 1.13 us
  Pallas kernels: 31.5 us -> 30.5 us
    ppermute x7 -> x8, waiting for transfers between devices: 3.97 us -> 1.15 us  [ring(): return lax.ppermute(x, 'blk', moves)]
    ppermute x7 -> x8, starting transfers between devices: 12.3 us -> 14.4 us  [ring(): return lax.ppermute(x, 'blk', moves)]
    pallas_call x10 -> x12, Pallas kernels: 31 us -> 29.8 us  [call(): pl.pallas_call(kernel, in_specs=[IN_VMEM] * len(args), out_specs=jax.tree...]
    reduce_sum x1 -> x0, other arithmetic: 1.15 us -> none  [scale(): norm = jnp.sum(feat * feat, axis=1, keepdims=True)]
    dynamic_slice x0 -> x1, local copies, waits for them, and re-layouts: none -> 1.15 us  [body(): lax.dynamic_slice_in_dim(x, rep * share, share)]
    ppermute x7 -> x11, starting transfers between devices: 1.72 us -> 2.7 us  [other_core(): return lax.ppermute(x, 'blk', [(b, b ^ 1) for b in range(blocks)])]
    ppermute x7 -> x11, waiting for transfers between devices: 2.35 us -> 2.52 us  [other_core(): return lax.ppermute(x, 'blk', [(b, b ^ 1) for b in range(blocks)])]
  transfers between devices with their start and end apart: 15 -> 20, of which waited for: 8 -> 8; matrix products, arithmetic and copies ran while one was open for 0% -> 0% of each run, Pallas kernels for 53% -> 52%
where the time goes in v6:
time: 57.3 us; the launch traced here: 57.1 us
  Pallas kernels  30.5 us (53%)
  starting transfers between devices  19 us (33%)
  waiting for transfers between devices  5.1 us (9%)
  local copies, waits for them, and re-layouts  1.22 us (2%)
  other arithmetic  1.13 us (2%)
    pallas_call x12, Pallas kernels, call(): pl.pallas_call(kernel, in_specs=[IN_VMEM] * len(args), out_specs=jax.tree...  29.8 us
    ppermute x8, starting transfers between devices, ring(): return lax.ppermute(x, 'blk', moves)  14.4 us
    ppermute x11, starting transfers between devices, other_core(): return lax.ppermute(x, 'blk', [(b, b ^ 1) for b in range(blocks)])  2.7 us
    ppermute x11, waiting for transfers between devices, other_core(): return lax.ppermute(x, 'blk', [(b, b ^ 1) for b in range(blocks)])  2.52 us
    ppermute x1, starting transfers between devices, body(): lax.ppermute(part, 'rep', [(r, (r + k + 1) % replicas) for r in range(rep...  1.91 us
    ppermute x1, waiting for transfers between devices, body(): lax.ppermute(part, 'rep', [(r, (r + k + 1) % replicas) for r in range(rep...  1.42 us
    ppermute x8, waiting for transfers between devices, ring(): return lax.ppermute(x, 'blk', moves)  1.15 us
    dynamic_slice x1, local copies, waits for them, and re-layouts, body(): lax.dynamic_slice_in_dim(x, rep * share, share)  1.15 us
  transfers between devices with their start and end apart: 20, of which 8 were waited for; matrix products, arithmetic and copies ran while one was open for 0% of the time, Pallas kernels for 52%

profile of v6, /device:TPU:0, one launch (start us, length us, event | category | flops | bytes accessed | tf_op | source)
XLA Modules:
  0.0 57.1 jit_solution(18365873209672678307)
XLA Ops:
  0.0 1.2 %constant_dynamic-slice_fusion = (f32[512,128]{1,0:T(8,128)S(1)}, f32[512,128]{1,0:T(8,128)S(1)}) fusion(f32[1024,128]{1,0:T(8,128)} %fac_ref, s32[]{:T(128)S(6)} %select_n.4, f32[1024,128]{1,0:T(8,128)} %feat_ref), kind=kLoop, calls=%fused_computation.9 | loop fusion | bytes 1048580 | tf_op jit(solution)/shard_map/dynamic_slice | solution.py:215
  1.2 0.1 broadcast_multiply_fusion.1
  1.3 0.1 broadcast_multiply_fusion
  1.5 3.1 %collective-permute-start.5 = (f32[512,256]{1,0:T(8,128)S(1)}, f32[512,256]{1,0:T(8,128)S(1)}, u32[]{:S(2)}, u32[]{:S(2)}) collective-permute-start(f32[512,256]{1,0:T(8,128)S(1)} %pad_maximum_fusion), channel_id=1, source_target_pairs={{0,8},{2,6},{8,16},{10,2},{16,24},{18,10},{24,28},{26,18},{28,20},... | collective-permute-start | bytes 1572872 | tf_op jit(solution)/shard_map/ppermute | solution.py:210
  4.6 0.3 own_rows.1
  4.9 0.1 collective-permute-start
  5.0 0.5 collective-permute-start.1
  5.5 0.1 collective-permute-start.2
  5.6 0.4 collective-permute-start.3
  6.0 0.3 collective-permute-done.refs_4_
  6.3 0.1 collective-permute-start.6
  6.5 0.0 collective-permute-done.1.refs_6_
  6.5 0.3 collective-permute-start.7
  6.9 0.2 collective-permute-start.8
  7.1 0.0 collective-permute-done.3.refs_7_
  7.1 0.3 collective-permute-start.9
  7.4 0.3 collective-permute-done.6.refs_0_
  7.7 1.6 %collective-permute-start.4 = (f32[512,256]{1,0:T(8,128)S(1)}, f32[512,256]{1,0:T(8,128)S(1)}, u32[]{:S(2)}, u32[]{:S(2)}) collective-permute-start(f32[512,256]{1,0:T(8,128)S(1)} %maximum_maximum_fusion), channel_id=1, source_target_pairs={{0,8},{2,6},{8,16},{10,2},{16,24},{18,10},{24,28},{26,18},{28,20},... | collective-permute-start | bytes 1572872 | tf_op jit(solution)/shard_map/ppermute | solution.py:210
  9.3 0.3 other_rows.1
  9.6 1.9 %pair_terms.12.refs_6_ = f32[1024,128]{1,0:T(8,128)S(1)} custom-call(bf16[2048,512]{1,0:T(8,128)(2,1)S(1)} %get-tuple-element.102.refs_0_, bf16[2048,512]{1,0:T(8,128)(2,1)S(1)} %get-tuple-element.103.refs_1_, f32[256,128]{1,0:T(8,128)S(1)} %get-tuple-element.68.refs_2_, f32[256,128]{1,0:T(8,128)S(1)} %get-tuple-element.69.refs_3_, ...), custom_call_target="tpu_custom_call" | custom-call | flops 1610612736 | bytes 4194304 | tf_op jit(solution)/shard_map/pair_terms/pallas_call | solution.py:25
  11.5 0.2 collective-permute-done.5.refs_2_
  11.7 2.1 %collective-permute-start.11 = (f32[512,256]{1,0:T(8,128)S(1)}, f32[512,256]{1,0:T(8,128)S(1)}, u32[]{:S(2)}, u32[]{:S(2)}) collective-permute-start(f32[512,256]{1,0:T(8,128)S(1)} %collective-permute-done.5.refs_2_), channel_id=1, source_target_pairs={{0,8},{2,6},{8,16},{10,2},{16,24},{18,10},{24,28},{26,18},{28,20},... | collective-permute-start | bytes 1572872 | tf_op jit(solution)/shard_map/ppermute | solution.py:210
  13.8 3.5 %pair_terms.13.refs_3_ = f32[2048,128]{1,0:T(8,128)S(1)} custom-call(bf16[2048,512]{1,0:T(8,128)(2,1)S(1)} %get-tuple-element.102.refs_0_, bf16[2048,512]{1,0:T(8,128)(2,1)S(1)} %get-tuple-element.103.refs_1_, f32[512,256]{1,0:T(8,128)S(1)} %collective-permute-done.5.refs_2_), custom_call_target="tpu_custom_call" | custom-call | flops 3221225472 | bytes 4194304 | tf_op jit(solution)/shard_map/pair_terms/pallas_call | solution.py:25
  17.3 1.9 %pair_terms.14.refs_6_ = f32[1024,128]{1,0:T(8,128)S(1)} custom-call(bf16[2048,512]{1,0:T(8,128)(2,1)S(1)} %get-tuple-element.102.refs_0_, bf16[2048,512]{1,0:T(8,128)(2,1)S(1)} %get-tuple-element.103.refs_1_, f32[256,128]{1,0:T(8,128)S(1)} %get-tuple-element.64.refs_2_, f32[256,128]{1,0:T(8,128)S(1)} %get-tuple-element.66.refs_3_, ...), custom_call_target="tpu_custom_call", output_to_operand_aliasing={{}: (6, {})} | custom-call | flops 1610612736 | bytes 4194304 | tf_op jit(solution)/shard_map/pair_terms/pallas_call | solution.py:25
  19.3 1.8 %collective-permute-start.10 = (f32[512,256]{1,0:T(8,128)S(1)}, f32[512,256]{1,0:T(8,128)S(1)}, u32[]{:S(2)}, u32[]{:S(2)}) collective-permute-start(f32[512,256]{1,0:T(8,128)S(1)} %collective-permute-done.4.refs_2_), channel_id=1, source_target_pairs={{0,8},{2,6},{8,16},{10,2},{16,24},{18,10},{24,28},{26,18},{28,20},... | collective-permute-start | bytes 1572872 | tf_op jit(solution)/shard_map/ppermute | solution.py:210
  21.1 3.6 %pair_terms.15.refs_3_ = f32[2048,128]{1,0:T(8,128)S(1)} custom-call(bf16[2048,512]{1,0:T(8,128)(2,1)S(1)} %get-tuple-element.102.refs_0_, bf16[2048,512]{1,0:T(8,128)(2,1)S(1)} %get-tuple-element.103.refs_1_, f32[512,256]{1,0:T(8,128)S(1)} %collective-permute-done.4.refs_2_, f32[2048,128]{1,0:T(8,128)S(1)} %pair_terms.13.refs_3_), custom_call_target="tpu_custom_call", output_to_operand_aliasing={{}: (3, {})} | custom-call | flops 3221225472 | bytes 4194304 | tf_op jit(solution)/shard_map/pair_terms/pallas_call | solution.py:25
  24.7 1.6 %collective-permute-start.13 = (f32[512,256]{1,0:T(8,128)S(1)}, f32[512,256]{1,0:T(8,128)S(1)}, u32[]{:S(2)}, u32[]{:S(2)}) collective-permute-start(f32[512,256]{1,0:T(8,128)S(1)} %collective-permute-done.11.refs_2_), channel_id=1, source_target_pairs={{0,8},{2,6},{8,16},{10,2},{16,24},{18,10},{24,28},{26,18},{28,20},... | collective-permute-start | bytes 1572872 | tf_op jit(solution)/shard_map/ppermute | solution.py:210
  26.4 3.6 %pair_terms.16.refs_3_ = f32[2048,128]{1,0:T(8,128)S(1)} custom-call(bf16[2048,512]{1,0:T(8,128)(2,1)S(1)} %get-tuple-element.102.refs_0_, bf16[2048,512]{1,0:T(8,128)(2,1)S(1)} %get-tuple-element.103.refs_1_, f32[512,256]{1,0:T(8,128)S(1)} %collective-permute-done.11.refs_2_, f32[2048,128]{1,0:T(8,128)S(1)} %pair_terms.15.refs_3_), custom_call_target="tpu_custom_call", output_to_operand_aliasing={{}: (3, {})} | custom-call | flops 3221225472 | bytes 4194304 | tf_op jit(solution)/shard_map/pair_terms/pallas_call | solution.py:25
  30.0 1.6 %collective-permute-start.12 = (f32[512,256]{1,0:T(8,128)S(1)}, f32[512,256]{1,0:T(8,128)S(1)}, u32[]{:S(2)}, u32[]{:S(2)}) collective-permute-start(f32[512,256]{1,0:T(8,128)S(1)} %collective-permute-done.10.refs_2_), channel_id=1, source_target_pairs={{0,8},{2,6},{8,16},{10,2},{16,24},{18,10},{24,28},{26,18},{28,20},... | collective-permute-start | bytes 1572872 | tf_op jit(solution)/shard_map/ppermute | solution.py:210
  31.6 3.6 %pair_terms.17.refs_3_ = f32[2048,128]{1,0:T(8,128)S(1)} custom-call(bf16[2048,512]{1,0:T(8,128)(2,1)S(1)} %get-tuple-element.102.refs_0_, bf16[2048,512]{1,0:T(8,128)(2,1)S(1)} %get-tuple-element.103.refs_1_, f32[512,256]{1,0:T(8,128)S(1)} %collective-permute-done.10.refs_2_, f32[2048,128]{1,0:T(8,128)S(1)} %pair_terms.16.refs_3_), custom_call_target="tpu_custom_call", output_to_operand_aliasing={{}: (3, {})} | custom-call | flops 3221225472 | bytes 4194304 | tf_op jit(solution)/shard_map/pair_terms/pallas_call | solution.py:25
  35.3 1.1 %collective-permute-start.14 = (f32[256,256]{1,0:T(8,128)S(1)}, f32[256,256]{1,0:T(8,128)S(1)}, u32[]{:S(2)}, u32[]{:S(2)}) collective-permute-start(f32[256,256]{1,0:T(8,128)S(1)} %get-tuple-element.117), channel_id=1, source_target_pairs={{0,8},{2,6},{8,16},{10,2},{16,24},{18,10},{24,28},{26,18},{28,20},... | collective-permute-start | bytes 786440 | tf_op jit(solution)/shard_map/ppermute | solution.py:210
  36.3 1.6 %collective-permute-start.15 = (f32[256,256]{1,0:T(8,128)S(1)}, f32[256,256]{1,0:T(8,128)S(1)}, u32[]{:S(2)}, u32[]{:S(2)}) collective-permute-start(f32[256,256]{1,0:T(8,128)S(1)} %get-tuple-element.118), channel_id=1, source_target_pairs={{0,8},{2,6},{8,16},{10,2},{16,24},{18,10},{24,28},{26,18},{28,20},... | collective-permute-start | bytes 786440 | tf_op jit(solution)/shard_map/ppermute | solution.py:210
  37.9 3.6 %pair_terms.18.refs_3_.refs_5_ = f32[2048,128]{1,0:T(8,128)S(1)} custom-call(bf16[2048,512]{1,0:T(8,128)(2,1)S(1)} %get-tuple-element.102.refs_0_, bf16[2048,512]{1,0:T(8,128)(2,1)S(1)} %get-tuple-element.103.refs_1_, f32[512,256]{1,0:T(8,128)S(1)} %collective-permute-done.13.refs_2_, f32[2048,128]{1,0:T(8,128)S(1)} %pair_terms.17.refs_3_), custom_call_target="tpu_custom_call", output_to_operand_aliasing={{}: (3, {})} | custom-call | flops 3221225472 | bytes 4194304 | tf_op jit(solution)/shard_map/pair_terms/pallas_call | solution.py:25
  41.6 1.9 %pair_terms.19.refs_3_ = f32[1024,128]{1,0:T(8,128)S(1)} custom-call(bf16[2048,512]{1,0:T(8,128)(2,1)S(1)} %get-tuple-element.102.refs_0_, bf16[2048,512]{1,0:T(8,128)(2,1)S(1)} %get-tuple-element.103.refs_1_, f32[512,256]{1,0:T(8,128)S(1)} %collective-permute-done.12.refs_2_, f32[2048,128]{1,0:T(8,128)S(1)} %pair_terms.18.refs_3_.refs_5_), custom_call_target="tpu_custom_call" | custom-call | flops 1610612736 | bytes 4194304 | tf_op jit(solution)/shard_map/pair_terms/pallas_call | solution.py:25
  43.5 1.1 %pair_terms.20.refs_3_ = f32[1024,128]{1,0:T(8,128)S(1)} custom-call(bf16[2048,512]{1,0:T(8,128)(2,1)S(1)} %get-tuple-element.102.refs_0_, bf16[2048,512]{1,0:T(8,128)(2,1)S(1)} %get-tuple-element.103.refs_1_, f32[256,256]{1,0:T(8,128)S(1)} %collective-permute-done.14.refs_2_.refs_3_, f32[1024,128]{1,0:T(8,128)S(1)} %pair_terms.19.refs_3_), custom_call_target="tpu_custom_call", output_to_operand_aliasing={{}: (3, {})} | custom-call | flops 805306368 | bytes 4194304 | tf_op jit(solution)/shard_map/pair_terms/pallas_call | solution.py:25
  44.6 0.9 %collective-permute-done.15.refs_2_.refs_4_ = f32[256,256]{1,0:T(8,128)S(1)} collective-permute-done((f32[256,256]{1,0:T(8,128)S(1)}, f32[256,256]{1,0:T(8,128)S(1)}, u32[]{:S(2)}, u32[]{:S(2)}) %collective-permute-start.15) | collective-permute-done | bytes 262176 | tf_op jit(solution)/shard_map/ppermute | solution.py:210
  45.5 0.7 %pair_terms.22 = f32[512,128]{1,0:T(8,128)S(1)} custom-call(bf16[2048,512]{1,0:T(8,128)(2,1)S(1)} %get-tuple-element.102.refs_0_, bf16[2048,512]{1,0:T(8,128)(2,1)S(1)} %get-tuple-element.103.refs_1_, f32[256,256]{1,0:T(8,128)S(1)} %collective-permute-done.15.refs_2_.refs_4_, f32[1024,128]{1,0:T(8,128)S(1)} %pair_terms.20.refs_3_), custom_call_target="tpu_custom_call" | custom-call | flops 402653184 | bytes 4194304 | tf_op jit(solution)/shard_map/pair_terms/pallas_call | solution.py:25
  46.2 0.1 collective-permute-start.16
  46.3 0.7 %pair_terms.21 = f32[512,128]{1,0:T(8,128)S(1)} custom-call(bf16[2048,512]{1,0:T(8,128)(2,1)S(1)} %get-tuple-element.102.refs_0_, bf16[2048,512]{1,0:T(8,128)(2,1)S(1)} %get-tuple-element.103.refs_1_, f32[256,256]{1,0:T(8,128)S(1)} %collective-permute-done.15.refs_2_.refs_4_, f32[1024,128]{1,0:T(8,128)S(1)} %pair_terms.20.refs_3_), custom_call_target="tpu_custom_call" | custom-call | flops 402653184 | bytes 4194304 | tf_op jit(solution)/shard_map/pair_terms/pallas_call | solution.py:25
  47.0 0.8 %collective-permute-done.16 = f32[512,128]{1,0:T(8,128)S(1)} collective-permute-done((f32[512,128]{1,0:T(8,128)S(1)}, f32[512,128]{1,0:T(8,128)S(1)}, u32[]{:S(2)}, u32[]{:S(2)}) %collective-permute-start.16) | collective-permute-done | bytes 262176 | tf_op jit(solution)/shard_map/ppermute | solution.py:213
  47.9 1.9 %collective-permute-start.19 = (f32[512,128]{1,0:T(8,128)S(1)}, f32[512,128]{1,0:T(8,128)S(1)}, u32[]{:S(2)}, u32[]{:S(2)}) collective-permute-start(f32[512,128]{1,0:T(8,128)S(1)} %add.14), channel_id=1, source_target_pairs={{0,1},{1,0},{2,3},{3,2},{4,5},{5,4},{6,7},{7,6},{8,9},{9,8},{10,11... | collective-permute-start | bytes 786440 | tf_op jit(solution)/shard_map/ppermute | solution.py:267
  49.8 3.5 %pair_terms.23 = f32[1024,128]{1,0:T(8,128)S(1)} custom-call(bf16[2048,512]{1,0:T(8,128)(2,1)S(1)} %get-tuple-element.102.refs_0_, bf16[2048,512]{1,0:T(8,128)(2,1)S(1)} %get-tuple-element.103.refs_1_, f32[512,256]{1,0:T(8,128)S(1)} %collective-permute-done.12.refs_2_, f32[256,256]{1,0:T(8,128)S(1)} %collective-permute-done.14.refs_2_.refs_3_, ...), custom_call_target="tpu_custom_call" | custom-call | flops 3221225472 | bytes 4194304 | tf_op jit(solution)/shard_map/pair_terms/pallas_call | solution.py:25
  53.3 0.1 collective-permute-start.17
  53.4 0.5 collective-permute-start.18
  53.9 0.8 %collective-permute-done.17 = f32[256,128]{1,0:T(8,128)S(1)} collective-permute-done((f32[256,128]{1,0:T(8,128)S(1)}, f32[256,128]{1,0:T(8,128)S(1)}, u32[]{:S(2)}, u32[]{:S(2)}) %collective-permute-start.17) | collective-permute-done | bytes 131104 | tf_op jit(solution)/shard_map/ppermute | solution.py:213
  54.8 0.2 collective-permute-done.18
  54.9 1.4 %collective-permute-done.19 = f32[512,128]{1,0:T(8,128)S(1)} collective-permute-done((f32[512,128]{1,0:T(8,128)S(1)}, f32[512,128]{1,0:T(8,128)S(1)}, u32[]{:S(2)}, u32[]{:S(2)}) %collective-permute-start.19) | collective-permute-done | bytes 262176 | tf_op jit(solution)/shard_map/ppermute | solution.py:267
  56.4 0.7 %fusion.1 = f32[512,128]{1,0:T(8,128)} fusion(f32[512,128]{1,0:T(8,128)S(1)} %collective-permute-done.19, f32[1024,128]{1,0:T(8,128)S(1)} %pair_terms.23, f32[256,128]{1,0:T(8,128)S(1)} %collective-permute-done.18, f32[256,128]{1,0:T(8,128)S(1)} %collective-permute-done.17), kind=kLoop, calls=%fused_computation.4 | loop fusion | flops 262144 | bytes 1048576 | tf_op jit(solution)/shard_map/mul | solution.py:274
  (20 shorter events, 0.2 us)
Async XLA Ops:
  0.0 4.6 %copy-start.1 = (f32[1024,128]{1,0:T(8,128)S(1)}, f32[1024,128]{1,0:T(8,128)}, u32[]{:S(2)}) copy-start(f32[1024,128]{1,0:T(8,128)} %fac_ref) | copy-start | bytes 1572868
  0.0 4.6 %copy-start = (f32[1024,128]{1,0:T(8,128)S(1)}, f32[1024,128]{1,0:T(8,128)}, u32[]{:S(2)}) copy-start(f32[1024,128]{1,0:T(8,128)} %feat_ref) | copy-start | bytes 1572868
  1.5 10.2 %collective-permute-start.5 = (f32[512,256]{1,0:T(8,128)S(1)}, f32[512,256]{1,0:T(8,128)S(1)}, u32[]{:S(2)}, u32[]{:S(2)}) collective-permute-start(f32[512,256]{1,0:T(8,128)S(1)} %pad_maximum_fusion), channel_id=1, source_target_pairs={{0,8},{2,6},{8,16},{10,2},{16,24},{18,10},{24,28},{26,18},{28,20},... | collective-permute-start | bytes 1572872 | tf_op jit(solution)/shard_map/ppermute | solution.py:210
  4.9 1.4 %collective-permute-start = (f32[256,128]{1,0:T(8,128)S(1)}, f32[256,128]{1,0:T(8,128)S(1)}, u32[]{:S(2)}, u32[]{:S(2)}) collective-permute-start(f32[256,128]{1,0:T(8,128)S(1)} %get-tuple-element.64.refs_2_), channel_id=1, source_target_pairs={{0,2},{2,0},{4,6},{6,4},{8,10},{10,8},{12,14},{14,12},{16,18},{18,... | collective-permute-start | bytes 393224 | tf_op jit(solution)/shard_map/ppermute | solution.py:213
  5.0 1.5 %collective-permute-start.1 = (f32[256,128]{1,0:T(8,128)S(1)}, f32[256,128]{1,0:T(8,128)S(1)}, u32[]{:S(2)}, u32[]{:S(2)}) collective-permute-start(f32[256,128]{1,0:T(8,128)S(1)} %get-tuple-element.65.refs_4_), channel_id=1, source_target_pairs={{0,2},{2,0},{4,6},{6,4},{8,10},{10,8},{12,14},{14,12},{16,18},{18,... | collective-permute-start | bytes 393224 | tf_op jit(solution)/shard_map/ppermute | solution.py:213
  5.5 1.4 %collective-permute-start.2 = (f32[256,128]{1,0:T(8,128)S(1)}, f32[256,128]{1,0:T(8,128)S(1)}, u32[]{:S(2)}, u32[]{:S(2)}) collective-permute-start(f32[256,128]{1,0:T(8,128)S(1)} %get-tuple-element.66.refs_3_), channel_id=1, source_target_pairs={{0,2},{2,0},{4,6},{6,4},{8,10},{10,8},{12,14},{14,12},{16,18},{18,... | collective-permute-start | bytes 393224 | tf_op jit(solution)/shard_map/ppermute | solution.py:213
  5.6 1.5 %collective-permute-start.3 = (f32[256,128]{1,0:T(8,128)S(1)}, f32[256,128]{1,0:T(8,128)S(1)}, u32[]{:S(2)}, u32[]{:S(2)}) collective-permute-start(f32[256,128]{1,0:T(8,128)S(1)} %get-tuple-element.67.refs_5_), channel_id=1, source_target_pairs={{0,2},{2,0},{4,6},{6,4},{8,10},{10,8},{12,14},{14,12},{16,18},{18,... | collective-permute-start | bytes 393224 | tf_op jit(solution)/shard_map/ppermute | solution.py:213
  6.3 1.3 %collective-permute-start.6 = (f32[256,128]{1,0:T(8,128)S(1)}, f32[256,128]{1,0:T(8,128)S(1)}, u32[]{:S(2)}, u32[]{:S(2)}) collective-permute-start(f32[256,128]{1,0:T(8,128)S(1)} %get-tuple-element.68.refs_2_), channel_id=1, source_target_pairs={{0,2},{2,0},{4,6},{6,4},{8,10},{10,8},{12,14},{14,12},{16,18},{18,... | collective-permute-start | bytes 393224 | tf_op jit(solution)/shard_map/ppermute | solution.py:213
  6.5 2.7 %collective-permute-start.7 = (f32[256,128]{1,0:T(8,128)S(1)}, f32[256,128]{1,0:T(8,128)S(1)}, u32[]{:S(2)}, u32[]{:S(2)}) collective-permute-start(f32[256,128]{1,0:T(8,128)S(1)} %get-tuple-element.69.refs_3_), channel_id=1, source_target_pairs={{0,2},{2,0},{4,6},{6,4},{8,10},{10,8},{12,14},{14,12},{16,18},{18,... | collective-permute-start | bytes 393224 | tf_op jit(solution)/shard_map/ppermute | solution.py:213
  6.9 2.4 %collective-permute-start.8 = (f32[256,128]{1,0:T(8,128)S(1)}, f32[256,128]{1,0:T(8,128)S(1)}, u32[]{:S(2)}, u32[]{:S(2)}) collective-permute-start(f32[256,128]{1,0:T(8,128)S(1)} %get-tuple-element.70.refs_4_), channel_id=1, source_target_pairs={{0,2},{2,0},{4,6},{6,4},{8,10},{10,8},{12,14},{14,12},{16,18},{18,... | collective-permute-start | bytes 393224 | tf_op jit(solution)/shard_map/ppermute | solution.py:213
  7.1 2.2 %collective-permute-start.9 = (f32[256,128]{1,0:T(8,128)S(1)}, f32[256,128]{1,0:T(8,128)S(1)}, u32[]{:S(2)}, u32[]{:S(2)}) collective-permute-start(f32[256,128]{1,0:T(8,128)S(1)} %get-tuple-element.71.refs_5_), channel_id=1, source_target_pairs={{0,2},{2,0},{4,6},{6,4},{8,10},{10,8},{12,14},{14,12},{16,18},{18,... | collective-permute-start | bytes 393224 | tf_op jit(solution)/shard_map/ppermute | solution.py:213
  7.7 11.6 %collective-permute-start.4 = (f32[512,256]{1,0:T(8,128)S(1)}, f32[512,256]{1,0:T(8,128)S(1)}, u32[]{:S(2)}, u32[]{:S(2)}) collective-permute-start(f32[512,256]{1,0:T(8,128)S(1)} %maximum_maximum_fusion), channel_id=1, source_target_pairs={{0,8},{2,6},{8,16},{10,2},{16,24},{18,10},{24,28},{26,18},{28,20},... | collective-permute-start | bytes 1572872 | tf_op jit(solution)/shard_map/ppermute | solution.py:210
  11.7 13.0 %collective-permute-start.11 = (f32[512,256]{1,0:T(8,128)S(1)}, f32[512,256]{1,0:T(8,128)S(1)}, u32[]{:S(2)}, u32[]{:S(2)}) collective-permute-start(f32[512,256]{1,0:T(8,128)S(1)} %collective-permute-done.5.refs_2_), channel_id=1, source_target_pairs={{0,8},{2,6},{8,16},{10,2},{16,24},{18,10},{24,28},{26,18},{28,20},... | collective-permute-start | bytes 1572872 | tf_op jit(solution)/shard_map/ppermute | solution.py:210
  19.3 10.7 %collective-permute-start.10 = (f32[512,256]{1,0:T(8,128)S(1)}, f32[512,256]{1,0:T(8,128)S(1)}, u32[]{:S(2)}, u32[]{:S(2)}) collective-permute-start(f32[512,256]{1,0:T(8,128)S(1)} %collective-permute-done.4.refs_2_), channel_id=1, source_target_pairs={{0,8},{2,6},{8,16},{10,2},{16,24},{18,10},{24,28},{26,18},{28,20},... | collective-permute-start | bytes 1572872 | tf_op jit(solution)/shard_map/ppermute | solution.py:210
  24.7 10.5 %collective-permute-start.13 = (f32[512,256]{1,0:T(8,128)S(1)}, f32[512,256]{1,0:T(8,128)S(1)}, u32[]{:S(2)}, u32[]{:S(2)}) collective-permute-start(f32[512,256]{1,0:T(8,128)S(1)} %collective-permute-done.11.refs_2_), channel_id=1, source_target_pairs={{0,8},{2,6},{8,16},{10,2},{16,24},{18,10},{24,28},{26,18},{28,20},... | collective-permute-start | bytes 1572872 | tf_op jit(solution)/shard_map/ppermute | solution.py:210
  30.0 11.5 %collective-permute-start.12 = (f32[512,256]{1,0:T(8,128)S(1)}, f32[512,256]{1,0:T(8,128)S(1)}, u32[]{:S(2)}, u32[]{:S(2)}) collective-permute-start(f32[512,256]{1,0:T(8,128)S(1)} %collective-permute-done.10.refs_2_), channel_id=1, source_target_pairs={{0,8},{2,6},{8,16},{10,2},{16,24},{18,10},{24,28},{26,18},{28,20},... | collective-permute-start | bytes 1572872 | tf_op jit(solution)/shard_map/ppermute | solution.py:210
  35.3 8.2 %collective-permute-start.14 = (f32[256,256]{1,0:T(8,128)S(1)}, f32[256,256]{1,0:T(8,128)S(1)}, u32[]{:S(2)}, u32[]{:S(2)}) collective-permute-start(f32[256,256]{1,0:T(8,128)S(1)} %get-tuple-element.117), channel_id=1, source_target_pairs={{0,8},{2,6},{8,16},{10,2},{16,24},{18,10},{24,28},{26,18},{28,20},... | collective-permute-start | bytes 786440 | tf_op jit(solution)/shard_map/ppermute | solution.py:210
  36.3 9.2 %collective-permute-start.15 = (f32[256,256]{1,0:T(8,128)S(1)}, f32[256,256]{1,0:T(8,128)S(1)}, u32[]{:S(2)}, u32[]{:S(2)}) collective-permute-start(f32[256,256]{1,0:T(8,128)S(1)} %get-tuple-element.118), channel_id=1, source_target_pairs={{0,8},{2,6},{8,16},{10,2},{16,24},{18,10},{24,28},{26,18},{28,20},... | collective-permute-start | bytes 786440 | tf_op jit(solution)/shard_map/ppermute | solution.py:210
  46.2 1.6 %collective-permute-start.16 = (f32[512,128]{1,0:T(8,128)S(1)}, f32[512,128]{1,0:T(8,128)S(1)}, u32[]{:S(2)}, u32[]{:S(2)}) collective-permute-start(f32[512,128]{1,0:T(8,128)S(1)} %pair_terms.22), channel_id=1, source_target_pairs={{0,2},{2,0},{4,6},{6,4},{8,10},{10,8},{12,14},{14,12},{16,18},{18,... | collective-permute-start | bytes 786440 | tf_op jit(solution)/shard_map/ppermute | solution.py:213
  47.9 8.5 %collective-permute-start.19 = (f32[512,128]{1,0:T(8,128)S(1)}, f32[512,128]{1,0:T(8,128)S(1)}, u32[]{:S(2)}, u32[]{:S(2)}) collective-permute-start(f32[512,128]{1,0:T(8,128)S(1)} %add.14), channel_id=1, source_target_pairs={{0,1},{1,0},{2,3},{3,2},{4,5},{5,4},{6,7},{7,6},{8,9},{9,8},{10,11... | collective-permute-start | bytes 786440 | tf_op jit(solution)/shard_map/ppermute | solution.py:267
  53.3 1.4 %collective-permute-start.17 = (f32[256,128]{1,0:T(8,128)S(1)}, f32[256,128]{1,0:T(8,128)S(1)}, u32[]{:S(2)}, u32[]{:S(2)}) collective-permute-start(f32[256,128]{1,0:T(8,128)S(1)} %get-tuple-element.115), channel_id=1, source_target_pairs={{0,2},{2,0},{4,6},{6,4},{8,10},{10,8},{12,14},{14,12},{16,18},{18,... | collective-permute-start | bytes 393224 | tf_op jit(solution)/shard_map/ppermute | solution.py:213
  53.4 1.5 %collective-permute-start.18 = (f32[256,128]{1,0:T(8,128)S(1)}, f32[256,128]{1,0:T(8,128)S(1)}, u32[]{:S(2)}, u32[]{:S(2)}) collective-permute-start(f32[256,128]{1,0:T(8,128)S(1)} %get-tuple-element.116), channel_id=1, source_target_pairs={{0,2},{2,0},{4,6},{6,4},{8,10},{10,8},{12,14},{14,12},{16,18},{18,... | collective-permute-start | bytes 393224 | tf_op jit(solution)/shard_map/ppermute | solution.py:213

commit v7 on v6

--- a/solution.py
+++ b/solution.py
@@ -212,8 +212,11 @@
     def other_core(x):
         return lax.ppermute(x, "blk", [(b, b ^ 1) for b in range(blocks)])
 
+    def scaled(x):
+        return jnp.concatenate(scale(x[:, :width], x[:, width:]), axis=1)
+
     slices = after([lax.dynamic_slice_in_dim(x, rep * share, share) for x in (features, factors)])
-    own = jnp.concatenate(scale(*slices), axis=1)
+    own = jnp.concatenate(slices, axis=1)
     first = ring(own)
     own, features, factors = after((own, features, factors))
     part = share // 2 if replicas <= 2 and share % 32 == 0 else count
@@ -238,6 +241,8 @@
     mine = pairs(feat, fac, own_block[:early], None, mine_at, 2 * share) if early else None
     for step in range(total - 1):
         here, feat, fac, acc, mine = after((flying[step % 2], feat, fac, acc, mine))
+        if step == 0:
+            here = scaled(here)
         if step + 2 < total:
             if cut and step + 3 == total:
                 last = [ring(here[:cut]), ring(here[cut:])]
@@ -250,7 +255,7 @@
             mine = pairs(feat, fac, own_block[early:], mine, mine_at, 2 * share, mine_at)
     if total < 2:
         mine = pairs(feat, fac, own_block[early:], mine, mine_at, 2 * share, mine_at)
-    last = last or [flying[(total - 1) % 2]]
+    last = last or [flying[(total - 1) % 2] if total > 1 else scaled(first)]
     late = [here, *last] if total > 1 else last
 
     theirs = acc

time: 57.3 us -> 57.3 us (level)
  starting transfers between devices: 19 us -> 18.3 us
  waiting for transfers between devices: 5.1 us -> 5.7 us
  transfers between devices with their start and end apart: 20 -> 20, of which waited for: 8 -> 8; matrix products, arithmetic and copies ran while one was open for 0% -> 1% of each run, Pallas kernels for 52% -> 52%
where the time goes in v7:
time: 57.3 us; the launch traced here: 57.1 us
  Pallas kernels  30.5 us (53%)
  starting transfers between devices  18.3 us (32%)
  waiting for transfers between devices  5.7 us (10%)
  local copies, waits for them, and re-layouts  1.25 us (2%)
  other arithmetic  1.13 us (2%)
    pallas_call x12, Pallas kernels, call(): pl.pallas_call(kernel, in_specs=[IN_VMEM] * len(args), out_specs=jax.tree...  29.8 us
    ppermute x8, starting transfers between devices, ring(): return lax.ppermute(x, 'blk', moves)  14.1 us
    ppermute x11, starting transfers between devices, other_core(): return lax.ppermute(x, 'blk', [(b, b ^ 1) for b in range(blocks)])  2.7 us
    ppermute x11, waiting for transfers between devices, other_core(): return lax.ppermute(x, 'blk', [(b, b ^ 1) for b in range(blocks)])  2.52 us
    ppermute x1, waiting for transfers between devices, body(): lax.ppermute(part, 'rep', [(r, (r + k + 1) % replicas) for r in range(rep...  1.67 us
    ppermute x1, starting transfers between devices, body(): lax.ppermute(part, 'rep', [(r, (r + k + 1) % replicas) for r in range(rep...  1.55 us
    ppermute x8, waiting for transfers between devices, ring(): return lax.ppermute(x, 'blk', moves)  1.51 us
    dynamic_slice x1, local copies, waits for them, and re-layouts, body(): lax.dynamic_slice_in_dim(x, rep * share, share)  1.15 us
  transfers between devices with their start and end apart: 20, of which 8 were waited for; matrix products, arithmetic and copies ran while one was open for 1% of the time, Pallas kernels for 52%

profile of v7, /device:TPU:0, one launch (start us, length us, event | category | flops | bytes accessed | tf_op | source)
XLA Modules:
  0.0 57.1 jit_solution(10317726973781364760)
XLA Ops:
  0.0 1.2 %constant_dynamic-slice_fusion = (f32[512,128]{1,0:T(8,128)S(1)}, f32[512,128]{1,0:T(8,128)S(1)}) fusion(f32[1024,128]{1,0:T(8,128)} %fac_ref, s32[]{:T(128)S(6)} %select_n.4, f32[1024,128]{1,0:T(8,128)} %feat_ref), kind=kLoop, calls=%fused_computation.11 | loop fusion | bytes 1048580 | tf_op jit(solution)/shard_map/dynamic_slice | solution.py:218
  1.2 3.1 %collective-permute-start.5 = (f32[512,256]{1,0:T(8,128)S(1)}, f32[512,256]{1,0:T(8,128)S(1)}, u32[]{:S(2)}, u32[]{:S(2)}) collective-permute-start(f32[512,256]{1,0:T(8,128)S(1)} %constant_dynamic-update-slice_fusion), channel_id=1, source_target_pairs={{0,8},{2,6},{8,16},{10,2},{16,24},{18,10},{24,28},{26,18},{28,20},... | collective-permute-start | bytes 1572872 | tf_op jit(solution)/shard_map/ppermute | solution.py:210
  4.3 0.3 own_rows.1
  4.6 0.1 collective-permute-start
  4.7 0.5 collective-permute-start.1
  5.2 0.1 collective-permute-start.2
  5.3 0.4 collective-permute-start.3
  5.7 0.3 collective-permute-done.refs_4_
  6.1 0.1 collective-permute-start.6
  6.2 0.0 collective-permute-done.1.refs_6_
  6.2 0.3 collective-permute-start.7
  6.6 0.2 collective-permute-start.8
  6.8 0.0 collective-permute-done.3.refs_7_
  6.8 0.3 collective-permute-start.9
  7.1 0.3 collective-permute-done.6.refs_0_
  7.4 1.6 %collective-permute-start.4 = (f32[512,256]{1,0:T(8,128)S(1)}, f32[512,256]{1,0:T(8,128)S(1)}, u32[]{:S(2)}, u32[]{:S(2)}) collective-permute-start(f32[512,256]{1,0:T(8,128)S(1)} %maximum_maximum_fusion), channel_id=1, source_target_pairs={{0,8},{2,6},{8,16},{10,2},{16,24},{18,10},{24,28},{26,18},{28,20},... | collective-permute-start | bytes 1572872 | tf_op jit(solution)/shard_map/ppermute | solution.py:210
  9.0 0.3 other_rows.1
  9.3 1.9 %pair_terms.12.refs_6_ = f32[1024,128]{1,0:T(8,128)S(1)} custom-call(bf16[2048,512]{1,0:T(8,128)(2,1)S(1)} %get-tuple-element.102.refs_0_, bf16[2048,512]{1,0:T(8,128)(2,1)S(1)} %get-tuple-element.103.refs_1_, f32[256,128]{1,0:T(8,128)S(1)} %get-tuple-element.68.refs_2_, f32[256,128]{1,0:T(8,128)S(1)} %get-tuple-element.69.refs_3_, ...), custom_call_target="tpu_custom_call" | custom-call | flops 1610612736 | bytes 4194304 | tf_op jit(solution)/shard_map/pair_terms/pallas_call | solution.py:25
  11.2 0.2 collective-permute-done.5
  11.4 0.1 slice_multiply_fusion.1
  11.6 0.1 slice_multiply_fusion
  11.7 2.1 %collective-permute-start.11 = (f32[512,256]{1,0:T(8,128)S(1)}, f32[512,256]{1,0:T(8,128)S(1)}, u32[]{:S(2)}, u32[]{:S(2)}) collective-permute-start(f32[512,256]{1,0:T(8,128)S(1)} %pad_maximum_fusion.refs_2_), channel_id=1, source_target_pairs={{0,8},{2,6},{8,16},{10,2},{16,24},{18,10},{24,28},{26,18},{28,20},... | collective-permute-start | bytes 1572872 | tf_op jit(solution)/shard_map/ppermute | solution.py:210
  13.9 3.5 %pair_terms.13.refs_3_ = f32[2048,128]{1,0:T(8,128)S(1)} custom-call(bf16[2048,512]{1,0:T(8,128)(2,1)S(1)} %get-tuple-element.102.refs_0_, bf16[2048,512]{1,0:T(8,128)(2,1)S(1)} %get-tuple-element.103.refs_1_, f32[512,256]{1,0:T(8,128)S(1)} %pad_maximum_fusion.refs_2_), custom_call_target="tpu_custom_call" | custom-call | flops 3221225472 | bytes 4194304 | tf_op jit(solution)/shard_map/pair_terms/pallas_call | solution.py:25
  17.4 1.9 %pair_terms.14.refs_6_ = f32[1024,128]{1,0:T(8,128)S(1)} custom-call(bf16[2048,512]{1,0:T(8,128)(2,1)S(1)} %get-tuple-element.102.refs_0_, bf16[2048,512]{1,0:T(8,128)(2,1)S(1)} %get-tuple-element.103.refs_1_, f32[256,128]{1,0:T(8,128)S(1)} %get-tuple-element.64.refs_2_, f32[256,128]{1,0:T(8,128)S(1)} %get-tuple-element.66.refs_3_, ...), custom_call_target="tpu_custom_call", output_to_operand_aliasing={{}: (6, {})} | custom-call | flops 1610612736 | bytes 4194304 | tf_op jit(solution)/shard_map/pair_terms/pallas_call | solution.py:25
  19.4 1.8 %collective-permute-start.10 = (f32[512,256]{1,0:T(8,128)S(1)}, f32[512,256]{1,0:T(8,128)S(1)}, u32[]{:S(2)}, u32[]{:S(2)}) collective-permute-start(f32[512,256]{1,0:T(8,128)S(1)} %collective-permute-done.4.refs_2_), channel_id=1, source_target_pairs={{0,8},{2,6},{8,16},{10,2},{16,24},{18,10},{24,28},{26,18},{28,20},... | collective-permute-start | bytes 1572872 | tf_op jit(solution)/shard_map/ppermute | solution.py:210
  21.2 3.6 %pair_terms.15.refs_3_ = f32[2048,128]{1,0:T(8,128)S(1)} custom-call(bf16[2048,512]{1,0:T(8,128)(2,1)S(1)} %get-tuple-element.102.refs_0_, bf16[2048,512]{1,0:T(8,128)(2,1)S(1)} %get-tuple-element.103.refs_1_, f32[512,256]{1,0:T(8,128)S(1)} %collective-permute-done.4.refs_2_, f32[2048,128]{1,0:T(8,128)S(1)} %pair_terms.13.refs_3_), custom_call_target="tpu_custom_call", output_to_operand_aliasing={{}: (3, {})} | custom-call | flops 3221225472 | bytes 4194304 | tf_op jit(solution)/shard_map/pair_terms/pallas_call | solution.py:25
  24.8 1.6 %collective-permute-start.13 = (f32[512,256]{1,0:T(8,128)S(1)}, f32[512,256]{1,0:T(8,128)S(1)}, u32[]{:S(2)}, u32[]{:S(2)}) collective-permute-start(f32[512,256]{1,0:T(8,128)S(1)} %collective-permute-done.11.refs_2_), channel_id=1, source_target_pairs={{0,8},{2,6},{8,16},{10,2},{16,24},{18,10},{24,28},{26,18},{28,20},... | collective-permute-start | bytes 1572872 | tf_op jit(solution)/shard_map/ppermute | solution.py:210
  26.5 3.6 %pair_terms.16.refs_3_ = f32[2048,128]{1,0:T(8,128)S(1)} custom-call(bf16[2048,512]{1,0:T(8,128)(2,1)S(1)} %get-tuple-element.102.refs_0_, bf16[2048,512]{1,0:T(8,128)(2,1)S(1)} %get-tuple-element.103.refs_1_, f32[512,256]{1,0:T(8,128)S(1)} %collective-permute-done.11.refs_2_, f32[2048,128]{1,0:T(8,128)S(1)} %pair_terms.15.refs_3_), custom_call_target="tpu_custom_call", output_to_operand_aliasing={{}: (3, {})} | custom-call | flops 3221225472 | bytes 4194304 | tf_op jit(solution)/shard_map/pair_terms/pallas_call | solution.py:25
  30.1 1.6 %collective-permute-start.12 = (f32[512,256]{1,0:T(8,128)S(1)}, f32[512,256]{1,0:T(8,128)S(1)}, u32[]{:S(2)}, u32[]{:S(2)}) collective-permute-start(f32[512,256]{1,0:T(8,128)S(1)} %collective-permute-done.10.refs_2_), channel_id=1, source_target_pairs={{0,8},{2,6},{8,16},{10,2},{16,24},{18,10},{24,28},{26,18},{28,20},... | collective-permute-start | bytes 1572872 | tf_op jit(solution)/shard_map/ppermute | solution.py:210
  31.7 3.6 %pair_terms.17.refs_3_ = f32[2048,128]{1,0:T(8,128)S(1)} custom-call(bf16[2048,512]{1,0:T(8,128)(2,1)S(1)} %get-tuple-element.102.refs_0_, bf16[2048,512]{1,0:T(8,128)(2,1)S(1)} %get-tuple-element.103.refs_1_, f32[512,256]{1,0:T(8,128)S(1)} %collective-permute-done.10.refs_2_, f32[2048,128]{1,0:T(8,128)S(1)} %pair_terms.16.refs_3_), custom_call_target="tpu_custom_call", output_to_operand_aliasing={{}: (3, {})} | custom-call | flops 3221225472 | bytes 4194304 | tf_op jit(solution)/shard_map/pair_terms/pallas_call | solution.py:25
  35.4 0.7 %collective-permute-start.14 = (f32[256,256]{1,0:T(8,128)S(1)}, f32[256,256]{1,0:T(8,128)S(1)}, u32[]{:S(2)}, u32[]{:S(2)}) collective-permute-start(f32[256,256]{1,0:T(8,128)S(1)} %get-tuple-element.117), channel_id=1, source_target_pairs={{0,8},{2,6},{8,16},{10,2},{16,24},{18,10},{24,28},{26,18},{28,20},... | collective-permute-start | bytes 786440 | tf_op jit(solution)/shard_map/ppermute | solution.py:210
  36.1 1.6 %collective-permute-start.15 = (f32[256,256]{1,0:T(8,128)S(1)}, f32[256,256]{1,0:T(8,128)S(1)}, u32[]{:S(2)}, u32[]{:S(2)}) collective-permute-start(f32[256,256]{1,0:T(8,128)S(1)} %get-tuple-element.118), channel_id=1, source_target_pairs={{0,8},{2,6},{8,16},{10,2},{16,24},{18,10},{24,28},{26,18},{28,20},... | collective-permute-start | bytes 786440 | tf_op jit(solution)/shard_map/ppermute | solution.py:210
  37.7 3.6 %pair_terms.18.refs_3_.refs_5_ = f32[2048,128]{1,0:T(8,128)S(1)} custom-call(bf16[2048,512]{1,0:T(8,128)(2,1)S(1)} %get-tuple-element.102.refs_0_, bf16[2048,512]{1,0:T(8,128)(2,1)S(1)} %get-tuple-element.103.refs_1_, f32[512,256]{1,0:T(8,128)S(1)} %collective-permute-done.13.refs_2_, f32[2048,128]{1,0:T(8,128)S(1)} %pair_terms.17.refs_3_), custom_call_target="tpu_custom_call", output_to_operand_aliasing={{}: (3, {})} | custom-call | flops 3221225472 | bytes 4194304 | tf_op jit(solution)/shard_map/pair_terms/pallas_call | solution.py:25
  41.3 1.9 %pair_terms.19.refs_3_ = f32[1024,128]{1,0:T(8,128)S(1)} custom-call(bf16[2048,512]{1,0:T(8,128)(2,1)S(1)} %get-tuple-element.102.refs_0_, bf16[2048,512]{1,0:T(8,128)(2,1)S(1)} %get-tuple-element.103.refs_1_, f32[512,256]{1,0:T(8,128)S(1)} %collective-permute-done.12.refs_2_, f32[2048,128]{1,0:T(8,128)S(1)} %pair_terms.18.refs_3_.refs_5_), custom_call_target="tpu_custom_call" | custom-call | flops 1610612736 | bytes 4194304 | tf_op jit(solution)/shard_map/pair_terms/pallas_call | solution.py:25
  43.2 1.1 %pair_terms.20.refs_3_ = f32[1024,128]{1,0:T(8,128)S(1)} custom-call(bf16[2048,512]{1,0:T(8,128)(2,1)S(1)} %get-tuple-element.102.refs_0_, bf16[2048,512]{1,0:T(8,128)(2,1)S(1)} %get-tuple-element.103.refs_1_, f32[256,256]{1,0:T(8,128)S(1)} %collective-permute-done.14.refs_2_.refs_3_, f32[1024,128]{1,0:T(8,128)S(1)} %pair_terms.19.refs_3_), custom_call_target="tpu_custom_call", output_to_operand_aliasing={{}: (3, {})} | custom-call | flops 805306368 | bytes 4194304 | tf_op jit(solution)/shard_map/pair_terms/pallas_call | solution.py:25
  44.4 1.3 %collective-permute-done.15.refs_2_.refs_4_ = f32[256,256]{1,0:T(8,128)S(1)} collective-permute-done((f32[256,256]{1,0:T(8,128)S(1)}, f32[256,256]{1,0:T(8,128)S(1)}, u32[]{:S(2)}, u32[]{:S(2)}) %collective-permute-start.15) | collective-permute-done | bytes 262176 | tf_op jit(solution)/shard_map/ppermute | solution.py:210
  45.6 0.7 %pair_terms.22 = f32[512,128]{1,0:T(8,128)S(1)} custom-call(bf16[2048,512]{1,0:T(8,128)(2,1)S(1)} %get-tuple-element.102.refs_0_, bf16[2048,512]{1,0:T(8,128)(2,1)S(1)} %get-tuple-element.103.refs_1_, f32[256,256]{1,0:T(8,128)S(1)} %collective-permute-done.15.refs_2_.refs_4_, f32[1024,128]{1,0:T(8,128)S(1)} %pair_terms.20.refs_3_), custom_call_target="tpu_custom_call" | custom-call | flops 402653184 | bytes 4194304 | tf_op jit(solution)/shard_map/pair_terms/pallas_call | solution.py:25
  46.3 0.1 collective-permute-start.16
  46.4 0.7 %pair_terms.21 = f32[512,128]{1,0:T(8,128)S(1)} custom-call(bf16[2048,512]{1,0:T(8,128)(2,1)S(1)} %get-tuple-element.102.refs_0_, bf16[2048,512]{1,0:T(8,128)(2,1)S(1)} %get-tuple-element.103.refs_1_, f32[256,256]{1,0:T(8,128)S(1)} %collective-permute-done.15.refs_2_.refs_4_, f32[1024,128]{1,0:T(8,128)S(1)} %pair_terms.20.refs_3_), custom_call_target="tpu_custom_call" | custom-call | flops 402653184 | bytes 4194304 | tf_op jit(solution)/shard_map/pair_terms/pallas_call | solution.py:25
  47.1 0.8 %collective-permute-done.16 = f32[512,128]{1,0:T(8,128)S(1)} collective-permute-done((f32[512,128]{1,0:T(8,128)S(1)}, f32[512,128]{1,0:T(8,128)S(1)}, u32[]{:S(2)}, u32[]{:S(2)}) %collective-permute-start.16) | collective-permute-done | bytes 262176 | tf_op jit(solution)/shard_map/ppermute | solution.py:213
  48.0 1.6 %collective-permute-start.19 = (f32[512,128]{1,0:T(8,128)S(1)}, f32[512,128]{1,0:T(8,128)S(1)}, u32[]{:S(2)}, u32[]{:S(2)}) collective-permute-start(f32[512,128]{1,0:T(8,128)S(1)} %add.14), channel_id=1, source_target_pairs={{0,1},{1,0},{2,3},{3,2},{4,5},{5,4},{6,7},{7,6},{8,9},{9,8},{10,11... | collective-permute-start | bytes 786440 | tf_op jit(solution)/shard_map/ppermute | solution.py:272
  49.5 3.6 %pair_terms.23 = f32[1024,128]{1,0:T(8,128)S(1)} custom-call(bf16[2048,512]{1,0:T(8,128)(2,1)S(1)} %get-tuple-element.102.refs_0_, bf16[2048,512]{1,0:T(8,128)(2,1)S(1)} %get-tuple-element.103.refs_1_, f32[512,256]{1,0:T(8,128)S(1)} %collective-permute-done.12.refs_2_, f32[256,256]{1,0:T(8,128)S(1)} %collective-permute-done.14.refs_2_.refs_3_, ...), custom_call_target="tpu_custom_call" | custom-call | flops 3221225472 | bytes 4194304 | tf_op jit(solution)/shard_map/pair_terms/pallas_call | solution.py:25
  53.1 0.1 collective-permute-start.17
  53.2 0.5 collective-permute-start.18
  53.7 0.8 %collective-permute-done.17 = f32[256,128]{1,0:T(8,128)S(1)} collective-permute-done((f32[256,128]{1,0:T(8,128)S(1)}, f32[256,128]{1,0:T(8,128)S(1)}, u32[]{:S(2)}, u32[]{:S(2)}) %collective-permute-start.17) | collective-permute-done | bytes 131104 | tf_op jit(solution)/shard_map/ppermute | solution.py:213
  54.5 0.2 collective-permute-done.18
  54.7 1.7 %collective-permute-done.19 = f32[512,128]{1,0:T(8,128)S(1)} collective-permute-done((f32[512,128]{1,0:T(8,128)S(1)}, f32[512,128]{1,0:T(8,128)S(1)}, u32[]{:S(2)}, u32[]{:S(2)}) %collective-permute-start.19) | collective-permute-done | bytes 262176 | tf_op jit(solution)/shard_map/ppermute | solution.py:272
  56.4 0.7 %fusion.1 = f32[512,128]{1,0:T(8,128)} fusion(f32[512,128]{1,0:T(8,128)S(1)} %collective-permute-done.19, f32[1024,128]{1,0:T(8,128)S(1)} %pair_terms.23, f32[256,128]{1,0:T(8,128)S(1)} %collective-permute-done.18, f32[256,128]{1,0:T(8,128)S(1)} %collective-permute-done.17), kind=kLoop, calls=%fused_computation.4 | loop fusion | flops 262144 | bytes 1048576 | tf_op jit(solution)/shard_map/mul | solution.py:279
  (22 shorter events, 0.2 us)
Async XLA Ops:
  0.0 4.3 %copy-start.1 = (f32[1024,128]{1,0:T(8,128)S(1)}, f32[1024,128]{1,0:T(8,128)}, u32[]{:S(2)}) copy-start(f32[1024,128]{1,0:T(8,128)} %fac_ref) | copy-start | bytes 1572868
  0.0 4.3 %copy-start = (f32[1024,128]{1,0:T(8,128)S(1)}, f32[1024,128]{1,0:T(8,128)}, u32[]{:S(2)}) copy-start(f32[1024,128]{1,0:T(8,128)} %feat_ref) | copy-start | bytes 1572868
  1.2 10.2 %collective-permute-start.5 = (f32[512,256]{1,0:T(8,128)S(1)}, f32[512,256]{1,0:T(8,128)S(1)}, u32[]{:S(2)}, u32[]{:S(2)}) collective-permute-start(f32[512,256]{1,0:T(8,128)S(1)} %constant_dynamic-update-slice_fusion), channel_id=1, source_target_pairs={{0,8},{2,6},{8,16},{10,2},{16,24},{18,10},{24,28},{26,18},{28,20},... | collective-permute-start | bytes 1572872 | tf_op jit(solution)/shard_map/ppermute | solution.py:210
  4.6 1.4 %collective-permute-start = (f32[256,128]{1,0:T(8,128)S(1)}, f32[256,128]{1,0:T(8,128)S(1)}, u32[]{:S(2)}, u32[]{:S(2)}) collective-permute-start(f32[256,128]{1,0:T(8,128)S(1)} %get-tuple-element.64.refs_2_), channel_id=1, source_target_pairs={{0,2},{2,0},{4,6},{6,4},{8,10},{10,8},{12,14},{14,12},{16,18},{18,... | collective-permute-start | bytes 393224 | tf_op jit(solution)/shard_map/ppermute | solution.py:213
  4.7 1.5 %collective-permute-start.1 = (f32[256,128]{1,0:T(8,128)S(1)}, f32[256,128]{1,0:T(8,128)S(1)}, u32[]{:S(2)}, u32[]{:S(2)}) collective-permute-start(f32[256,128]{1,0:T(8,128)S(1)} %get-tuple-element.65.refs_4_), channel_id=1, source_target_pairs={{0,2},{2,0},{4,6},{6,4},{8,10},{10,8},{12,14},{14,12},{16,18},{18,... | collective-permute-start | bytes 393224 | tf_op jit(solution)/shard_map/ppermute | solution.py:213
  5.2 1.4 %collective-permute-start.2 = (f32[256,128]{1,0:T(8,128)S(1)}, f32[256,128]{1,0:T(8,128)S(1)}, u32[]{:S(2)}, u32[]{:S(2)}) collective-permute-start(f32[256,128]{1,0:T(8,128)S(1)} %get-tuple-element.66.refs_3_), channel_id=1, source_target_pairs={{0,2},{2,0},{4,6},{6,4},{8,10},{10,8},{12,14},{14,12},{16,18},{18,... | collective-permute-start | bytes 393224 | tf_op jit(solution)/shard_map/ppermute | solution.py:213
  5.3 1.5 %collective-permute-start.3 = (f32[256,128]{1,0:T(8,128)S(1)}, f32[256,128]{1,0:T(8,128)S(1)}, u32[]{:S(2)}, u32[]{:S(2)}) collective-permute-start(f32[256,128]{1,0:T(8,128)S(1)} %get-tuple-element.67.refs_5_), channel_id=1, source_target_pairs={{0,2},{2,0},{4,6},{6,4},{8,10},{10,8},{12,14},{14,12},{16,18},{18,... | collective-permute-start | bytes 393224 | tf_op jit(solution)/shard_map/ppermute | solution.py:213
  6.1 1.3 %collective-permute-start.6 = (f32[256,128]{1,0:T(8,128)S(1)}, f32[256,128]{1,0:T(8,128)S(1)}, u32[]{:S(2)}, u32[]{:S(2)}) collective-permute-start(f32[256,128]{1,0:T(8,128)S(1)} %get-tuple-element.68.refs_2_), channel_id=1, source_target_pairs={{0,2},{2,0},{4,6},{6,4},{8,10},{10,8},{12,14},{14,12},{16,18},{18,... | collective-permute-start | bytes 393224 | tf_op jit(solution)/shard_map/ppermute | solution.py:213
  6.2 2.7 %collective-permute-start.7 = (f32[256,128]{1,0:T(8,128)S(1)}, f32[256,128]{1,0:T(8,128)S(1)}, u32[]{:S(2)}, u32[]{:S(2)}) collective-permute-start(f32[256,128]{1,0:T(8,128)S(1)} %get-tuple-element.69.refs_3_), channel_id=1, source_target_pairs={{0,2},{2,0},{4,6},{6,4},{8,10},{10,8},{12,14},{14,12},{16,18},{18,... | collective-permute-start | bytes 393224 | tf_op jit(solution)/shard_map/ppermute | solution.py:213
  6.6 2.4 %collective-permute-start.8 = (f32[256,128]{1,0:T(8,128)S(1)}, f32[256,128]{1,0:T(8,128)S(1)}, u32[]{:S(2)}, u32[]{:S(2)}) collective-permute-start(f32[256,128]{1,0:T(8,128)S(1)} %get-tuple-element.70.refs_4_), channel_id=1, source_target_pairs={{0,2},{2,0},{4,6},{6,4},{8,10},{10,8},{12,14},{14,12},{16,18},{18,... | collective-permute-start | bytes 393224 | tf_op jit(solution)/shard_map/ppermute | solution.py:213
  6.8 2.2 %collective-permute-start.9 = (f32[256,128]{1,0:T(8,128)S(1)}, f32[256,128]{1,0:T(8,128)S(1)}, u32[]{:S(2)}, u32[]{:S(2)}) collective-permute-start(f32[256,128]{1,0:T(8,128)S(1)} %get-tuple-element.71.refs_5_), channel_id=1, source_target_pairs={{0,2},{2,0},{4,6},{6,4},{8,10},{10,8},{12,14},{14,12},{16,18},{18,... | collective-permute-start | bytes 393224 | tf_op jit(solution)/shard_map/ppermute | solution.py:213
  7.4 12.0 %collective-permute-start.4 = (f32[512,256]{1,0:T(8,128)S(1)}, f32[512,256]{1,0:T(8,128)S(1)}, u32[]{:S(2)}, u32[]{:S(2)}) collective-permute-start(f32[512,256]{1,0:T(8,128)S(1)} %maximum_maximum_fusion), channel_id=1, source_target_pairs={{0,8},{2,6},{8,16},{10,2},{16,24},{18,10},{24,28},{26,18},{28,20},... | collective-permute-start | bytes 1572872 | tf_op jit(solution)/shard_map/ppermute | solution.py:210
  11.7 13.1 %collective-permute-start.11 = (f32[512,256]{1,0:T(8,128)S(1)}, f32[512,256]{1,0:T(8,128)S(1)}, u32[]{:S(2)}, u32[]{:S(2)}) collective-permute-start(f32[512,256]{1,0:T(8,128)S(1)} %pad_maximum_fusion.refs_2_), channel_id=1, source_target_pairs={{0,8},{2,6},{8,16},{10,2},{16,24},{18,10},{24,28},{26,18},{28,20},... | collective-permute-start | bytes 1572872 | tf_op jit(solution)/shard_map/ppermute | solution.py:210
  19.4 10.7 %collective-permute-start.10 = (f32[512,256]{1,0:T(8,128)S(1)}, f32[512,256]{1,0:T(8,128)S(1)}, u32[]{:S(2)}, u32[]{:S(2)}) collective-permute-start(f32[512,256]{1,0:T(8,128)S(1)} %collective-permute-done.4.refs_2_), channel_id=1, source_target_pairs={{0,8},{2,6},{8,16},{10,2},{16,24},{18,10},{24,28},{26,18},{28,20},... | collective-permute-start | bytes 1572872 | tf_op jit(solution)/shard_map/ppermute | solution.py:210
  24.8 10.5 %collective-permute-start.13 = (f32[512,256]{1,0:T(8,128)S(1)}, f32[512,256]{1,0:T(8,128)S(1)}, u32[]{:S(2)}, u32[]{:S(2)}) collective-permute-start(f32[512,256]{1,0:T(8,128)S(1)} %collective-permute-done.11.refs_2_), channel_id=1, source_target_pairs={{0,8},{2,6},{8,16},{10,2},{16,24},{18,10},{24,28},{26,18},{28,20},... | collective-permute-start | bytes 1572872 | tf_op jit(solution)/shard_map/ppermute | solution.py:210
  30.1 11.2 %collective-permute-start.12 = (f32[512,256]{1,0:T(8,128)S(1)}, f32[512,256]{1,0:T(8,128)S(1)}, u32[]{:S(2)}, u32[]{:S(2)}) collective-permute-start(f32[512,256]{1,0:T(8,128)S(1)} %collective-permute-done.10.refs_2_), channel_id=1, source_target_pairs={{0,8},{2,6},{8,16},{10,2},{16,24},{18,10},{24,28},{26,18},{28,20},... | collective-permute-start | bytes 1572872 | tf_op jit(solution)/shard_map/ppermute | solution.py:210
  35.4 7.8 %collective-permute-start.14 = (f32[256,256]{1,0:T(8,128)S(1)}, f32[256,256]{1,0:T(8,128)S(1)}, u32[]{:S(2)}, u32[]{:S(2)}) collective-permute-start(f32[256,256]{1,0:T(8,128)S(1)} %get-tuple-element.117), channel_id=1, source_target_pairs={{0,8},{2,6},{8,16},{10,2},{16,24},{18,10},{24,28},{26,18},{28,20},... | collective-permute-start | bytes 786440 | tf_op jit(solution)/shard_map/ppermute | solution.py:210
  36.1 9.6 %collective-permute-start.15 = (f32[256,256]{1,0:T(8,128)S(1)}, f32[256,256]{1,0:T(8,128)S(1)}, u32[]{:S(2)}, u32[]{:S(2)}) collective-permute-start(f32[256,256]{1,0:T(8,128)S(1)} %get-tuple-element.118), channel_id=1, source_target_pairs={{0,8},{2,6},{8,16},{10,2},{16,24},{18,10},{24,28},{26,18},{28,20},... | collective-permute-start | bytes 786440 | tf_op jit(solution)/shard_map/ppermute | solution.py:210
  46.3 1.6 %collective-permute-start.16 = (f32[512,128]{1,0:T(8,128)S(1)}, f32[512,128]{1,0:T(8,128)S(1)}, u32[]{:S(2)}, u32[]{:S(2)}) collective-permute-start(f32[512,128]{1,0:T(8,128)S(1)} %pair_terms.22), channel_id=1, source_target_pairs={{0,2},{2,0},{4,6},{6,4},{8,10},{10,8},{12,14},{14,12},{16,18},{18,... | collective-permute-start | bytes 786440 | tf_op jit(solution)/shard_map/ppermute | solution.py:213
  48.0 8.4 %collective-permute-start.19 = (f32[512,128]{1,0:T(8,128)S(1)}, f32[512,128]{1,0:T(8,128)S(1)}, u32[]{:S(2)}, u32[]{:S(2)}) collective-permute-start(f32[512,128]{1,0:T(8,128)S(1)} %add.14), channel_id=1, source_target_pairs={{0,1},{1,0},{2,3},{3,2},{4,5},{5,4},{6,7},{7,6},{8,9},{9,8},{10,11... | collective-permute-start | bytes 786440 | tf_op jit(solution)/shard_map/ppermute | solution.py:272
  53.1 1.4 %collective-permute-start.17 = (f32[256,128]{1,0:T(8,128)S(1)}, f32[256,128]{1,0:T(8,128)S(1)}, u32[]{:S(2)}, u32[]{:S(2)}) collective-permute-start(f32[256,128]{1,0:T(8,128)S(1)} %get-tuple-element.115), channel_id=1, source_target_pairs={{0,2},{2,0},{4,6},{6,4},{8,10},{10,8},{12,14},{14,12},{16,18},{18,... | collective-permute-start | bytes 393224 | tf_op jit(solution)/shard_map/ppermute | solution.py:213
  53.2 1.5 %collective-permute-start.18 = (f32[256,128]{1,0:T(8,128)S(1)}, f32[256,128]{1,0:T(8,128)S(1)}, u32[]{:S(2)}, u32[]{:S(2)}) collective-permute-start(f32[256,128]{1,0:T(8,128)S(1)} %get-tuple-element.116), channel_id=1, source_target_pairs={{0,2},{2,0},{4,6},{6,4},{8,10},{10,8},{12,14},{14,12},{16,18},{18,... | collective-permute-start | bytes 393224 | tf_op jit(solution)/shard_map/ppermute | solution.py:213

commit v8 on v7

--- a/solution.py
+++ b/solution.py
@@ -206,7 +206,10 @@
     def ring(x):
         moves = []
         for p in range(homes):
-            moves += [(order[p] * 2 + c, order[(p + 1 - 2 * c) % homes] * 2 + c) for c in range(2)]
+            for c in range(2):
+                onward = (p + c) % 2 == 0 if homes % 2 == 0 else c == 0
+                core = 1 - c if homes % 2 == 0 else c
+                moves.append((order[p] * 2 + c, order[(p + (1 if onward else -1)) % homes] * 2 + core))
         return lax.ppermute(x, "blk", moves)
 
     def other_core(x):

time: 57.3 us -> 56.5 us (0.986)
  waiting for transfers between devices: 5.7 us -> 4.45 us
    ppermute x11, starting transfers between devices: 2.7 us -> 3.69 us  [other_core(): return lax.ppermute(x, 'blk', [(b, b ^ 1) for b in range(blocks)])]
    ppermute x8, starting transfers between devices: 14.1 us -> 13.1 us  [ring(): return lax.ppermute(x, 'blk', moves)]
    ppermute x8, waiting for transfers between devices: 1.51 us -> 0.81 us  [ring(): return lax.ppermute(x, 'blk', moves)]
  transfers between devices with their start and end apart: 20 -> 20, of which waited for: 8 -> 7; matrix products, arithmetic and copies ran while one was open for 1% -> 1% of each run, Pallas kernels for 52% -> 53%
where the time goes in v8:
time: 56.5 us; the launch traced here: 56.3 us
  Pallas kernels  30.5 us (54%)
  starting transfers between devices  18.8 us (33%)
  waiting for transfers between devices  4.45 us (8%)
  local copies, waits for them, and re-layouts  1.25 us (2%)
  other arithmetic  1.13 us (2%)
    pallas_call x12, Pallas kernels, call(): pl.pallas_call(kernel, in_specs=[IN_VMEM] * len(args), out_specs=jax.tree...  29.8 us
    ppermute x8, starting transfers between devices, ring(): return lax.ppermute(x, 'blk', moves)  13.1 us
    ppermute x11, starting transfers between devices, other_core(): return lax.ppermute(x, 'blk', [(b, b ^ 1) for b in range(blocks)])  3.69 us
    ppermute x11, waiting for transfers between devices, other_core(): return lax.ppermute(x, 'blk', [(b, b ^ 1) for b in range(blocks)])  2.16 us
    ppermute x1, starting transfers between devices, body(): lax.ppermute(part, 'rep', [(r, (r + k + 1) % replicas) for r in range(rep...  1.98 us
    ppermute x1, waiting for transfers between devices, body(): lax.ppermute(part, 'rep', [(r, (r + k + 1) % replicas) for r in range(rep...  1.48 us
    dynamic_slice x1, local copies, waits for them, and re-layouts, body(): lax.dynamic_slice_in_dim(x, rep * share, share)  1.15 us
  transfers between devices with their start and end apart: 20, of which 7 were waited for; matrix products, arithmetic and copies ran while one was open for 1% of the time, Pallas kernels for 53%

profile of v8, /device:TPU:0, one launch (start us, length us, event | category | flops | bytes accessed | tf_op | source)
XLA Modules:
  0.0 56.3 jit_solution(8694972986482903668)
XLA Ops:
  0.0 1.2 %constant_dynamic-slice_fusion = (f32[512,128]{1,0:T(8,128)S(1)}, f32[512,128]{1,0:T(8,128)S(1)}) fusion(f32[1024,128]{1,0:T(8,128)} %fac_ref, s32[]{:T(128)S(6)} %select_n.4, f32[1024,128]{1,0:T(8,128)} %feat_ref), kind=kLoop, calls=%fused_computation.11 | loop fusion | bytes 1048580 | tf_op jit(solution)/shard_map/dynamic_slice | solution.py:221
  1.2 2.5 %collective-permute-start.5 = (f32[512,256]{1,0:T(8,128)S(1)}, f32[512,256]{1,0:T(8,128)S(1)}, u32[]{:S(2)}, u32[]{:S(2)}) collective-permute-start(f32[512,256]{1,0:T(8,128)S(1)} %constant_dynamic-update-slice_fusion), channel_id=1, source_target_pairs={{0,10},{2,4},{8,2},{10,16},{16,26},{18,8},{24,18},{26,28},{28,22},... | collective-permute-start | bytes 1572872 | tf_op jit(solution)/shard_map/ppermute | solution.py:213
  3.7 0.3 own_rows.1
  4.1 0.7 %collective-permute-start = (f32[256,128]{1,0:T(8,128)S(1)}, f32[256,128]{1,0:T(8,128)S(1)}, u32[]{:S(2)}, u32[]{:S(2)}) collective-permute-start(f32[256,128]{1,0:T(8,128)S(1)} %get-tuple-element.64.refs_2_), channel_id=1, source_target_pairs={{0,2},{2,0},{4,6},{6,4},{8,10},{10,8},{12,14},{14,12},{16,18},{18,... | collective-permute-start | bytes 393224 | tf_op jit(solution)/shard_map/ppermute | solution.py:216
  4.8 0.1 collective-permute-start.1
  4.8 0.4 collective-permute-start.2
  5.3 0.1 collective-permute-start.3
  5.4 0.4 collective-permute-done.refs_4_
  5.8 0.4 collective-permute-start.6
  6.1 0.0 collective-permute-done.1.refs_6_
  6.1 0.2 collective-permute-start.7
  6.3 0.3 collective-permute-start.8
  6.6 0.0 collective-permute-done.3.refs_7_
  6.6 0.2 collective-permute-start.9
  6.9 0.2 collective-permute-done.6.refs_0_
  7.1 1.6 %collective-permute-start.4 = (f32[512,256]{1,0:T(8,128)S(1)}, f32[512,256]{1,0:T(8,128)S(1)}, u32[]{:S(2)}, u32[]{:S(2)}) collective-permute-start(f32[512,256]{1,0:T(8,128)S(1)} %maximum_maximum_fusion), channel_id=1, source_target_pairs={{0,10},{2,4},{8,2},{10,16},{16,26},{18,8},{24,18},{26,28},{28,22},... | collective-permute-start | bytes 1572872 | tf_op jit(solution)/shard_map/ppermute | solution.py:213
  8.7 0.3 other_rows.1
  9.0 1.9 %pair_terms.12.refs_6_ = f32[1024,128]{1,0:T(8,128)S(1)} custom-call(bf16[2048,512]{1,0:T(8,128)(2,1)S(1)} %get-tuple-element.102.refs_0_, bf16[2048,512]{1,0:T(8,128)(2,1)S(1)} %get-tuple-element.103.refs_1_, f32[256,128]{1,0:T(8,128)S(1)} %get-tuple-element.68.refs_2_, f32[256,128]{1,0:T(8,128)S(1)} %get-tuple-element.69.refs_3_, ...), custom_call_target="tpu_custom_call" | custom-call | flops 1610612736 | bytes 4194304 | tf_op jit(solution)/shard_map/pair_terms/pallas_call | solution.py:25
  10.9 0.0 collective-permute-done.5
  10.9 0.1 slice_multiply_fusion.1
  11.1 0.1 slice_multiply_fusion
  11.3 1.8 %collective-permute-start.11 = (f32[512,256]{1,0:T(8,128)S(1)}, f32[512,256]{1,0:T(8,128)S(1)}, u32[]{:S(2)}, u32[]{:S(2)}) collective-permute-start(f32[512,256]{1,0:T(8,128)S(1)} %pad_maximum_fusion.refs_2_), channel_id=1, source_target_pairs={{0,10},{2,4},{8,2},{10,16},{16,26},{18,8},{24,18},{26,28},{28,22},... | collective-permute-start | bytes 1572872 | tf_op jit(solution)/shard_map/ppermute | solution.py:213
  13.0 3.5 %pair_terms.13.refs_3_ = f32[2048,128]{1,0:T(8,128)S(1)} custom-call(bf16[2048,512]{1,0:T(8,128)(2,1)S(1)} %get-tuple-element.102.refs_0_, bf16[2048,512]{1,0:T(8,128)(2,1)S(1)} %get-tuple-element.103.refs_1_, f32[512,256]{1,0:T(8,128)S(1)} %pad_maximum_fusion.refs_2_), custom_call_target="tpu_custom_call" | custom-call | flops 3221225472 | bytes 4194304 | tf_op jit(solution)/shard_map/pair_terms/pallas_call | solution.py:25
  16.6 1.9 %pair_terms.14.refs_6_ = f32[1024,128]{1,0:T(8,128)S(1)} custom-call(bf16[2048,512]{1,0:T(8,128)(2,1)S(1)} %get-tuple-element.102.refs_0_, bf16[2048,512]{1,0:T(8,128)(2,1)S(1)} %get-tuple-element.103.refs_1_, f32[256,128]{1,0:T(8,128)S(1)} %get-tuple-element.64.refs_2_, f32[256,128]{1,0:T(8,128)S(1)} %get-tuple-element.66.refs_3_, ...), custom_call_target="tpu_custom_call", output_to_operand_aliasing={{}: (6, {})} | custom-call | flops 1610612736 | bytes 4194304 | tf_op jit(solution)/shard_map/pair_terms/pallas_call | solution.py:25
  18.5 1.8 %collective-permute-start.10 = (f32[512,256]{1,0:T(8,128)S(1)}, f32[512,256]{1,0:T(8,128)S(1)}, u32[]{:S(2)}, u32[]{:S(2)}) collective-permute-start(f32[512,256]{1,0:T(8,128)S(1)} %collective-permute-done.4.refs_2_), channel_id=1, source_target_pairs={{0,10},{2,4},{8,2},{10,16},{16,26},{18,8},{24,18},{26,28},{28,22},... | collective-permute-start | bytes 1572872 | tf_op jit(solution)/shard_map/ppermute | solution.py:213
  20.3 3.6 %pair_terms.15.refs_3_ = f32[2048,128]{1,0:T(8,128)S(1)} custom-call(bf16[2048,512]{1,0:T(8,128)(2,1)S(1)} %get-tuple-element.102.refs_0_, bf16[2048,512]{1,0:T(8,128)(2,1)S(1)} %get-tuple-element.103.refs_1_, f32[512,256]{1,0:T(8,128)S(1)} %collective-permute-done.4.refs_2_, f32[2048,128]{1,0:T(8,128)S(1)} %pair_terms.13.refs_3_), custom_call_target="tpu_custom_call", output_to_operand_aliasing={{}: (3, {})} | custom-call | flops 3221225472 | bytes 4194304 | tf_op jit(solution)/shard_map/pair_terms/pallas_call | solution.py:25
  24.0 1.4 %collective-permute-start.13 = (f32[512,256]{1,0:T(8,128)S(1)}, f32[512,256]{1,0:T(8,128)S(1)}, u32[]{:S(2)}, u32[]{:S(2)}) collective-permute-start(f32[512,256]{1,0:T(8,128)S(1)} %collective-permute-done.11.refs_2_), channel_id=1, source_target_pairs={{0,10},{2,4},{8,2},{10,16},{16,26},{18,8},{24,18},{26,28},{28,22},... | collective-permute-start | bytes 1572872 | tf_op jit(solution)/shard_map/ppermute | solution.py:213
  25.3 3.6 %pair_terms.16.refs_3_ = f32[2048,128]{1,0:T(8,128)S(1)} custom-call(bf16[2048,512]{1,0:T(8,128)(2,1)S(1)} %get-tuple-element.102.refs_0_, bf16[2048,512]{1,0:T(8,128)(2,1)S(1)} %get-tuple-element.103.refs_1_, f32[512,256]{1,0:T(8,128)S(1)} %collective-permute-done.11.refs_2_, f32[2048,128]{1,0:T(8,128)S(1)} %pair_terms.15.refs_3_), custom_call_target="tpu_custom_call", output_to_operand_aliasing={{}: (3, {})} | custom-call | flops 3221225472 | bytes 4194304 | tf_op jit(solution)/shard_map/pair_terms/pallas_call | solution.py:25
  29.0 1.6 %collective-permute-start.12 = (f32[512,256]{1,0:T(8,128)S(1)}, f32[512,256]{1,0:T(8,128)S(1)}, u32[]{:S(2)}, u32[]{:S(2)}) collective-permute-start(f32[512,256]{1,0:T(8,128)S(1)} %collective-permute-done.10.refs_2_), channel_id=1, source_target_pairs={{0,10},{2,4},{8,2},{10,16},{16,26},{18,8},{24,18},{26,28},{28,22},... | collective-permute-start | bytes 1572872 | tf_op jit(solution)/shard_map/ppermute | solution.py:213
  30.6 3.6 %pair_terms.17.refs_3_ = f32[2048,128]{1,0:T(8,128)S(1)} custom-call(bf16[2048,512]{1,0:T(8,128)(2,1)S(1)} %get-tuple-element.102.refs_0_, bf16[2048,512]{1,0:T(8,128)(2,1)S(1)} %get-tuple-element.103.refs_1_, f32[512,256]{1,0:T(8,128)S(1)} %collective-permute-done.10.refs_2_, f32[2048,128]{1,0:T(8,128)S(1)} %pair_terms.16.refs_3_), custom_call_target="tpu_custom_call", output_to_operand_aliasing={{}: (3, {})} | custom-call | flops 3221225472 | bytes 4194304 | tf_op jit(solution)/shard_map/pair_terms/pallas_call | solution.py:25
  34.2 0.9 %collective-permute-start.14 = (f32[256,256]{1,0:T(8,128)S(1)}, f32[256,256]{1,0:T(8,128)S(1)}, u32[]{:S(2)}, u32[]{:S(2)}) collective-permute-start(f32[256,256]{1,0:T(8,128)S(1)} %get-tuple-element.117), channel_id=1, source_target_pairs={{0,10},{2,4},{8,2},{10,16},{16,26},{18,8},{24,18},{26,28},{28,22},... | collective-permute-start | bytes 786440 | tf_op jit(solution)/shard_map/ppermute | solution.py:213
  35.2 1.6 %collective-permute-start.15 = (f32[256,256]{1,0:T(8,128)S(1)}, f32[256,256]{1,0:T(8,128)S(1)}, u32[]{:S(2)}, u32[]{:S(2)}) collective-permute-start(f32[256,256]{1,0:T(8,128)S(1)} %get-tuple-element.118), channel_id=1, source_target_pairs={{0,10},{2,4},{8,2},{10,16},{16,26},{18,8},{24,18},{26,28},{28,22},... | collective-permute-start | bytes 786440 | tf_op jit(solution)/shard_map/ppermute | solution.py:213
  36.8 3.6 %pair_terms.18.refs_3_.refs_5_ = f32[2048,128]{1,0:T(8,128)S(1)} custom-call(bf16[2048,512]{1,0:T(8,128)(2,1)S(1)} %get-tuple-element.102.refs_0_, bf16[2048,512]{1,0:T(8,128)(2,1)S(1)} %get-tuple-element.103.refs_1_, f32[512,256]{1,0:T(8,128)S(1)} %collective-permute-done.13.refs_2_, f32[2048,128]{1,0:T(8,128)S(1)} %pair_terms.17.refs_3_), custom_call_target="tpu_custom_call", output_to_operand_aliasing={{}: (3, {})} | custom-call | flops 3221225472 | bytes 4194304 | tf_op jit(solution)/shard_map/pair_terms/pallas_call | solution.py:25
  40.4 1.9 %pair_terms.19.refs_3_ = f32[1024,128]{1,0:T(8,128)S(1)} custom-call(bf16[2048,512]{1,0:T(8,128)(2,1)S(1)} %get-tuple-element.102.refs_0_, bf16[2048,512]{1,0:T(8,128)(2,1)S(1)} %get-tuple-element.103.refs_1_, f32[512,256]{1,0:T(8,128)S(1)} %collective-permute-done.12.refs_2_, f32[2048,128]{1,0:T(8,128)S(1)} %pair_terms.18.refs_3_.refs_5_), custom_call_target="tpu_custom_call" | custom-call | flops 1610612736 | bytes 4194304 | tf_op jit(solution)/shard_map/pair_terms/pallas_call | solution.py:25
  42.3 1.1 %pair_terms.20.refs_3_ = f32[1024,128]{1,0:T(8,128)S(1)} custom-call(bf16[2048,512]{1,0:T(8,128)(2,1)S(1)} %get-tuple-element.102.refs_0_, bf16[2048,512]{1,0:T(8,128)(2,1)S(1)} %get-tuple-element.103.refs_1_, f32[256,256]{1,0:T(8,128)S(1)} %collective-permute-done.14.refs_2_.refs_3_, f32[1024,128]{1,0:T(8,128)S(1)} %pair_terms.19.refs_3_), custom_call_target="tpu_custom_call", output_to_operand_aliasing={{}: (3, {})} | custom-call | flops 805306368 | bytes 4194304 | tf_op jit(solution)/shard_map/pair_terms/pallas_call | solution.py:25
  43.5 0.8 %collective-permute-done.15.refs_2_.refs_4_ = f32[256,256]{1,0:T(8,128)S(1)} collective-permute-done((f32[256,256]{1,0:T(8,128)S(1)}, f32[256,256]{1,0:T(8,128)S(1)}, u32[]{:S(2)}, u32[]{:S(2)}) %collective-permute-start.15) | collective-permute-done | bytes 262176 | tf_op jit(solution)/shard_map/ppermute | solution.py:213
  44.2 0.7 %pair_terms.22 = f32[512,128]{1,0:T(8,128)S(1)} custom-call(bf16[2048,512]{1,0:T(8,128)(2,1)S(1)} %get-tuple-element.102.refs_0_, bf16[2048,512]{1,0:T(8,128)(2,1)S(1)} %get-tuple-element.103.refs_1_, f32[256,256]{1,0:T(8,128)S(1)} %collective-permute-done.15.refs_2_.refs_4_, f32[1024,128]{1,0:T(8,128)S(1)} %pair_terms.20.refs_3_), custom_call_target="tpu_custom_call" | custom-call | flops 402653184 | bytes 4194304 | tf_op jit(solution)/shard_map/pair_terms/pallas_call | solution.py:25
  44.9 0.8 %collective-permute-start.16 = (f32[512,128]{1,0:T(8,128)S(1)}, f32[512,128]{1,0:T(8,128)S(1)}, u32[]{:S(2)}, u32[]{:S(2)}) collective-permute-start(f32[512,128]{1,0:T(8,128)S(1)} %pair_terms.22), channel_id=1, source_target_pairs={{0,2},{2,0},{4,6},{6,4},{8,10},{10,8},{12,14},{14,12},{16,18},{18,... | collective-permute-start | bytes 786440 | tf_op jit(solution)/shard_map/ppermute | solution.py:216
  45.7 0.7 %pair_terms.21 = f32[512,128]{1,0:T(8,128)S(1)} custom-call(bf16[2048,512]{1,0:T(8,128)(2,1)S(1)} %get-tuple-element.102.refs_0_, bf16[2048,512]{1,0:T(8,128)(2,1)S(1)} %get-tuple-element.103.refs_1_, f32[256,256]{1,0:T(8,128)S(1)} %collective-permute-done.15.refs_2_.refs_4_, f32[1024,128]{1,0:T(8,128)S(1)} %pair_terms.20.refs_3_), custom_call_target="tpu_custom_call" | custom-call | flops 402653184 | bytes 4194304 | tf_op jit(solution)/shard_map/pair_terms/pallas_call | solution.py:25
  46.4 0.5 collective-permute-done.16
  46.9 2.0 %collective-permute-start.19 = (f32[512,128]{1,0:T(8,128)S(1)}, f32[512,128]{1,0:T(8,128)S(1)}, u32[]{:S(2)}, u32[]{:S(2)}) collective-permute-start(f32[512,128]{1,0:T(8,128)S(1)} %add.14), channel_id=1, source_target_pairs={{0,1},{1,0},{2,3},{3,2},{4,5},{5,4},{6,7},{7,6},{8,9},{9,8},{10,11... | collective-permute-start | bytes 786440 | tf_op jit(solution)/shard_map/ppermute | solution.py:275
  48.9 3.6 %pair_terms.23 = f32[1024,128]{1,0:T(8,128)S(1)} custom-call(bf16[2048,512]{1,0:T(8,128)(2,1)S(1)} %get-tuple-element.102.refs_0_, bf16[2048,512]{1,0:T(8,128)(2,1)S(1)} %get-tuple-element.103.refs_1_, f32[512,256]{1,0:T(8,128)S(1)} %collective-permute-done.12.refs_2_, f32[256,256]{1,0:T(8,128)S(1)} %collective-permute-done.14.refs_2_.refs_3_, ...), custom_call_target="tpu_custom_call" | custom-call | flops 3221225472 | bytes 4194304 | tf_op jit(solution)/shard_map/pair_terms/pallas_call | solution.py:25
  52.5 0.1 collective-permute-start.17
  52.6 0.5 collective-permute-start.18
  53.1 0.8 %collective-permute-done.17 = f32[256,128]{1,0:T(8,128)S(1)} collective-permute-done((f32[256,128]{1,0:T(8,128)S(1)}, f32[256,128]{1,0:T(8,128)S(1)}, u32[]{:S(2)}, u32[]{:S(2)}) %collective-permute-start.17) | collective-permute-done | bytes 131104 | tf_op jit(solution)/shard_map/ppermute | solution.py:216
  53.9 0.2 collective-permute-done.18
  54.1 1.5 %collective-permute-done.19 = f32[512,128]{1,0:T(8,128)S(1)} collective-permute-done((f32[512,128]{1,0:T(8,128)S(1)}, f32[512,128]{1,0:T(8,128)S(1)}, u32[]{:S(2)}, u32[]{:S(2)}) %collective-permute-start.19) | collective-permute-done | bytes 262176 | tf_op jit(solution)/shard_map/ppermute | solution.py:275
  55.6 0.7 %fusion.1 = f32[512,128]{1,0:T(8,128)} fusion(f32[512,128]{1,0:T(8,128)S(1)} %collective-permute-done.19, f32[1024,128]{1,0:T(8,128)S(1)} %pair_terms.23, f32[256,128]{1,0:T(8,128)S(1)} %collective-permute-done.18, f32[256,128]{1,0:T(8,128)S(1)} %collective-permute-done.17), kind=kLoop, calls=%fused_computation.4 | loop fusion | flops 262144 | bytes 1048576 | tf_op jit(solution)/shard_map/mul | solution.py:282
  (22 shorter events, 0.2 us)
Async XLA Ops:
  0.0 3.7 %copy-start.1 = (f32[1024,128]{1,0:T(8,128)S(1)}, f32[1024,128]{1,0:T(8,128)}, u32[]{:S(2)}) copy-start(f32[1024,128]{1,0:T(8,128)} %fac_ref) | copy-start | bytes 1572868
  0.0 3.7 %copy-start = (f32[1024,128]{1,0:T(8,128)S(1)}, f32[1024,128]{1,0:T(8,128)}, u32[]{:S(2)}) copy-start(f32[1024,128]{1,0:T(8,128)} %feat_ref) | copy-start | bytes 1572868
  1.2 9.7 %collective-permute-start.5 = (f32[512,256]{1,0:T(8,128)S(1)}, f32[512,256]{1,0:T(8,128)S(1)}, u32[]{:S(2)}, u32[]{:S(2)}) collective-permute-start(f32[512,256]{1,0:T(8,128)S(1)} %constant_dynamic-update-slice_fusion), channel_id=1, source_target_pairs={{0,10},{2,4},{8,2},{10,16},{16,26},{18,8},{24,18},{26,28},{28,22},... | collective-permute-start | bytes 1572872 | tf_op jit(solution)/shard_map/ppermute | solution.py:213
  4.1 1.7 %collective-permute-start = (f32[256,128]{1,0:T(8,128)S(1)}, f32[256,128]{1,0:T(8,128)S(1)}, u32[]{:S(2)}, u32[]{:S(2)}) collective-permute-start(f32[256,128]{1,0:T(8,128)S(1)} %get-tuple-element.64.refs_2_), channel_id=1, source_target_pairs={{0,2},{2,0},{4,6},{6,4},{8,10},{10,8},{12,14},{14,12},{16,18},{18,... | collective-permute-start | bytes 393224 | tf_op jit(solution)/shard_map/ppermute | solution.py:216
  4.8 1.4 %collective-permute-start.1 = (f32[256,128]{1,0:T(8,128)S(1)}, f32[256,128]{1,0:T(8,128)S(1)}, u32[]{:S(2)}, u32[]{:S(2)}) collective-permute-start(f32[256,128]{1,0:T(8,128)S(1)} %get-tuple-element.65.refs_4_), channel_id=1, source_target_pairs={{0,2},{2,0},{4,6},{6,4},{8,10},{10,8},{12,14},{14,12},{16,18},{18,... | collective-permute-start | bytes 393224 | tf_op jit(solution)/shard_map/ppermute | solution.py:216
  4.8 1.5 %collective-permute-start.2 = (f32[256,128]{1,0:T(8,128)S(1)}, f32[256,128]{1,0:T(8,128)S(1)}, u32[]{:S(2)}, u32[]{:S(2)}) collective-permute-start(f32[256,128]{1,0:T(8,128)S(1)} %get-tuple-element.66.refs_3_), channel_id=1, source_target_pairs={{0,2},{2,0},{4,6},{6,4},{8,10},{10,8},{12,14},{14,12},{16,18},{18,... | collective-permute-start | bytes 393224 | tf_op jit(solution)/shard_map/ppermute | solution.py:216
  5.3 1.4 %collective-permute-start.3 = (f32[256,128]{1,0:T(8,128)S(1)}, f32[256,128]{1,0:T(8,128)S(1)}, u32[]{:S(2)}, u32[]{:S(2)}) collective-permute-start(f32[256,128]{1,0:T(8,128)S(1)} %get-tuple-element.67.refs_5_), channel_id=1, source_target_pairs={{0,2},{2,0},{4,6},{6,4},{8,10},{10,8},{12,14},{14,12},{16,18},{18,... | collective-permute-start | bytes 393224 | tf_op jit(solution)/shard_map/ppermute | solution.py:216
  5.8 1.3 %collective-permute-start.6 = (f32[256,128]{1,0:T(8,128)S(1)}, f32[256,128]{1,0:T(8,128)S(1)}, u32[]{:S(2)}, u32[]{:S(2)}) collective-permute-start(f32[256,128]{1,0:T(8,128)S(1)} %get-tuple-element.68.refs_2_), channel_id=1, source_target_pairs={{0,2},{2,0},{4,6},{6,4},{8,10},{10,8},{12,14},{14,12},{16,18},{18,... | collective-permute-start | bytes 393224 | tf_op jit(solution)/shard_map/ppermute | solution.py:216
  6.1 2.6 %collective-permute-start.7 = (f32[256,128]{1,0:T(8,128)S(1)}, f32[256,128]{1,0:T(8,128)S(1)}, u32[]{:S(2)}, u32[]{:S(2)}) collective-permute-start(f32[256,128]{1,0:T(8,128)S(1)} %get-tuple-element.69.refs_3_), channel_id=1, source_target_pairs={{0,2},{2,0},{4,6},{6,4},{8,10},{10,8},{12,14},{14,12},{16,18},{18,... | collective-permute-start | bytes 393224 | tf_op jit(solution)/shard_map/ppermute | solution.py:216
  6.3 2.4 %collective-permute-start.8 = (f32[256,128]{1,0:T(8,128)S(1)}, f32[256,128]{1,0:T(8,128)S(1)}, u32[]{:S(2)}, u32[]{:S(2)}) collective-permute-start(f32[256,128]{1,0:T(8,128)S(1)} %get-tuple-element.70.refs_4_), channel_id=1, source_target_pairs={{0,2},{2,0},{4,6},{6,4},{8,10},{10,8},{12,14},{14,12},{16,18},{18,... | collective-permute-start | bytes 393224 | tf_op jit(solution)/shard_map/ppermute | solution.py:216
  6.6 2.1 %collective-permute-start.9 = (f32[256,128]{1,0:T(8,128)S(1)}, f32[256,128]{1,0:T(8,128)S(1)}, u32[]{:S(2)}, u32[]{:S(2)}) collective-permute-start(f32[256,128]{1,0:T(8,128)S(1)} %get-tuple-element.71.refs_5_), channel_id=1, source_target_pairs={{0,2},{2,0},{4,6},{6,4},{8,10},{10,8},{12,14},{14,12},{16,18},{18,... | collective-permute-start | bytes 393224 | tf_op jit(solution)/shard_map/ppermute | solution.py:216
  7.1 11.4 %collective-permute-start.4 = (f32[512,256]{1,0:T(8,128)S(1)}, f32[512,256]{1,0:T(8,128)S(1)}, u32[]{:S(2)}, u32[]{:S(2)}) collective-permute-start(f32[512,256]{1,0:T(8,128)S(1)} %maximum_maximum_fusion), channel_id=1, source_target_pairs={{0,10},{2,4},{8,2},{10,16},{16,26},{18,8},{24,18},{26,28},{28,22},... | collective-permute-start | bytes 1572872 | tf_op jit(solution)/shard_map/ppermute | solution.py:213
  11.3 12.7 %collective-permute-start.11 = (f32[512,256]{1,0:T(8,128)S(1)}, f32[512,256]{1,0:T(8,128)S(1)}, u32[]{:S(2)}, u32[]{:S(2)}) collective-permute-start(f32[512,256]{1,0:T(8,128)S(1)} %pad_maximum_fusion.refs_2_), channel_id=1, source_target_pairs={{0,10},{2,4},{8,2},{10,16},{16,26},{18,8},{24,18},{26,28},{28,22},... | collective-permute-start | bytes 1572872 | tf_op jit(solution)/shard_map/ppermute | solution.py:213
  18.5 10.5 %collective-permute-start.10 = (f32[512,256]{1,0:T(8,128)S(1)}, f32[512,256]{1,0:T(8,128)S(1)}, u32[]{:S(2)}, u32[]{:S(2)}) collective-permute-start(f32[512,256]{1,0:T(8,128)S(1)} %collective-permute-done.4.refs_2_), channel_id=1, source_target_pairs={{0,10},{2,4},{8,2},{10,16},{16,26},{18,8},{24,18},{26,28},{28,22},... | collective-permute-start | bytes 1572872 | tf_op jit(solution)/shard_map/ppermute | solution.py:213
  24.0 10.2 %collective-permute-start.13 = (f32[512,256]{1,0:T(8,128)S(1)}, f32[512,256]{1,0:T(8,128)S(1)}, u32[]{:S(2)}, u32[]{:S(2)}) collective-permute-start(f32[512,256]{1,0:T(8,128)S(1)} %collective-permute-done.11.refs_2_), channel_id=1, source_target_pairs={{0,10},{2,4},{8,2},{10,16},{16,26},{18,8},{24,18},{26,28},{28,22},... | collective-permute-start | bytes 1572872 | tf_op jit(solution)/shard_map/ppermute | solution.py:213
  29.0 11.4 %collective-permute-start.12 = (f32[512,256]{1,0:T(8,128)S(1)}, f32[512,256]{1,0:T(8,128)S(1)}, u32[]{:S(2)}, u32[]{:S(2)}) collective-permute-start(f32[512,256]{1,0:T(8,128)S(1)} %collective-permute-done.10.refs_2_), channel_id=1, source_target_pairs={{0,10},{2,4},{8,2},{10,16},{16,26},{18,8},{24,18},{26,28},{28,22},... | collective-permute-start | bytes 1572872 | tf_op jit(solution)/shard_map/ppermute | solution.py:213
  34.2 8.1 %collective-permute-start.14 = (f32[256,256]{1,0:T(8,128)S(1)}, f32[256,256]{1,0:T(8,128)S(1)}, u32[]{:S(2)}, u32[]{:S(2)}) collective-permute-start(f32[256,256]{1,0:T(8,128)S(1)} %get-tuple-element.117), channel_id=1, source_target_pairs={{0,10},{2,4},{8,2},{10,16},{16,26},{18,8},{24,18},{26,28},{28,22},... | collective-permute-start | bytes 786440 | tf_op jit(solution)/shard_map/ppermute | solution.py:213
  35.2 9.1 %collective-permute-start.15 = (f32[256,256]{1,0:T(8,128)S(1)}, f32[256,256]{1,0:T(8,128)S(1)}, u32[]{:S(2)}, u32[]{:S(2)}) collective-permute-start(f32[256,256]{1,0:T(8,128)S(1)} %get-tuple-element.118), channel_id=1, source_target_pairs={{0,10},{2,4},{8,2},{10,16},{16,26},{18,8},{24,18},{26,28},{28,22},... | collective-permute-start | bytes 786440 | tf_op jit(solution)/shard_map/ppermute | solution.py:213
  44.9 2.0 %collective-permute-start.16 = (f32[512,128]{1,0:T(8,128)S(1)}, f32[512,128]{1,0:T(8,128)S(1)}, u32[]{:S(2)}, u32[]{:S(2)}) collective-permute-start(f32[512,128]{1,0:T(8,128)S(1)} %pair_terms.22), channel_id=1, source_target_pairs={{0,2},{2,0},{4,6},{6,4},{8,10},{10,8},{12,14},{14,12},{16,18},{18,... | collective-permute-start | bytes 786440 | tf_op jit(solution)/shard_map/ppermute | solution.py:216
  46.9 8.7 %collective-permute-start.19 = (f32[512,128]{1,0:T(8,128)S(1)}, f32[512,128]{1,0:T(8,128)S(1)}, u32[]{:S(2)}, u32[]{:S(2)}) collective-permute-start(f32[512,128]{1,0:T(8,128)S(1)} %add.14), channel_id=1, source_target_pairs={{0,1},{1,0},{2,3},{3,2},{4,5},{5,4},{6,7},{7,6},{8,9},{9,8},{10,11... | collective-permute-start | bytes 786440 | tf_op jit(solution)/shard_map/ppermute | solution.py:275
  52.5 1.4 %collective-permute-start.17 = (f32[256,128]{1,0:T(8,128)S(1)}, f32[256,128]{1,0:T(8,128)S(1)}, u32[]{:S(2)}, u32[]{:S(2)}) collective-permute-start(f32[256,128]{1,0:T(8,128)S(1)} %get-tuple-element.115), channel_id=1, source_target_pairs={{0,2},{2,0},{4,6},{6,4},{8,10},{10,8},{12,14},{14,12},{16,18},{18,... | collective-permute-start | bytes 393224 | tf_op jit(solution)/shard_map/ppermute | solution.py:216
  52.6 1.5 %collective-permute-start.18 = (f32[256,128]{1,0:T(8,128)S(1)}, f32[256,128]{1,0:T(8,128)S(1)}, u32[]{:S(2)}, u32[]{:S(2)}) collective-permute-start(f32[256,128]{1,0:T(8,128)S(1)} %get-tuple-element.116), channel_id=1, source_target_pairs={{0,2},{2,0},{4,6},{6,4},{8,10},{10,8},{12,14},{14,12},{16,18},{18,... | collective-permute-start | bytes 393224 | tf_op jit(solution)/shard_map/ppermute | solution.py:216

commit v9 on v8

--- a/solution.py
+++ b/solution.py
@@ -261,6 +261,11 @@
     last = last or [flying[(total - 1) % 2] if total > 1 else scaled(first)]
     late = [here, *last] if total > 1 else last
 
+    def across(by):
+        return [
+            (b * replicas + r, (b ^ 1) * replicas + (r + by) % replicas) for b in range(blocks) for r in range(replicas)
+        ]
+
     theirs = acc
     for x in late[:-1] if mine_at else []:
         x, theirs = after((x, theirs))
@@ -270,9 +275,9 @@
     arrived = []
     for k in range(replicas - 1):
         at = k * 2 * share
-        received = other_core(pairs(feat, fac, [end], theirs, at, share))
-        part = pairs(feat, fac, [end], theirs, at + share, share) + received
-        arrived.append(lax.ppermute(part, "rep", [(r, (r + k + 1) % replicas) for r in range(replicas)]))
+        received = other_core(pairs(feat, fac, [end], theirs, at + share, share))
+        part = pairs(feat, fac, [end], theirs, at, share) + received
+        arrived.append(lax.ppermute(part, ("blk", "rep"), across(k + 1)))
         acc, part = after((acc, part))
     part = pairs(feat, fac, late, acc, mine_at, 2 * share, 0, mine)
     half = share // 2

time: 56.5 us -> 56 us (level)
  no operation moved by 1% of the time
where the time goes in v9:
time: 56 us; the launch traced here: 55.9 us
  Pallas kernels  30.5 us (54%)
  starting transfers between devices  18.5 us (33%)
  waiting for transfers between devices  4.27 us (8%)
  local copies, waits for them, and re-layouts  1.25 us (2%)
  other arithmetic  1.13 us (2%)
    pallas_call x12, Pallas kernels, call(): pl.pallas_call(kernel, in_specs=[IN_VMEM] * len(args), out_specs=jax.tree...  29.8 us
    ppermute x8, starting transfers between devices, ring(): return lax.ppermute(x, 'blk', moves)  13.1 us
    ppermute x11, starting transfers between devices, other_core(): return lax.ppermute(x, 'blk', [(b, b ^ 1) for b in range(blocks)])  3.7 us
    ppermute x11, waiting for transfers between devices, other_core(): return lax.ppermute(x, 'blk', [(b, b ^ 1) for b in range(blocks)])  2.35 us
    ppermute x1, starting transfers between devices, body(): arrived.append(lax.ppermute(part, ('blk', 'rep'), across(k + 1)))  1.72 us
    dynamic_slice x1, local copies, waits for them, and re-layouts, body(): lax.dynamic_slice_in_dim(x, rep * share, share)  1.15 us
  transfers between devices with their start and end apart: 20, of which 7 were waited for; matrix products, arithmetic and copies ran while one was open for 1% of the time, Pallas kernels for 53%

profile of v9, /device:TPU:0, one launch (start us, length us, event | category | flops | bytes accessed | tf_op | source)
XLA Modules:
  0.0 55.9 jit_solution(2313857280478355804)
XLA Ops:
  0.0 1.2 %constant_dynamic-slice_fusion = (f32[512,128]{1,0:T(8,128)S(1)}, f32[512,128]{1,0:T(8,128)S(1)}) fusion(f32[1024,128]{1,0:T(8,128)} %fac_ref, s32[]{:T(128)S(6)} %select_n.4, f32[1024,128]{1,0:T(8,128)} %feat_ref), kind=kLoop, calls=%fused_computation.11 | loop fusion | bytes 1048580 | tf_op jit(solution)/shard_map/dynamic_slice | solution.py:221
  1.2 2.5 %collective-permute-start.5 = (f32[512,256]{1,0:T(8,128)S(1)}, f32[512,256]{1,0:T(8,128)S(1)}, u32[]{:S(2)}, u32[]{:S(2)}) collective-permute-start(f32[512,256]{1,0:T(8,128)S(1)} %constant_dynamic-update-slice_fusion), channel_id=1, source_target_pairs={{0,10},{2,4},{8,2},{10,16},{16,26},{18,8},{24,18},{26,28},{28,22},... | collective-permute-start | bytes 1572872 | tf_op jit(solution)/shard_map/ppermute | solution.py:213
  3.7 0.3 own_rows.1
  4.1 0.7 %collective-permute-start = (f32[256,128]{1,0:T(8,128)S(1)}, f32[256,128]{1,0:T(8,128)S(1)}, u32[]{:S(2)}, u32[]{:S(2)}) collective-permute-start(f32[256,128]{1,0:T(8,128)S(1)} %get-tuple-element.64.refs_2_), channel_id=1, source_target_pairs={{0,2},{2,0},{4,6},{6,4},{8,10},{10,8},{12,14},{14,12},{16,18},{18,... | collective-permute-start | bytes 393224 | tf_op jit(solution)/shard_map/ppermute | solution.py:216
  4.8 0.1 collective-permute-start.1
  4.8 0.4 collective-permute-start.2
  5.3 0.1 collective-permute-start.3
  5.4 0.4 collective-permute-done.refs_4_
  5.8 0.4 collective-permute-start.6
  6.1 0.2 collective-permute-start.7
  6.3 0.0 collective-permute-done.2.refs_5_
  6.3 0.3 collective-permute-start.8
  6.6 0.0 collective-permute-done.3.refs_7_
  6.6 0.2 collective-permute-start.9
  6.9 0.2 collective-permute-done.6.refs_0_
  7.1 1.6 %collective-permute-start.4 = (f32[512,256]{1,0:T(8,128)S(1)}, f32[512,256]{1,0:T(8,128)S(1)}, u32[]{:S(2)}, u32[]{:S(2)}) collective-permute-start(f32[512,256]{1,0:T(8,128)S(1)} %maximum_maximum_fusion), channel_id=1, source_target_pairs={{0,10},{2,4},{8,2},{10,16},{16,26},{18,8},{24,18},{26,28},{28,22},... | collective-permute-start | bytes 1572872 | tf_op jit(solution)/shard_map/ppermute | solution.py:213
  8.7 0.0 collective-permute-done.7.refs_1_
  8.7 0.3 other_rows.1
  9.0 1.9 %pair_terms.12.refs_6_ = f32[1024,128]{1,0:T(8,128)S(1)} custom-call(bf16[2048,512]{1,0:T(8,128)(2,1)S(1)} %get-tuple-element.102.refs_0_, bf16[2048,512]{1,0:T(8,128)(2,1)S(1)} %get-tuple-element.103.refs_1_, f32[256,128]{1,0:T(8,128)S(1)} %get-tuple-element.68.refs_2_, f32[256,128]{1,0:T(8,128)S(1)} %get-tuple-element.69.refs_3_, ...), custom_call_target="tpu_custom_call" | custom-call | flops 1610612736 | bytes 4194304 | tf_op jit(solution)/shard_map/pair_terms/pallas_call | solution.py:25
  10.9 0.1 slice_multiply_fusion.1
  11.1 0.1 slice_multiply_fusion
  11.3 1.8 %collective-permute-start.11 = (f32[512,256]{1,0:T(8,128)S(1)}, f32[512,256]{1,0:T(8,128)S(1)}, u32[]{:S(2)}, u32[]{:S(2)}) collective-permute-start(f32[512,256]{1,0:T(8,128)S(1)} %pad_maximum_fusion.refs_2_), channel_id=1, source_target_pairs={{0,10},{2,4},{8,2},{10,16},{16,26},{18,8},{24,18},{26,28},{28,22},... | collective-permute-start | bytes 1572872 | tf_op jit(solution)/shard_map/ppermute | solution.py:213
  13.0 3.5 %pair_terms.13.refs_3_ = f32[2048,128]{1,0:T(8,128)S(1)} custom-call(bf16[2048,512]{1,0:T(8,128)(2,1)S(1)} %get-tuple-element.102.refs_0_, bf16[2048,512]{1,0:T(8,128)(2,1)S(1)} %get-tuple-element.103.refs_1_, f32[512,256]{1,0:T(8,128)S(1)} %pad_maximum_fusion.refs_2_), custom_call_target="tpu_custom_call" | custom-call | flops 3221225472 | bytes 4194304 | tf_op jit(solution)/shard_map/pair_terms/pallas_call | solution.py:25
  16.6 1.9 %pair_terms.14.refs_6_ = f32[1024,128]{1,0:T(8,128)S(1)} custom-call(bf16[2048,512]{1,0:T(8,128)(2,1)S(1)} %get-tuple-element.102.refs_0_, bf16[2048,512]{1,0:T(8,128)(2,1)S(1)} %get-tuple-element.103.refs_1_, f32[256,128]{1,0:T(8,128)S(1)} %get-tuple-element.64.refs_2_, f32[256,128]{1,0:T(8,128)S(1)} %get-tuple-element.66.refs_3_, ...), custom_call_target="tpu_custom_call", output_to_operand_aliasing={{}: (6, {})} | custom-call | flops 1610612736 | bytes 4194304 | tf_op jit(solution)/shard_map/pair_terms/pallas_call | solution.py:25
  18.5 1.8 %collective-permute-start.10 = (f32[512,256]{1,0:T(8,128)S(1)}, f32[512,256]{1,0:T(8,128)S(1)}, u32[]{:S(2)}, u32[]{:S(2)}) collective-permute-start(f32[512,256]{1,0:T(8,128)S(1)} %collective-permute-done.4.refs_2_), channel_id=1, source_target_pairs={{0,10},{2,4},{8,2},{10,16},{16,26},{18,8},{24,18},{26,28},{28,22},... | collective-permute-start | bytes 1572872 | tf_op jit(solution)/shard_map/ppermute | solution.py:213
  20.3 3.6 %pair_terms.15.refs_3_ = f32[2048,128]{1,0:T(8,128)S(1)} custom-call(bf16[2048,512]{1,0:T(8,128)(2,1)S(1)} %get-tuple-element.102.refs_0_, bf16[2048,512]{1,0:T(8,128)(2,1)S(1)} %get-tuple-element.103.refs_1_, f32[512,256]{1,0:T(8,128)S(1)} %collective-permute-done.4.refs_2_, f32[2048,128]{1,0:T(8,128)S(1)} %pair_terms.13.refs_3_), custom_call_target="tpu_custom_call", output_to_operand_aliasing={{}: (3, {})} | custom-call | flops 3221225472 | bytes 4194304 | tf_op jit(solution)/shard_map/pair_terms/pallas_call | solution.py:25
  24.0 1.4 %collective-permute-start.13 = (f32[512,256]{1,0:T(8,128)S(1)}, f32[512,256]{1,0:T(8,128)S(1)}, u32[]{:S(2)}, u32[]{:S(2)}) collective-permute-start(f32[512,256]{1,0:T(8,128)S(1)} %collective-permute-done.11.refs_2_), channel_id=1, source_target_pairs={{0,10},{2,4},{8,2},{10,16},{16,26},{18,8},{24,18},{26,28},{28,22},... | collective-permute-start | bytes 1572872 | tf_op jit(solution)/shard_map/ppermute | solution.py:213
  25.3 3.6 %pair_terms.16.refs_3_ = f32[2048,128]{1,0:T(8,128)S(1)} custom-call(bf16[2048,512]{1,0:T(8,128)(2,1)S(1)} %get-tuple-element.102.refs_0_, bf16[2048,512]{1,0:T(8,128)(2,1)S(1)} %get-tuple-element.103.refs_1_, f32[512,256]{1,0:T(8,128)S(1)} %collective-permute-done.11.refs_2_, f32[2048,128]{1,0:T(8,128)S(1)} %pair_terms.15.refs_3_), custom_call_target="tpu_custom_call", output_to_operand_aliasing={{}: (3, {})} | custom-call | flops 3221225472 | bytes 4194304 | tf_op jit(solution)/shard_map/pair_terms/pallas_call | solution.py:25
  29.0 1.6 %collective-permute-start.12 = (f32[512,256]{1,0:T(8,128)S(1)}, f32[512,256]{1,0:T(8,128)S(1)}, u32[]{:S(2)}, u32[]{:S(2)}) collective-permute-start(f32[512,256]{1,0:T(8,128)S(1)} %collective-permute-done.10.refs_2_), channel_id=1, source_target_pairs={{0,10},{2,4},{8,2},{10,16},{16,26},{18,8},{24,18},{26,28},{28,22},... | collective-permute-start | bytes 1572872 | tf_op jit(solution)/shard_map/ppermute | solution.py:213
  30.6 3.6 %pair_terms.17.refs_3_ = f32[2048,128]{1,0:T(8,128)S(1)} custom-call(bf16[2048,512]{1,0:T(8,128)(2,1)S(1)} %get-tuple-element.102.refs_0_, bf16[2048,512]{1,0:T(8,128)(2,1)S(1)} %get-tuple-element.103.refs_1_, f32[512,256]{1,0:T(8,128)S(1)} %collective-permute-done.10.refs_2_, f32[2048,128]{1,0:T(8,128)S(1)} %pair_terms.16.refs_3_), custom_call_target="tpu_custom_call", output_to_operand_aliasing={{}: (3, {})} | custom-call | flops 3221225472 | bytes 4194304 | tf_op jit(solution)/shard_map/pair_terms/pallas_call | solution.py:25
  34.2 0.9 %collective-permute-start.14 = (f32[256,256]{1,0:T(8,128)S(1)}, f32[256,256]{1,0:T(8,128)S(1)}, u32[]{:S(2)}, u32[]{:S(2)}) collective-permute-start(f32[256,256]{1,0:T(8,128)S(1)} %get-tuple-element.117), channel_id=1, source_target_pairs={{0,10},{2,4},{8,2},{10,16},{16,26},{18,8},{24,18},{26,28},{28,22},... | collective-permute-start | bytes 786440 | tf_op jit(solution)/shard_map/ppermute | solution.py:213
  35.2 1.6 %collective-permute-start.15 = (f32[256,256]{1,0:T(8,128)S(1)}, f32[256,256]{1,0:T(8,128)S(1)}, u32[]{:S(2)}, u32[]{:S(2)}) collective-permute-start(f32[256,256]{1,0:T(8,128)S(1)} %get-tuple-element.118), channel_id=1, source_target_pairs={{0,10},{2,4},{8,2},{10,16},{16,26},{18,8},{24,18},{26,28},{28,22},... | collective-permute-start | bytes 786440 | tf_op jit(solution)/shard_map/ppermute | solution.py:213
  36.8 3.6 %pair_terms.18.refs_3_.refs_5_ = f32[2048,128]{1,0:T(8,128)S(1)} custom-call(bf16[2048,512]{1,0:T(8,128)(2,1)S(1)} %get-tuple-element.102.refs_0_, bf16[2048,512]{1,0:T(8,128)(2,1)S(1)} %get-tuple-element.103.refs_1_, f32[512,256]{1,0:T(8,128)S(1)} %collective-permute-done.13.refs_2_, f32[2048,128]{1,0:T(8,128)S(1)} %pair_terms.17.refs_3_), custom_call_target="tpu_custom_call", output_to_operand_aliasing={{}: (3, {})} | custom-call | flops 3221225472 | bytes 4194304 | tf_op jit(solution)/shard_map/pair_terms/pallas_call | solution.py:25
  40.4 1.9 %pair_terms.19.refs_3_ = f32[1024,128]{1,0:T(8,128)S(1)} custom-call(bf16[2048,512]{1,0:T(8,128)(2,1)S(1)} %get-tuple-element.102.refs_0_, bf16[2048,512]{1,0:T(8,128)(2,1)S(1)} %get-tuple-element.103.refs_1_, f32[512,256]{1,0:T(8,128)S(1)} %collective-permute-done.12.refs_2_, f32[2048,128]{1,0:T(8,128)S(1)} %pair_terms.18.refs_3_.refs_5_), custom_call_target="tpu_custom_call" | custom-call | flops 1610612736 | bytes 4194304 | tf_op jit(solution)/shard_map/pair_terms/pallas_call | solution.py:25
  42.3 1.1 %pair_terms.20.refs_3_ = f32[1024,128]{1,0:T(8,128)S(1)} custom-call(bf16[2048,512]{1,0:T(8,128)(2,1)S(1)} %get-tuple-element.102.refs_0_, bf16[2048,512]{1,0:T(8,128)(2,1)S(1)} %get-tuple-element.103.refs_1_, f32[256,256]{1,0:T(8,128)S(1)} %collective-permute-done.14.refs_2_.refs_3_, f32[1024,128]{1,0:T(8,128)S(1)} %pair_terms.19.refs_3_), custom_call_target="tpu_custom_call", output_to_operand_aliasing={{}: (3, {})} | custom-call | flops 805306368 | bytes 4194304 | tf_op jit(solution)/shard_map/pair_terms/pallas_call | solution.py:25
  43.5 0.8 %collective-permute-done.15.refs_2_.refs_4_ = f32[256,256]{1,0:T(8,128)S(1)} collective-permute-done((f32[256,256]{1,0:T(8,128)S(1)}, f32[256,256]{1,0:T(8,128)S(1)}, u32[]{:S(2)}, u32[]{:S(2)}) %collective-permute-start.15) | collective-permute-done | bytes 262176 | tf_op jit(solution)/shard_map/ppermute | solution.py:213
  44.2 0.7 %pair_terms.22 = f32[512,128]{1,0:T(8,128)S(1)} custom-call(bf16[2048,512]{1,0:T(8,128)(2,1)S(1)} %get-tuple-element.102.refs_0_, bf16[2048,512]{1,0:T(8,128)(2,1)S(1)} %get-tuple-element.103.refs_1_, f32[256,256]{1,0:T(8,128)S(1)} %collective-permute-done.15.refs_2_.refs_4_, f32[1024,128]{1,0:T(8,128)S(1)} %pair_terms.20.refs_3_), custom_call_target="tpu_custom_call" | custom-call | flops 402653184 | bytes 4194304 | tf_op jit(solution)/shard_map/pair_terms/pallas_call | solution.py:25
  44.9 0.8 %collective-permute-start.16 = (f32[512,128]{1,0:T(8,128)S(1)}, f32[512,128]{1,0:T(8,128)S(1)}, u32[]{:S(2)}, u32[]{:S(2)}) collective-permute-start(f32[512,128]{1,0:T(8,128)S(1)} %pair_terms.22), channel_id=1, source_target_pairs={{0,2},{2,0},{4,6},{6,4},{8,10},{10,8},{12,14},{14,12},{16,18},{18,... | collective-permute-start | bytes 786440 | tf_op jit(solution)/shard_map/ppermute | solution.py:216
  45.7 0.7 %pair_terms.21 = f32[512,128]{1,0:T(8,128)S(1)} custom-call(bf16[2048,512]{1,0:T(8,128)(2,1)S(1)} %get-tuple-element.102.refs_0_, bf16[2048,512]{1,0:T(8,128)(2,1)S(1)} %get-tuple-element.103.refs_1_, f32[256,256]{1,0:T(8,128)S(1)} %collective-permute-done.15.refs_2_.refs_4_, f32[1024,128]{1,0:T(8,128)S(1)} %pair_terms.20.refs_3_), custom_call_target="tpu_custom_call" | custom-call | flops 402653184 | bytes 4194304 | tf_op jit(solution)/shard_map/pair_terms/pallas_call | solution.py:25
  46.4 0.5 collective-permute-done.16
  46.9 1.7 %collective-permute-start.19 = (f32[512,128]{1,0:T(8,128)S(1)}, f32[512,128]{1,0:T(8,128)S(1)}, u32[]{:S(2)}, u32[]{:S(2)}) collective-permute-start(f32[512,128]{1,0:T(8,128)S(1)} %add.14), channel_id=1, source_target_pairs={{0,3},{1,2},{2,1},{3,0},{4,7},{5,6},{6,5},{7,4},{8,11},{9,10},{10,... | collective-permute-start | bytes 786440 | tf_op jit(solution)/shard_map/ppermute | solution.py:280
  48.6 3.5 %pair_terms.23 = f32[1024,128]{1,0:T(8,128)S(1)} custom-call(bf16[2048,512]{1,0:T(8,128)(2,1)S(1)} %get-tuple-element.102.refs_0_, bf16[2048,512]{1,0:T(8,128)(2,1)S(1)} %get-tuple-element.103.refs_1_, f32[512,256]{1,0:T(8,128)S(1)} %collective-permute-done.12.refs_2_, f32[256,256]{1,0:T(8,128)S(1)} %collective-permute-done.14.refs_2_.refs_3_, ...), custom_call_target="tpu_custom_call" | custom-call | flops 3221225472 | bytes 4194304 | tf_op jit(solution)/shard_map/pair_terms/pallas_call | solution.py:25
  52.2 0.4 collective-permute-start.17
  52.7 0.1 collective-permute-start.18
  52.8 0.8 %collective-permute-done.17 = f32[256,128]{1,0:T(8,128)S(1)} collective-permute-done((f32[256,128]{1,0:T(8,128)S(1)}, f32[256,128]{1,0:T(8,128)S(1)}, u32[]{:S(2)}, u32[]{:S(2)}) %collective-permute-start.17) | collective-permute-done | bytes 131104 | tf_op jit(solution)/shard_map/ppermute | solution.py:216
  53.6 0.4 collective-permute-done.18
  54.0 1.1 %collective-permute-done.19 = f32[512,128]{1,0:T(8,128)S(1)} collective-permute-done((f32[512,128]{1,0:T(8,128)S(1)}, f32[512,128]{1,0:T(8,128)S(1)}, u32[]{:S(2)}, u32[]{:S(2)}) %collective-permute-start.19) | collective-permute-done | bytes 262176 | tf_op jit(solution)/shard_map/ppermute | solution.py:280
  55.1 0.7 %fusion.1 = f32[512,128]{1,0:T(8,128)} fusion(f32[512,128]{1,0:T(8,128)S(1)} %collective-permute-done.19, f32[1024,128]{1,0:T(8,128)S(1)} %pair_terms.23, f32[256,128]{1,0:T(8,128)S(1)} %collective-permute-done.18, f32[256,128]{1,0:T(8,128)S(1)} %collective-permute-done.17), kind=kLoop, calls=%fused_computation.4 | loop fusion | flops 262144 | bytes 1048576 | tf_op jit(solution)/shard_map/mul | solution.py:287
  (22 shorter events, 0.2 us)
Async XLA Ops:
  0.0 3.7 %copy-start.1 = (f32[1024,128]{1,0:T(8,128)S(1)}, f32[1024,128]{1,0:T(8,128)}, u32[]{:S(2)}) copy-start(f32[1024,128]{1,0:T(8,128)} %fac_ref) | copy-start | bytes 1572868
  0.0 3.7 %copy-start = (f32[1024,128]{1,0:T(8,128)S(1)}, f32[1024,128]{1,0:T(8,128)}, u32[]{:S(2)}) copy-start(f32[1024,128]{1,0:T(8,128)} %feat_ref) | copy-start | bytes 1572868
  1.2 9.7 %collective-permute-start.5 = (f32[512,256]{1,0:T(8,128)S(1)}, f32[512,256]{1,0:T(8,128)S(1)}, u32[]{:S(2)}, u32[]{:S(2)}) collective-permute-start(f32[512,256]{1,0:T(8,128)S(1)} %constant_dynamic-update-slice_fusion), channel_id=1, source_target_pairs={{0,10},{2,4},{8,2},{10,16},{16,26},{18,8},{24,18},{26,28},{28,22},... | collective-permute-start | bytes 1572872 | tf_op jit(solution)/shard_map/ppermute | solution.py:213
  4.1 1.7 %collective-permute-start = (f32[256,128]{1,0:T(8,128)S(1)}, f32[256,128]{1,0:T(8,128)S(1)}, u32[]{:S(2)}, u32[]{:S(2)}) collective-permute-start(f32[256,128]{1,0:T(8,128)S(1)} %get-tuple-element.64.refs_2_), channel_id=1, source_target_pairs={{0,2},{2,0},{4,6},{6,4},{8,10},{10,8},{12,14},{14,12},{16,18},{18,... | collective-permute-start | bytes 393224 | tf_op jit(solution)/shard_map/ppermute | solution.py:216
  4.8 1.4 %collective-permute-start.1 = (f32[256,128]{1,0:T(8,128)S(1)}, f32[256,128]{1,0:T(8,128)S(1)}, u32[]{:S(2)}, u32[]{:S(2)}) collective-permute-start(f32[256,128]{1,0:T(8,128)S(1)} %get-tuple-element.65.refs_4_), channel_id=1, source_target_pairs={{0,2},{2,0},{4,6},{6,4},{8,10},{10,8},{12,14},{14,12},{16,18},{18,... | collective-permute-start | bytes 393224 | tf_op jit(solution)/shard_map/ppermute | solution.py:216
  4.8 1.5 %collective-permute-start.2 = (f32[256,128]{1,0:T(8,128)S(1)}, f32[256,128]{1,0:T(8,128)S(1)}, u32[]{:S(2)}, u32[]{:S(2)}) collective-permute-start(f32[256,128]{1,0:T(8,128)S(1)} %get-tuple-element.66.refs_3_), channel_id=1, source_target_pairs={{0,2},{2,0},{4,6},{6,4},{8,10},{10,8},{12,14},{14,12},{16,18},{18,... | collective-permute-start | bytes 393224 | tf_op jit(solution)/shard_map/ppermute | solution.py:216
  5.3 1.4 %collective-permute-start.3 = (f32[256,128]{1,0:T(8,128)S(1)}, f32[256,128]{1,0:T(8,128)S(1)}, u32[]{:S(2)}, u32[]{:S(2)}) collective-permute-start(f32[256,128]{1,0:T(8,128)S(1)} %get-tuple-element.67.refs_5_), channel_id=1, source_target_pairs={{0,2},{2,0},{4,6},{6,4},{8,10},{10,8},{12,14},{14,12},{16,18},{18,... | collective-permute-start | bytes 393224 | tf_op jit(solution)/shard_map/ppermute | solution.py:216
  5.8 1.3 %collective-permute-start.6 = (f32[256,128]{1,0:T(8,128)S(1)}, f32[256,128]{1,0:T(8,128)S(1)}, u32[]{:S(2)}, u32[]{:S(2)}) collective-permute-start(f32[256,128]{1,0:T(8,128)S(1)} %get-tuple-element.68.refs_2_), channel_id=1, source_target_pairs={{0,2},{2,0},{4,6},{6,4},{8,10},{10,8},{12,14},{14,12},{16,18},{18,... | collective-permute-start | bytes 393224 | tf_op jit(solution)/shard_map/ppermute | solution.py:216
  6.1 2.6 %collective-permute-start.7 = (f32[256,128]{1,0:T(8,128)S(1)}, f32[256,128]{1,0:T(8,128)S(1)}, u32[]{:S(2)}, u32[]{:S(2)}) collective-permute-start(f32[256,128]{1,0:T(8,128)S(1)} %get-tuple-element.69.refs_3_), channel_id=1, source_target_pairs={{0,2},{2,0},{4,6},{6,4},{8,10},{10,8},{12,14},{14,12},{16,18},{18,... | collective-permute-start | bytes 393224 | tf_op jit(solution)/shard_map/ppermute | solution.py:216
  6.3 2.4 %collective-permute-start.8 = (f32[256,128]{1,0:T(8,128)S(1)}, f32[256,128]{1,0:T(8,128)S(1)}, u32[]{:S(2)}, u32[]{:S(2)}) collective-permute-start(f32[256,128]{1,0:T(8,128)S(1)} %get-tuple-element.70.refs_4_), channel_id=1, source_target_pairs={{0,2},{2,0},{4,6},{6,4},{8,10},{10,8},{12,14},{14,12},{16,18},{18,... | collective-permute-start | bytes 393224 | tf_op jit(solution)/shard_map/ppermute | solution.py:216
  6.6 2.1 %collective-permute-start.9 = (f32[256,128]{1,0:T(8,128)S(1)}, f32[256,128]{1,0:T(8,128)S(1)}, u32[]{:S(2)}, u32[]{:S(2)}) collective-permute-start(f32[256,128]{1,0:T(8,128)S(1)} %get-tuple-element.71.refs_5_), channel_id=1, source_target_pairs={{0,2},{2,0},{4,6},{6,4},{8,10},{10,8},{12,14},{14,12},{16,18},{18,... | collective-permute-start | bytes 393224 | tf_op jit(solution)/shard_map/ppermute | solution.py:216
  7.1 11.4 %collective-permute-start.4 = (f32[512,256]{1,0:T(8,128)S(1)}, f32[512,256]{1,0:T(8,128)S(1)}, u32[]{:S(2)}, u32[]{:S(2)}) collective-permute-start(f32[512,256]{1,0:T(8,128)S(1)} %maximum_maximum_fusion), channel_id=1, source_target_pairs={{0,10},{2,4},{8,2},{10,16},{16,26},{18,8},{24,18},{26,28},{28,22},... | collective-permute-start | bytes 1572872 | tf_op jit(solution)/shard_map/ppermute | solution.py:213
  11.3 12.7 %collective-permute-start.11 = (f32[512,256]{1,0:T(8,128)S(1)}, f32[512,256]{1,0:T(8,128)S(1)}, u32[]{:S(2)}, u32[]{:S(2)}) collective-permute-start(f32[512,256]{1,0:T(8,128)S(1)} %pad_maximum_fusion.refs_2_), channel_id=1, source_target_pairs={{0,10},{2,4},{8,2},{10,16},{16,26},{18,8},{24,18},{26,28},{28,22},... | collective-permute-start | bytes 1572872 | tf_op jit(solution)/shard_map/ppermute | solution.py:213
  18.5 10.5 %collective-permute-start.10 = (f32[512,256]{1,0:T(8,128)S(1)}, f32[512,256]{1,0:T(8,128)S(1)}, u32[]{:S(2)}, u32[]{:S(2)}) collective-permute-start(f32[512,256]{1,0:T(8,128)S(1)} %collective-permute-done.4.refs_2_), channel_id=1, source_target_pairs={{0,10},{2,4},{8,2},{10,16},{16,26},{18,8},{24,18},{26,28},{28,22},... | collective-permute-start | bytes 1572872 | tf_op jit(solution)/shard_map/ppermute | solution.py:213
  24.0 10.2 %collective-permute-start.13 = (f32[512,256]{1,0:T(8,128)S(1)}, f32[512,256]{1,0:T(8,128)S(1)}, u32[]{:S(2)}, u32[]{:S(2)}) collective-permute-start(f32[512,256]{1,0:T(8,128)S(1)} %collective-permute-done.11.refs_2_), channel_id=1, source_target_pairs={{0,10},{2,4},{8,2},{10,16},{16,26},{18,8},{24,18},{26,28},{28,22},... | collective-permute-start | bytes 1572872 | tf_op jit(solution)/shard_map/ppermute | solution.py:213
  29.0 11.4 %collective-permute-start.12 = (f32[512,256]{1,0:T(8,128)S(1)}, f32[512,256]{1,0:T(8,128)S(1)}, u32[]{:S(2)}, u32[]{:S(2)}) collective-permute-start(f32[512,256]{1,0:T(8,128)S(1)} %collective-permute-done.10.refs_2_), channel_id=1, source_target_pairs={{0,10},{2,4},{8,2},{10,16},{16,26},{18,8},{24,18},{26,28},{28,22},... | collective-permute-start | bytes 1572872 | tf_op jit(solution)/shard_map/ppermute | solution.py:213
  34.2 8.1 %collective-permute-start.14 = (f32[256,256]{1,0:T(8,128)S(1)}, f32[256,256]{1,0:T(8,128)S(1)}, u32[]{:S(2)}, u32[]{:S(2)}) collective-permute-start(f32[256,256]{1,0:T(8,128)S(1)} %get-tuple-element.117), channel_id=1, source_target_pairs={{0,10},{2,4},{8,2},{10,16},{16,26},{18,8},{24,18},{26,28},{28,22},... | collective-permute-start | bytes 786440 | tf_op jit(solution)/shard_map/ppermute | solution.py:213
  35.2 9.1 %collective-permute-start.15 = (f32[256,256]{1,0:T(8,128)S(1)}, f32[256,256]{1,0:T(8,128)S(1)}, u32[]{:S(2)}, u32[]{:S(2)}) collective-permute-start(f32[256,256]{1,0:T(8,128)S(1)} %get-tuple-element.118), channel_id=1, source_target_pairs={{0,10},{2,4},{8,2},{10,16},{16,26},{18,8},{24,18},{26,28},{28,22},... | collective-permute-start | bytes 786440 | tf_op jit(solution)/shard_map/ppermute | solution.py:213
  44.9 2.0 %collective-permute-start.16 = (f32[512,128]{1,0:T(8,128)S(1)}, f32[512,128]{1,0:T(8,128)S(1)}, u32[]{:S(2)}, u32[]{:S(2)}) collective-permute-start(f32[512,128]{1,0:T(8,128)S(1)} %pair_terms.22), channel_id=1, source_target_pairs={{0,2},{2,0},{4,6},{6,4},{8,10},{10,8},{12,14},{14,12},{16,18},{18,... | collective-permute-start | bytes 786440 | tf_op jit(solution)/shard_map/ppermute | solution.py:216
  46.9 8.2 %collective-permute-start.19 = (f32[512,128]{1,0:T(8,128)S(1)}, f32[512,128]{1,0:T(8,128)S(1)}, u32[]{:S(2)}, u32[]{:S(2)}) collective-permute-start(f32[512,128]{1,0:T(8,128)S(1)} %add.14), channel_id=1, source_target_pairs={{0,3},{1,2},{2,1},{3,0},{4,7},{5,6},{6,5},{7,4},{8,11},{9,10},{10,... | collective-permute-start | bytes 786440 | tf_op jit(solution)/shard_map/ppermute | solution.py:280
  52.2 1.4 %collective-permute-start.17 = (f32[256,128]{1,0:T(8,128)S(1)}, f32[256,128]{1,0:T(8,128)S(1)}, u32[]{:S(2)}, u32[]{:S(2)}) collective-permute-start(f32[256,128]{1,0:T(8,128)S(1)} %get-tuple-element.115), channel_id=1, source_target_pairs={{0,2},{2,0},{4,6},{6,4},{8,10},{10,8},{12,14},{14,12},{16,18},{18,... | collective-permute-start | bytes 393224 | tf_op jit(solution)/shard_map/ppermute | solution.py:216
  52.7 1.3 %collective-permute-start.18 = (f32[256,128]{1,0:T(8,128)S(1)}, f32[256,128]{1,0:T(8,128)S(1)}, u32[]{:S(2)}, u32[]{:S(2)}) collective-permute-start(f32[256,128]{1,0:T(8,128)S(1)} %get-tuple-element.116), channel_id=1, source_target_pairs={{0,2},{2,0},{4,6},{6,4},{8,10},{10,8},{12,14},{14,12},{16,18},{18,... | collective-permute-start | bytes 393224 | tf_op jit(solution)/shard_map/ppermute | solution.py:216

commit v10 on v9

--- a/solution.py
+++ b/solution.py
@@ -253,7 +253,7 @@
                 flying[step % 2] = ring(here)
         if step + 2 < total:
             acc = pairs(feat, fac, [here], acc)
-        if step == 0:
+        if step == min(3, total - 2):
             acc, mine = after((acc, mine))
             mine = pairs(feat, fac, own_block[early:], mine, mine_at, 2 * share, mine_at)
     if total < 2:

time: 56 us -> 56.2 us (level)
  starting transfers between devices: 18.5 us -> 19.3 us
    ppermute x8, starting transfers between devices: 13.1 us -> 14.4 us  [ring(): return lax.ppermute(x, 'blk', moves)]
    ppermute x8, waiting for transfers between devices: 0.81 us -> 0.02 us  [ring(): return lax.ppermute(x, 'blk', moves)]
  transfers between devices with their start and end apart: 20 -> 20, of which waited for: 7 -> 6; matrix products, arithmetic and copies ran while one was open for 1% -> 1% of each run, Pallas kernels for 53% -> 53%
where the time goes in v10:
time: 56.2 us; the launch traced here: 56.1 us
  Pallas kernels  30.5 us (54%)
  starting transfers between devices  19.3 us (34%)
  waiting for transfers between devices  3.72 us (7%)
  local copies, waits for them, and re-layouts  1.25 us (2%)
  other arithmetic  1.13 us (2%)
    pallas_call x12, Pallas kernels, call(): pl.pallas_call(kernel, in_specs=[IN_VMEM] * len(args), out_specs=jax.tree...  29.8 us
    ppermute x8, starting transfers between devices, ring(): return lax.ppermute(x, 'blk', moves)  14.4 us
    ppermute x11, starting transfers between devices, other_core(): return lax.ppermute(x, 'blk', [(b, b ^ 1) for b in range(blocks)])  3.29 us
    ppermute x11, waiting for transfers between devices, other_core(): return lax.ppermute(x, 'blk', [(b, b ^ 1) for b in range(blocks)])  2.4 us
    ppermute x1, starting transfers between devices, body(): arrived.append(lax.ppermute(part, ('blk', 'rep'), across(k + 1)))  1.57 us
    ppermute x1, waiting for transfers between devices, body(): arrived.append(lax.ppermute(part, ('blk', 'rep'), across(k + 1)))  1.3 us
    dynamic_slice x1, local copies, waits for them, and re-layouts, body(): lax.dynamic_slice_in_dim(x, rep * share, share)  1.15 us
  transfers between devices with their start and end apart: 20, of which 6 were waited for; matrix products, arithmetic and copies ran while one was open for 1% of the time, Pallas kernels for 53%

profile of v10, /device:TPU:0, one launch (start us, length us, event | category | flops | bytes accessed | tf_op | source)
XLA Modules:
  0.0 56.1 jit_solution(17227214800277289763)
XLA Ops:
  0.0 1.2 %constant_dynamic-slice_fusion = (f32[512,128]{1,0:T(8,128)S(1)}, f32[512,128]{1,0:T(8,128)S(1)}) fusion(f32[1024,128]{1,0:T(8,128)} %fac_ref, s32[]{:T(128)S(6)} %select_n.4, f32[1024,128]{1,0:T(8,128)} %feat_ref), kind=kLoop, calls=%fused_computation.11 | loop fusion | bytes 1048580 | tf_op jit(solution)/shard_map/dynamic_slice | solution.py:221
  1.2 2.5 %collective-permute-start.5 = (f32[512,256]{1,0:T(8,128)S(1)}, f32[512,256]{1,0:T(8,128)S(1)}, u32[]{:S(2)}, u32[]{:S(2)}) collective-permute-start(f32[512,256]{1,0:T(8,128)S(1)} %constant_dynamic-update-slice_fusion), channel_id=1, source_target_pairs={{0,10},{2,4},{8,2},{10,16},{16,26},{18,8},{24,18},{26,28},{28,22},... | collective-permute-start | bytes 1572872 | tf_op jit(solution)/shard_map/ppermute | solution.py:213
  3.7 0.3 own_rows.1
  4.1 0.7 %collective-permute-start = (f32[256,128]{1,0:T(8,128)S(1)}, f32[256,128]{1,0:T(8,128)S(1)}, u32[]{:S(2)}, u32[]{:S(2)}) collective-permute-start(f32[256,128]{1,0:T(8,128)S(1)} %get-tuple-element.64.refs_2_), channel_id=1, source_target_pairs={{0,2},{2,0},{4,6},{6,4},{8,10},{10,8},{12,14},{14,12},{16,18},{18,... | collective-permute-start | bytes 393224 | tf_op jit(solution)/shard_map/ppermute | solution.py:216
  4.8 0.1 collective-permute-start.1
  4.8 0.4 collective-permute-start.2
  5.3 0.1 collective-permute-start.3
  5.4 0.4 collective-permute-done.refs_4_
  5.8 0.4 collective-permute-start.6
  6.1 0.2 collective-permute-start.7
  6.3 0.0 collective-permute-done.2.refs_5_
  6.3 0.3 collective-permute-start.8
  6.6 0.2 collective-permute-start.9
  6.9 0.2 collective-permute-done.6.refs_0_
  7.1 1.6 %collective-permute-start.4 = (f32[512,256]{1,0:T(8,128)S(1)}, f32[512,256]{1,0:T(8,128)S(1)}, u32[]{:S(2)}, u32[]{:S(2)}) collective-permute-start(f32[512,256]{1,0:T(8,128)S(1)} %maximum_maximum_fusion), channel_id=1, source_target_pairs={{0,10},{2,4},{8,2},{10,16},{16,26},{18,8},{24,18},{26,28},{28,22},... | collective-permute-start | bytes 1572872 | tf_op jit(solution)/shard_map/ppermute | solution.py:213
  8.7 0.0 collective-permute-done.7.refs_1_
  8.7 0.0 collective-permute-done.8.refs_2_
  8.7 0.0 collective-permute-done.9.refs_3_
  8.7 0.3 other_rows.1
  9.0 1.9 %pair_terms.12.refs_6_ = f32[1024,128]{1,0:T(8,128)S(1)} custom-call(bf16[2048,512]{1,0:T(8,128)(2,1)S(1)} %get-tuple-element.102.refs_0_, bf16[2048,512]{1,0:T(8,128)(2,1)S(1)} %get-tuple-element.103.refs_1_, f32[256,128]{1,0:T(8,128)S(1)} %get-tuple-element.68.refs_2_, f32[256,128]{1,0:T(8,128)S(1)} %get-tuple-element.69.refs_3_, ...), custom_call_target="tpu_custom_call" | custom-call | flops 1610612736 | bytes 4194304 | tf_op jit(solution)/shard_map/pair_terms/pallas_call | solution.py:25
  10.9 0.1 slice_multiply_fusion.1
  11.1 0.1 slice_multiply_fusion
  11.3 1.8 %collective-permute-start.11 = (f32[512,256]{1,0:T(8,128)S(1)}, f32[512,256]{1,0:T(8,128)S(1)}, u32[]{:S(2)}, u32[]{:S(2)}) collective-permute-start(f32[512,256]{1,0:T(8,128)S(1)} %pad_maximum_fusion.refs_2_), channel_id=1, source_target_pairs={{0,10},{2,4},{8,2},{10,16},{16,26},{18,8},{24,18},{26,28},{28,22},... | collective-permute-start | bytes 1572872 | tf_op jit(solution)/shard_map/ppermute | solution.py:213
  13.0 3.5 %pair_terms.13.refs_3_ = f32[2048,128]{1,0:T(8,128)S(1)} custom-call(bf16[2048,512]{1,0:T(8,128)(2,1)S(1)} %get-tuple-element.102.refs_0_, bf16[2048,512]{1,0:T(8,128)(2,1)S(1)} %get-tuple-element.103.refs_1_, f32[512,256]{1,0:T(8,128)S(1)} %pad_maximum_fusion.refs_2_), custom_call_target="tpu_custom_call" | custom-call | flops 3221225472 | bytes 4194304 | tf_op jit(solution)/shard_map/pair_terms/pallas_call | solution.py:25
  16.6 1.7 %collective-permute-start.10 = (f32[512,256]{1,0:T(8,128)S(1)}, f32[512,256]{1,0:T(8,128)S(1)}, u32[]{:S(2)}, u32[]{:S(2)}) collective-permute-start(f32[512,256]{1,0:T(8,128)S(1)} %collective-permute-done.4.refs_2_), channel_id=1, source_target_pairs={{0,10},{2,4},{8,2},{10,16},{16,26},{18,8},{24,18},{26,28},{28,22},... | collective-permute-start | bytes 1572872 | tf_op jit(solution)/shard_map/ppermute | solution.py:213
  18.2 3.6 %pair_terms.14.refs_3_ = f32[2048,128]{1,0:T(8,128)S(1)} custom-call(bf16[2048,512]{1,0:T(8,128)(2,1)S(1)} %get-tuple-element.102.refs_0_, bf16[2048,512]{1,0:T(8,128)(2,1)S(1)} %get-tuple-element.103.refs_1_, f32[512,256]{1,0:T(8,128)S(1)} %collective-permute-done.4.refs_2_, f32[2048,128]{1,0:T(8,128)S(1)} %pair_terms.13.refs_3_), custom_call_target="tpu_custom_call", output_to_operand_aliasing={{}: (3, {})} | custom-call | flops 3221225472 | bytes 4194304 | tf_op jit(solution)/shard_map/pair_terms/pallas_call | solution.py:25
  21.9 2.0 %collective-permute-start.13 = (f32[512,256]{1,0:T(8,128)S(1)}, f32[512,256]{1,0:T(8,128)S(1)}, u32[]{:S(2)}, u32[]{:S(2)}) collective-permute-start(f32[512,256]{1,0:T(8,128)S(1)} %collective-permute-done.11.refs_2_), channel_id=1, source_target_pairs={{0,10},{2,4},{8,2},{10,16},{16,26},{18,8},{24,18},{26,28},{28,22},... | collective-permute-start | bytes 1572872 | tf_op jit(solution)/shard_map/ppermute | solution.py:213
  23.9 3.6 %pair_terms.15.refs_3_ = f32[2048,128]{1,0:T(8,128)S(1)} custom-call(bf16[2048,512]{1,0:T(8,128)(2,1)S(1)} %get-tuple-element.102.refs_0_, bf16[2048,512]{1,0:T(8,128)(2,1)S(1)} %get-tuple-element.103.refs_1_, f32[512,256]{1,0:T(8,128)S(1)} %collective-permute-done.11.refs_2_, f32[2048,128]{1,0:T(8,128)S(1)} %pair_terms.14.refs_3_), custom_call_target="tpu_custom_call", output_to_operand_aliasing={{}: (3, {})} | custom-call | flops 3221225472 | bytes 4194304 | tf_op jit(solution)/shard_map/pair_terms/pallas_call | solution.py:25
  27.5 2.0 %collective-permute-start.12 = (f32[512,256]{1,0:T(8,128)S(1)}, f32[512,256]{1,0:T(8,128)S(1)}, u32[]{:S(2)}, u32[]{:S(2)}) collective-permute-start(f32[512,256]{1,0:T(8,128)S(1)} %collective-permute-done.10.refs_2_), channel_id=1, source_target_pairs={{0,10},{2,4},{8,2},{10,16},{16,26},{18,8},{24,18},{26,28},{28,22},... | collective-permute-start | bytes 1572872 | tf_op jit(solution)/shard_map/ppermute | solution.py:213
  29.5 3.6 %pair_terms.16.refs_3_ = f32[2048,128]{1,0:T(8,128)S(1)} custom-call(bf16[2048,512]{1,0:T(8,128)(2,1)S(1)} %get-tuple-element.102.refs_0_, bf16[2048,512]{1,0:T(8,128)(2,1)S(1)} %get-tuple-element.103.refs_1_, f32[512,256]{1,0:T(8,128)S(1)} %collective-permute-done.10.refs_2_, f32[2048,128]{1,0:T(8,128)S(1)} %pair_terms.15.refs_3_), custom_call_target="tpu_custom_call", output_to_operand_aliasing={{}: (3, {})} | custom-call | flops 3221225472 | bytes 4194304 | tf_op jit(solution)/shard_map/pair_terms/pallas_call | solution.py:25
  33.1 1.9 %pair_terms.17.refs_6_ = f32[1024,128]{1,0:T(8,128)S(1)} custom-call(bf16[2048,512]{1,0:T(8,128)(2,1)S(1)} %get-tuple-element.102.refs_0_, bf16[2048,512]{1,0:T(8,128)(2,1)S(1)} %get-tuple-element.103.refs_1_, f32[256,128]{1,0:T(8,128)S(1)} %get-tuple-element.64.refs_2_, f32[256,128]{1,0:T(8,128)S(1)} %get-tuple-element.66.refs_3_, ...), custom_call_target="tpu_custom_call", output_to_operand_aliasing={{}: (6, {})} | custom-call | flops 1610612736 | bytes 4194304 | tf_op jit(solution)/shard_map/pair_terms/pallas_call | solution.py:25
  35.1 1.6 %collective-permute-start.14 = (f32[256,256]{1,0:T(8,128)S(1)}, f32[256,256]{1,0:T(8,128)S(1)}, u32[]{:S(2)}, u32[]{:S(2)}) collective-permute-start(f32[256,256]{1,0:T(8,128)S(1)} %get-tuple-element.117), channel_id=1, source_target_pairs={{0,10},{2,4},{8,2},{10,16},{16,26},{18,8},{24,18},{26,28},{28,22},... | collective-permute-start | bytes 786440 | tf_op jit(solution)/shard_map/ppermute | solution.py:213
  36.7 1.3 %collective-permute-start.15 = (f32[256,256]{1,0:T(8,128)S(1)}, f32[256,256]{1,0:T(8,128)S(1)}, u32[]{:S(2)}, u32[]{:S(2)}) collective-permute-start(f32[256,256]{1,0:T(8,128)S(1)} %get-tuple-element.118), channel_id=1, source_target_pairs={{0,10},{2,4},{8,2},{10,16},{16,26},{18,8},{24,18},{26,28},{28,22},... | collective-permute-start | bytes 786440 | tf_op jit(solution)/shard_map/ppermute | solution.py:213
  38.0 3.6 %pair_terms.18.refs_3_.refs_5_ = f32[2048,128]{1,0:T(8,128)S(1)} custom-call(bf16[2048,512]{1,0:T(8,128)(2,1)S(1)} %get-tuple-element.102.refs_0_, bf16[2048,512]{1,0:T(8,128)(2,1)S(1)} %get-tuple-element.103.refs_1_, f32[512,256]{1,0:T(8,128)S(1)} %collective-permute-done.13.refs_2_, f32[2048,128]{1,0:T(8,128)S(1)} %pair_terms.16.refs_3_), custom_call_target="tpu_custom_call", output_to_operand_aliasing={{}: (3, {})} | custom-call | flops 3221225472 | bytes 4194304 | tf_op jit(solution)/shard_map/pair_terms/pallas_call | solution.py:25
  41.7 1.9 %pair_terms.19.refs_3_ = f32[1024,128]{1,0:T(8,128)S(1)} custom-call(bf16[2048,512]{1,0:T(8,128)(2,1)S(1)} %get-tuple-element.102.refs_0_, bf16[2048,512]{1,0:T(8,128)(2,1)S(1)} %get-tuple-element.103.refs_1_, f32[512,256]{1,0:T(8,128)S(1)} %collective-permute-done.12.refs_2_, f32[2048,128]{1,0:T(8,128)S(1)} %pair_terms.18.refs_3_.refs_5_), custom_call_target="tpu_custom_call" | custom-call | flops 1610612736 | bytes 4194304 | tf_op jit(solution)/shard_map/pair_terms/pallas_call | solution.py:25
  43.6 1.1 %pair_terms.20.refs_3_ = f32[1024,128]{1,0:T(8,128)S(1)} custom-call(bf16[2048,512]{1,0:T(8,128)(2,1)S(1)} %get-tuple-element.102.refs_0_, bf16[2048,512]{1,0:T(8,128)(2,1)S(1)} %get-tuple-element.103.refs_1_, f32[256,256]{1,0:T(8,128)S(1)} %collective-permute-done.14.refs_2_.refs_3_, f32[1024,128]{1,0:T(8,128)S(1)} %pair_terms.19.refs_3_), custom_call_target="tpu_custom_call", output_to_operand_aliasing={{}: (3, {})} | custom-call | flops 805306368 | bytes 4194304 | tf_op jit(solution)/shard_map/pair_terms/pallas_call | solution.py:25
  44.8 0.7 %pair_terms.22 = f32[512,128]{1,0:T(8,128)S(1)} custom-call(bf16[2048,512]{1,0:T(8,128)(2,1)S(1)} %get-tuple-element.102.refs_0_, bf16[2048,512]{1,0:T(8,128)(2,1)S(1)} %get-tuple-element.103.refs_1_, f32[256,256]{1,0:T(8,128)S(1)} %collective-permute-done.15.refs_2_.refs_4_, f32[1024,128]{1,0:T(8,128)S(1)} %pair_terms.20.refs_3_), custom_call_target="tpu_custom_call" | custom-call | flops 402653184 | bytes 4194304 | tf_op jit(solution)/shard_map/pair_terms/pallas_call | solution.py:25
  45.4 0.4 collective-permute-start.16
  45.8 0.7 %pair_terms.21 = f32[512,128]{1,0:T(8,128)S(1)} custom-call(bf16[2048,512]{1,0:T(8,128)(2,1)S(1)} %get-tuple-element.102.refs_0_, bf16[2048,512]{1,0:T(8,128)(2,1)S(1)} %get-tuple-element.103.refs_1_, f32[256,256]{1,0:T(8,128)S(1)} %collective-permute-done.15.refs_2_.refs_4_, f32[1024,128]{1,0:T(8,128)S(1)} %pair_terms.20.refs_3_), custom_call_target="tpu_custom_call" | custom-call | flops 402653184 | bytes 4194304 | tf_op jit(solution)/shard_map/pair_terms/pallas_call | solution.py:25
  46.5 0.5 collective-permute-done.16
  47.1 1.6 %collective-permute-start.19 = (f32[512,128]{1,0:T(8,128)S(1)}, f32[512,128]{1,0:T(8,128)S(1)}, u32[]{:S(2)}, u32[]{:S(2)}) collective-permute-start(f32[512,128]{1,0:T(8,128)S(1)} %add.14), channel_id=1, source_target_pairs={{0,3},{1,2},{2,1},{3,0},{4,7},{5,6},{6,5},{7,4},{8,11},{9,10},{10,... | collective-permute-start | bytes 786440 | tf_op jit(solution)/shard_map/ppermute | solution.py:280
  48.6 3.5 %pair_terms.23 = f32[1024,128]{1,0:T(8,128)S(1)} custom-call(bf16[2048,512]{1,0:T(8,128)(2,1)S(1)} %get-tuple-element.102.refs_0_, bf16[2048,512]{1,0:T(8,128)(2,1)S(1)} %get-tuple-element.103.refs_1_, f32[512,256]{1,0:T(8,128)S(1)} %collective-permute-done.12.refs_2_, f32[256,256]{1,0:T(8,128)S(1)} %collective-permute-done.14.refs_2_.refs_3_, ...), custom_call_target="tpu_custom_call" | custom-call | flops 3221225472 | bytes 4194304 | tf_op jit(solution)/shard_map/pair_terms/pallas_call | solution.py:25
  52.2 0.4 collective-permute-start.17
  52.7 0.1 collective-permute-start.18
  52.8 0.8 %collective-permute-done.17 = f32[256,128]{1,0:T(8,128)S(1)} collective-permute-done((f32[256,128]{1,0:T(8,128)S(1)}, f32[256,128]{1,0:T(8,128)S(1)}, u32[]{:S(2)}, u32[]{:S(2)}) %collective-permute-start.17) | collective-permute-done | bytes 131104 | tf_op jit(solution)/shard_map/ppermute | solution.py:216
  53.6 0.4 collective-permute-done.18
  54.0 1.3 %collective-permute-done.19 = f32[512,128]{1,0:T(8,128)S(1)} collective-permute-done((f32[512,128]{1,0:T(8,128)S(1)}, f32[512,128]{1,0:T(8,128)S(1)}, u32[]{:S(2)}, u32[]{:S(2)}) %collective-permute-start.19) | collective-permute-done | bytes 262176 | tf_op jit(solution)/shard_map/ppermute | solution.py:280
  55.3 0.7 %fusion.1 = f32[512,128]{1,0:T(8,128)} fusion(f32[512,128]{1,0:T(8,128)S(1)} %collective-permute-done.19, f32[1024,128]{1,0:T(8,128)S(1)} %pair_terms.23, f32[256,128]{1,0:T(8,128)S(1)} %collective-permute-done.18, f32[256,128]{1,0:T(8,128)S(1)} %collective-permute-done.17), kind=kLoop, calls=%fused_computation.4 | loop fusion | flops 262144 | bytes 1048576 | tf_op jit(solution)/shard_map/mul | solution.py:287
  (22 shorter events, 0.2 us)
Async XLA Ops:
  0.0 3.7 %copy-start.1 = (f32[1024,128]{1,0:T(8,128)S(1)}, f32[1024,128]{1,0:T(8,128)}, u32[]{:S(2)}) copy-start(f32[1024,128]{1,0:T(8,128)} %fac_ref) | copy-start | bytes 1572868
  0.0 3.7 %copy-start = (f32[1024,128]{1,0:T(8,128)S(1)}, f32[1024,128]{1,0:T(8,128)}, u32[]{:S(2)}) copy-start(f32[1024,128]{1,0:T(8,128)} %feat_ref) | copy-start | bytes 1572868
  1.2 9.7 %collective-permute-start.5 = (f32[512,256]{1,0:T(8,128)S(1)}, f32[512,256]{1,0:T(8,128)S(1)}, u32[]{:S(2)}, u32[]{:S(2)}) collective-permute-start(f32[512,256]{1,0:T(8,128)S(1)} %constant_dynamic-update-slice_fusion), channel_id=1, source_target_pairs={{0,10},{2,4},{8,2},{10,16},{16,26},{18,8},{24,18},{26,28},{28,22},... | collective-permute-start | bytes 1572872 | tf_op jit(solution)/shard_map/ppermute | solution.py:213
  4.1 1.7 %collective-permute-start = (f32[256,128]{1,0:T(8,128)S(1)}, f32[256,128]{1,0:T(8,128)S(1)}, u32[]{:S(2)}, u32[]{:S(2)}) collective-permute-start(f32[256,128]{1,0:T(8,128)S(1)} %get-tuple-element.64.refs_2_), channel_id=1, source_target_pairs={{0,2},{2,0},{4,6},{6,4},{8,10},{10,8},{12,14},{14,12},{16,18},{18,... | collective-permute-start | bytes 393224 | tf_op jit(solution)/shard_map/ppermute | solution.py:216
  4.8 1.4 %collective-permute-start.1 = (f32[256,128]{1,0:T(8,128)S(1)}, f32[256,128]{1,0:T(8,128)S(1)}, u32[]{:S(2)}, u32[]{:S(2)}) collective-permute-start(f32[256,128]{1,0:T(8,128)S(1)} %get-tuple-element.65.refs_4_), channel_id=1, source_target_pairs={{0,2},{2,0},{4,6},{6,4},{8,10},{10,8},{12,14},{14,12},{16,18},{18,... | collective-permute-start | bytes 393224 | tf_op jit(solution)/shard_map/ppermute | solution.py:216
  4.8 1.5 %collective-permute-start.2 = (f32[256,128]{1,0:T(8,128)S(1)}, f32[256,128]{1,0:T(8,128)S(1)}, u32[]{:S(2)}, u32[]{:S(2)}) collective-permute-start(f32[256,128]{1,0:T(8,128)S(1)} %get-tuple-element.66.refs_3_), channel_id=1, source_target_pairs={{0,2},{2,0},{4,6},{6,4},{8,10},{10,8},{12,14},{14,12},{16,18},{18,... | collective-permute-start | bytes 393224 | tf_op jit(solution)/shard_map/ppermute | solution.py:216
  5.3 1.4 %collective-permute-start.3 = (f32[256,128]{1,0:T(8,128)S(1)}, f32[256,128]{1,0:T(8,128)S(1)}, u32[]{:S(2)}, u32[]{:S(2)}) collective-permute-start(f32[256,128]{1,0:T(8,128)S(1)} %get-tuple-element.67.refs_5_), channel_id=1, source_target_pairs={{0,2},{2,0},{4,6},{6,4},{8,10},{10,8},{12,14},{14,12},{16,18},{18,... | collective-permute-start | bytes 393224 | tf_op jit(solution)/shard_map/ppermute | solution.py:216
  5.8 1.3 %collective-permute-start.6 = (f32[256,128]{1,0:T(8,128)S(1)}, f32[256,128]{1,0:T(8,128)S(1)}, u32[]{:S(2)}, u32[]{:S(2)}) collective-permute-start(f32[256,128]{1,0:T(8,128)S(1)} %get-tuple-element.68.refs_2_), channel_id=1, source_target_pairs={{0,2},{2,0},{4,6},{6,4},{8,10},{10,8},{12,14},{14,12},{16,18},{18,... | collective-permute-start | bytes 393224 | tf_op jit(solution)/shard_map/ppermute | solution.py:216
  6.1 2.6 %collective-permute-start.7 = (f32[256,128]{1,0:T(8,128)S(1)}, f32[256,128]{1,0:T(8,128)S(1)}, u32[]{:S(2)}, u32[]{:S(2)}) collective-permute-start(f32[256,128]{1,0:T(8,128)S(1)} %get-tuple-element.69.refs_3_), channel_id=1, source_target_pairs={{0,2},{2,0},{4,6},{6,4},{8,10},{10,8},{12,14},{14,12},{16,18},{18,... | collective-permute-start | bytes 393224 | tf_op jit(solution)/shard_map/ppermute | solution.py:216
  6.3 2.4 %collective-permute-start.8 = (f32[256,128]{1,0:T(8,128)S(1)}, f32[256,128]{1,0:T(8,128)S(1)}, u32[]{:S(2)}, u32[]{:S(2)}) collective-permute-start(f32[256,128]{1,0:T(8,128)S(1)} %get-tuple-element.70.refs_4_), channel_id=1, source_target_pairs={{0,2},{2,0},{4,6},{6,4},{8,10},{10,8},{12,14},{14,12},{16,18},{18,... | collective-permute-start | bytes 393224 | tf_op jit(solution)/shard_map/ppermute | solution.py:216
  6.6 2.1 %collective-permute-start.9 = (f32[256,128]{1,0:T(8,128)S(1)}, f32[256,128]{1,0:T(8,128)S(1)}, u32[]{:S(2)}, u32[]{:S(2)}) collective-permute-start(f32[256,128]{1,0:T(8,128)S(1)} %get-tuple-element.71.refs_5_), channel_id=1, source_target_pairs={{0,2},{2,0},{4,6},{6,4},{8,10},{10,8},{12,14},{14,12},{16,18},{18,... | collective-permute-start | bytes 393224 | tf_op jit(solution)/shard_map/ppermute | solution.py:216
  7.1 9.5 %collective-permute-start.4 = (f32[512,256]{1,0:T(8,128)S(1)}, f32[512,256]{1,0:T(8,128)S(1)}, u32[]{:S(2)}, u32[]{:S(2)}) collective-permute-start(f32[512,256]{1,0:T(8,128)S(1)} %maximum_maximum_fusion), channel_id=1, source_target_pairs={{0,10},{2,4},{8,2},{10,16},{16,26},{18,8},{24,18},{26,28},{28,22},... | collective-permute-start | bytes 1572872 | tf_op jit(solution)/shard_map/ppermute | solution.py:213
  11.3 10.6 %collective-permute-start.11 = (f32[512,256]{1,0:T(8,128)S(1)}, f32[512,256]{1,0:T(8,128)S(1)}, u32[]{:S(2)}, u32[]{:S(2)}) collective-permute-start(f32[512,256]{1,0:T(8,128)S(1)} %pad_maximum_fusion.refs_2_), channel_id=1, source_target_pairs={{0,10},{2,4},{8,2},{10,16},{16,26},{18,8},{24,18},{26,28},{28,22},... | collective-permute-start | bytes 1572872 | tf_op jit(solution)/shard_map/ppermute | solution.py:213
  16.6 10.9 %collective-permute-start.10 = (f32[512,256]{1,0:T(8,128)S(1)}, f32[512,256]{1,0:T(8,128)S(1)}, u32[]{:S(2)}, u32[]{:S(2)}) collective-permute-start(f32[512,256]{1,0:T(8,128)S(1)} %collective-permute-done.4.refs_2_), channel_id=1, source_target_pairs={{0,10},{2,4},{8,2},{10,16},{16,26},{18,8},{24,18},{26,28},{28,22},... | collective-permute-start | bytes 1572872 | tf_op jit(solution)/shard_map/ppermute | solution.py:213
  21.9 13.2 %collective-permute-start.13 = (f32[512,256]{1,0:T(8,128)S(1)}, f32[512,256]{1,0:T(8,128)S(1)}, u32[]{:S(2)}, u32[]{:S(2)}) collective-permute-start(f32[512,256]{1,0:T(8,128)S(1)} %collective-permute-done.11.refs_2_), channel_id=1, source_target_pairs={{0,10},{2,4},{8,2},{10,16},{16,26},{18,8},{24,18},{26,28},{28,22},... | collective-permute-start | bytes 1572872 | tf_op jit(solution)/shard_map/ppermute | solution.py:213
  27.5 14.2 %collective-permute-start.12 = (f32[512,256]{1,0:T(8,128)S(1)}, f32[512,256]{1,0:T(8,128)S(1)}, u32[]{:S(2)}, u32[]{:S(2)}) collective-permute-start(f32[512,256]{1,0:T(8,128)S(1)} %collective-permute-done.10.refs_2_), channel_id=1, source_target_pairs={{0,10},{2,4},{8,2},{10,16},{16,26},{18,8},{24,18},{26,28},{28,22},... | collective-permute-start | bytes 1572872 | tf_op jit(solution)/shard_map/ppermute | solution.py:213
  35.1 8.5 %collective-permute-start.14 = (f32[256,256]{1,0:T(8,128)S(1)}, f32[256,256]{1,0:T(8,128)S(1)}, u32[]{:S(2)}, u32[]{:S(2)}) collective-permute-start(f32[256,256]{1,0:T(8,128)S(1)} %get-tuple-element.117), channel_id=1, source_target_pairs={{0,10},{2,4},{8,2},{10,16},{16,26},{18,8},{24,18},{26,28},{28,22},... | collective-permute-start | bytes 786440 | tf_op jit(solution)/shard_map/ppermute | solution.py:213
  36.7 8.0 %collective-permute-start.15 = (f32[256,256]{1,0:T(8,128)S(1)}, f32[256,256]{1,0:T(8,128)S(1)}, u32[]{:S(2)}, u32[]{:S(2)}) collective-permute-start(f32[256,256]{1,0:T(8,128)S(1)} %get-tuple-element.118), channel_id=1, source_target_pairs={{0,10},{2,4},{8,2},{10,16},{16,26},{18,8},{24,18},{26,28},{28,22},... | collective-permute-start | bytes 786440 | tf_op jit(solution)/shard_map/ppermute | solution.py:213
  45.4 1.6 %collective-permute-start.16 = (f32[512,128]{1,0:T(8,128)S(1)}, f32[512,128]{1,0:T(8,128)S(1)}, u32[]{:S(2)}, u32[]{:S(2)}) collective-permute-start(f32[512,128]{1,0:T(8,128)S(1)} %pair_terms.22), channel_id=1, source_target_pairs={{0,2},{2,0},{4,6},{6,4},{8,10},{10,8},{12,14},{14,12},{16,18},{18,... | collective-permute-start | bytes 786440 | tf_op jit(solution)/shard_map/ppermute | solution.py:216
  47.1 8.2 %collective-permute-start.19 = (f32[512,128]{1,0:T(8,128)S(1)}, f32[512,128]{1,0:T(8,128)S(1)}, u32[]{:S(2)}, u32[]{:S(2)}) collective-permute-start(f32[512,128]{1,0:T(8,128)S(1)} %add.14), channel_id=1, source_target_pairs={{0,3},{1,2},{2,1},{3,0},{4,7},{5,6},{6,5},{7,4},{8,11},{9,10},{10,... | collective-permute-start | bytes 786440 | tf_op jit(solution)/shard_map/ppermute | solution.py:280
  52.2 1.4 %collective-permute-start.17 = (f32[256,128]{1,0:T(8,128)S(1)}, f32[256,128]{1,0:T(8,128)S(1)}, u32[]{:S(2)}, u32[]{:S(2)}) collective-permute-start(f32[256,128]{1,0:T(8,128)S(1)} %get-tuple-element.115), channel_id=1, source_target_pairs={{0,2},{2,0},{4,6},{6,4},{8,10},{10,8},{12,14},{14,12},{16,18},{18,... | collective-permute-start | bytes 393224 | tf_op jit(solution)/shard_map/ppermute | solution.py:216
  52.7 1.3 %collective-permute-start.18 = (f32[256,128]{1,0:T(8,128)S(1)}, f32[256,128]{1,0:T(8,128)S(1)}, u32[]{:S(2)}, u32[]{:S(2)}) collective-permute-start(f32[256,128]{1,0:T(8,128)S(1)} %get-tuple-element.116), channel_id=1, source_target_pairs={{0,2},{2,0},{4,6},{6,4},{8,10},{10,8},{12,14},{14,12},{16,18},{18,... | collective-permute-start | bytes 393224 | tf_op jit(solution)/shard_map/ppermute | solution.py:216
